TPU v7x, 256 devices: a whole 4x4x8 slice. The times are simulated.
256 devices in a mesh: ops: 32 (over y, x, core), sec: 8 (over z).
Axes of the slice: x: 4, y: 4, z: 8, core: 2. Of those that a mesh axis runs over, the one named last changes fastest.
Arguments:
- left_ops: bfloat16 [128, 16, 256, 256], P('ops', 'sec'), as said below
- right_ops: bfloat16 [128, 16, 256, 256], P('ops', 'sec'), as said below
- pattern: int32 [128, 16], P('ops', 'sec'), may hold values from 0 to 1, as said below
- guess_vector: float32 [16, 256, 256], P('sec'), may hold values from -6 to 6
- precond: float32 [16, 256, 256], P('sec'), may hold values from 0.5 to 8
- rotation: bfloat16 [16, 256, 256], P('sec', None, 'ops'), may hold values from -1.5 to 1.5
Outputs:
- new_state: float32 [16, 256, 256], P('sec', 'ops')
- energy: float32 [1], replicated
- renormalized: bfloat16 [128, 16, 256, 256], P('ops', 'sec')
Inputs may be any that keep to these rules, and one draw needn't show every extreme that they name: pattern[k, s] is 1 where operator k has a block in sector s, else 0. Every block left_ops[k, s] is symmetric. Every block right_ops[k, s] is symmetric.
All inputs are finite; a program needn't handle non-finite values.
Results may differ from a plain program's by a relative error of at most 0.009.
Values may be sent and summed in bfloat16 or wider, within the bound.
No kernel may reach another device: no remote copies, remote signals or barrier semaphores. Data moves between devices by JAX's collectives and lax.ppermute only.
A program may use at most 64 MiB of HBM per device.

v0:
```python
import jax
import jax.numpy as jnp
from jax import lax
from jax.sharding import PartitionSpec as P


def local_sigma(vector, left_ops, right_ops, pattern):
    vec_low = vector.astype(jnp.bfloat16)
    halfway = jnp.einsum(
        "ksij,sjl->ksil", left_ops, vec_low, preferred_element_type=jnp.float32
    ).astype(jnp.bfloat16)
    halfway = halfway * pattern.astype(jnp.bfloat16)[:, :, None, None]
    return jnp.einsum("ksil,ksml->sim", halfway, right_ops, preferred_element_type=jnp.float32)


def local(left_ops, right_ops, pattern, guess_vector, precond, rotation):
    sector_count = guess_vector.shape[0]
    states = guess_vector.shape[1]
    row_count = states // lax.axis_size("ops")
    row_start = lax.axis_index("ops") * row_count
    entries = float(sector_count * lax.axis_size("sec") * states * states)

    def owned(array):
        return lax.dynamic_slice_in_dim(array, row_start, row_count, 1)

    rotate_full = lax.all_gather(rotation, "ops", axis=2, tiled=True)
    rotated = jnp.einsum(
        "ksij,sjl->ksil", left_ops, rotate_full, preferred_element_type=jnp.float32
    ).astype(jnp.bfloat16)
    renormalized = jnp.einsum(
        "sji,ksjl->ksil", rotate_full, rotated, preferred_element_type=jnp.float32
    ).astype(jnp.bfloat16)
    guess_rows = owned(guess_vector)
    guess_sum = lax.psum(jnp.sum(guess_rows * guess_rows), ("ops", "sec"))
    first_full = guess_vector * (1.0 / jnp.sqrt(guess_sum / entries + 1e-06))

    def apply_whole(vector):
        return lax.psum(local_sigma(vector, left_ops, right_ops, pattern), "ops")

    def local_part(array):
        return owned(array)

    def local_product(left, right):
        return jnp.sum(local_part(left) * local_part(right))

    image_first = apply_whole(first_full)
    rayleigh_first = lax.psum(local_product(first_full, image_first), ("ops", "sec")) / entries
    correction = (image_first - rayleigh_first * first_full) / precond
    correlation = lax.psum(local_product(first_full, correction), ("ops", "sec")) / entries
    orthogonal = correction - correlation * first_full
    orth_square = lax.psum(local_product(orthogonal, orthogonal), ("ops", "sec")) / entries
    second = orthogonal * (1.0 / jnp.sqrt(orth_square + 1e-06))
    image_second = apply_whole(second)
    coupling_sum, second_sum = lax.psum(
        (local_product(first_full, image_second), local_product(second, image_second)),
        ("ops", "sec"),
    )
    coupling = coupling_sum / entries
    rayleigh_second = second_sum / entries
    half_gap = (rayleigh_first - rayleigh_second) / 2
    energy = (rayleigh_first + rayleigh_second) / 2 - jnp.sqrt(
        half_gap * half_gap + coupling * coupling
    )
    weight_first = rayleigh_second - energy
    weight_second = -coupling
    scaling = jnp.sqrt(weight_first * weight_first + weight_second * weight_second)
    combined = (weight_first * first_full + weight_second * second) / scaling
    new_state = local_part(combined)
    return (new_state, jnp.reshape(energy, (1,)), renormalized)


def solution(mesh):
    return jax.shard_map(
        local,
        mesh=mesh,
        in_specs=(
            P("ops", "sec", None, None),
            P("ops", "sec", None, None),
            P("ops", "sec"),
            P("sec", None, None),
            P("sec", None, None),
            P("sec", None, "ops"),
        ),
        out_specs=(P("sec", "ops", None), P(), P("ops", "sec", None, None)),
        check_vma=False,
    )
```

profile of v0, /device:TPU:1, one launch (start us, length us, event | category | flops | bytes accessed | tf_op | source)
XLA Modules:
  0.0 659.4 jit_solution(3782549998908427796)
XLA Ops:
  7.2 0.0 copy-start
  7.2 0.0 copy-start.4
  7.2 0.0 all-reduce.4.cloned.1.call-start
  7.2 1.4 multiply_reduce_fusion.5
  8.6 81.4 %psum.56 = f32[]{:T(128)} all-reduce(f32[]{:T(128)} %multiply_reduce_fusion.5), channel_id=1, replica_groups=mesh['ops'=32,'sec'=8] {'ops','sec'}, use_global_device_ids=true, to_apply=%region_1.0 | all-reduce | flops 1 | bytes 8 | tf_op jit(solution)/shard_map/psum | solution.py:34
  90.7 1.1 broadcast_multiply_fusion.1
  91.8 0.0 copy-done.4
  91.8 0.0 copy-done
  91.8 0.0 copy-start.1
  91.8 0.0 copy-start.2
  91.9 2.8 fusion.8
  94.7 0.0 all-reduce.4.cloned.1.call-update
  94.7 0.0 all-reduce.6.cloned.1.call-start
  94.8 108.9 %all-reduce.4.cloned.1.call-done = f32[2,256,256]{2,1,0:T(8,128)} async-done(((f32[2,256,256]{2,1,0:T(8,128)}), f32[2,256,256]{2,1,0:T(8,128)}) %all-reduce.4.cloned.1.call-update) | async-done | bytes 524304 | tf_op jit(solution)/shard_map/psum | solution.py:38
  203.6 1.3 multiply_reduce_fusion.4
  205.0 76.8 %psum.58 = f32[]{:T(128)} all-reduce(f32[]{:T(128)} %multiply_reduce_fusion.4), channel_id=1, replica_groups=mesh['ops'=32,'sec'=8] {'ops','sec'}, use_global_device_ids=true, to_apply=%region_4.0 | all-reduce | flops 1 | bytes 8 | tf_op jit(solution)/shard_map/psum | solution.py:47
  282.5 0.0 copy-done.1
  282.5 0.0 copy-done.2
  282.5 1.1 subtract_divide_fusion
  283.6 0.0 copy-start.3
  283.6 0.6 multiply_reduce_fusion.3
  284.2 73.4 %psum.59 = f32[]{:T(128)} all-reduce(f32[]{:T(128)} %multiply_reduce_fusion.3), channel_id=1, replica_groups=mesh['ops'=32,'sec'=8] {'ops','sec'}, use_global_device_ids=true, to_apply=%region_6.0 | all-reduce | flops 1 | bytes 8 | tf_op jit(solution)/shard_map/psum | solution.py:49
  358.3 0.1 multiply_subtract_fusion
  358.5 0.6 multiply_reduce_fusion.2
  359.1 0.0 copy-done.3
  359.1 24.0 %all_gather.3 = bf16[2,256,256]{1,2,0:T(8,128)(2,1)S(1)} all-gather(bf16[2,256,8]{1,2,0:T(8,128)(2,1)S(1)} %copy-done.3), channel_id=1, replica_groups=mesh['ops'=32,'sec'=8] {'ops'}, dimensions={2}, use_global_device_ids=true | all-gather | bytes 270336 | tf_op jit(solution)/shard_map/all_gather | solution.py:26
  383.0 73.3 %psum.60 = f32[]{:T(128)} all-reduce(f32[]{:T(128)} %multiply_reduce_fusion.2), channel_id=1, replica_groups=mesh['ops'=32,'sec'=8] {'ops','sec'}, use_global_device_ids=true, to_apply=%region_8.0 | all-reduce | flops 1 | bytes 8 | tf_op jit(solution)/shard_map/psum | solution.py:51
  457.1 2.8 fusion.9
  459.9 0.0 all-reduce.6.cloned.1.call-update
  459.9 0.7 fusion.3
  460.6 1.3 copy.11
  461.9 108.0 %all-reduce.6.cloned.1.call-done = f32[2,256,256]{2,1,0:T(8,128)} async-done(((f32[2,256,256]{2,1,0:T(8,128)}), f32[2,256,256]{2,1,0:T(8,128)}) %all-reduce.6.cloned.1.call-update) | async-done | bytes 524304 | tf_op jit(solution)/shard_map/psum | solution.py:38
  569.9 1.3 multiply_reduce_fusion
  571.2 76.9 %all-reduce = (f32[]{:T(128)}, f32[]{:T(128)}) all-reduce(f32[]{:T(128)} %get-tuple-element.7, f32[]{:T(128)} %get-tuple-element.6), channel_id=1, replica_groups=mesh['ops'=32,'sec'=8] {'ops','sec'}, use_global_device_ids=true, to_apply=%region_11.0 | all-reduce | flops 2 | bytes 16 | tf_op jit(solution)/shard_map/psum | solution.py:54
  650.8 0.6 add_divide_fusion
  (2 shorter events, 0.0 us)
Async XLA Ops:
  7.2 84.7 %copy-start = (bf16[4,2,256,256]{3,2,1,0:T(8,128)(2,1)S(1)}, bf16[4,2,256,256]{3,2,1,0:T(8,128)(2,1)}, u32[]{:S(2)}) copy-start(bf16[4,2,256,256]{3,2,1,0:T(8,128)(2,1)} %param.6) | copy-start | bytes 3145732
  7.2 84.6 %copy-start.4 = (s32[4,2]{0,1:T(2,128)S(1)}, s32[4,2]{0,1:T(2,128)}, u32[]{:S(2)}) copy-start(s32[4,2]{0,1:T(2,128)} %param.8) | copy-start | bytes 100
  7.2 196.4 %all-reduce.4.cloned.1.call-start = ((), (), s32[]{:S(2)}) async-start(), calls=%async_computation | async-start | bytes 1048576 | tf_op jit(solution)/shard_map/psum | solution.py:38
  91.8 190.6 %copy-start.1 = (f32[2,256,256]{2,1,0:T(8,128)S(1)}, f32[2,256,256]{2,1,0:T(8,128)}, u32[]{:S(2)}) copy-start(f32[2,256,256]{2,1,0:T(8,128)} %param.9) | copy-start | bytes 1572868
  91.8 190.6 %copy-start.2 = (f32[2,256,256]{2,1,0:T(8,128)S(1)}, f32[2,256,256]{2,1,0:T(8,128)}, u32[]{:S(2)}) copy-start(f32[2,256,256]{2,1,0:T(8,128)} %param.10) | copy-start | bytes 1572868
  94.7 475.2 %all-reduce.6.cloned.1.call-start = ((), (), s32[]{:S(2)}) async-start(), calls=%async_computation.1 | async-start | bytes 1048576 | tf_op jit(solution)/shard_map/psum | solution.py:38
  283.6 75.4 %copy-start.3 = (bf16[2,256,8]{1,2,0:T(8,128)(2,1)S(1)}, bf16[2,256,8]{1,2,0:T(8,128)(2,1)}, u32[]{:S(2)}) copy-start(bf16[2,256,8]{1,2,0:T(8,128)(2,1)} %param.11) | copy-start | bytes 24580
Sparse Core Ops, SparseCore 0:
  94.8 108.7 all-reduce.3
  460.0 109.8 all-reduce.5
where the time goes:
time: 661 us; the launch traced here: 659 us
  blocking collectives  406 us (61%)
  waiting for transfers between devices  217 us (33%)
  between operations  20.7 us (3%)
  other arithmetic  8.28 us (1%)
    psum x2, waiting for transfers between devices, apply_whole(): return lax.psum(local_sigma(vector, left_ops, right_ops, pattern), 'ops')  217 us
    psum x1, blocking collectives, local(): guess_sum = lax.psum(jnp.sum(guess_rows * guess_rows), ('ops', 'sec'))  81.4 us
    psum x1, blocking collectives, local(): lax.psum((local_product(first_full, image_second), local_product(second,...  76.9 us
    psum x1, blocking collectives, local(): lax.psum(local_product(first_full, image_first), ('ops', 'sec')) / entries  76.8 us
    psum x1, blocking collectives, local(): lax.psum(local_product(first_full, correction), ('ops', 'sec')) / entries  73.4 us
    psum x1, blocking collectives, local(): lax.psum(local_product(orthogonal, orthogonal), ('ops', 'sec')) / entries  73.3 us
    all_gather x1, blocking collectives, local(): rotate_full = lax.all_gather(rotation, 'ops', axis=2, tiled=True)  24 us
  transfers between devices with their start and end apart: 2, of which 2 were waited for; matrix products, arithmetic and copies ran while one was open for 0% of the time, Pallas kernels for 0%

commit v1 on v0

v1 whole, which is shorter than its diff:
```python
import jax
import jax.numpy as jnp
from jax import lax
from jax.experimental import pallas as pl
from jax.experimental.pallas import tpu as pltpu
from jax.sharding import Mesh, PartitionSpec as P

F32 = jnp.float32
BF16 = jnp.bfloat16
OPS = ("chip", "core")
VMEM = pl.BlockSpec(memory_space=pltpu.VMEM)
SMEM = pl.BlockSpec(memory_space=pltpu.SMEM)
HBM = pl.BlockSpec(memory_space=pltpu.HBM)


def dot(a, b):
    return jnp.dot(a, b, preferred_element_type=F32)


def sigma_block(s, x, pattern, left, right):
    total = None
    for k in range(left.shape[0]):
        half = (dot(left[k, s], x) * pattern[k, s].astype(F32)).astype(BF16)
        term = dot(half, right[k, s])
        total = term if total is None else total + term
    return total


def partial_kernel(pattern, left_hbm, right_hbm, guess_hbm, rot, out, left, right, guess, left_sem, right_sem, guess_sem):
    ops, sectors = left.shape[:2]
    copies = {}
    for s in range(sectors):
        copies["g", s] = pltpu.make_async_copy(guess_hbm.at[s], guess.at[s], guess_sem.at[s])
        copies["g", s].start()
        for k in range(ops):
            copies["l", k, s] = pltpu.make_async_copy(left_hbm.at[k, s], left.at[k, s], left_sem.at[k, s])
            copies["l", k, s].start()
        for k in range(ops):
            copies["r", k, s] = pltpu.make_async_copy(right_hbm.at[k, s], right.at[k, s], right_sem.at[k, s])
            copies["r", k, s].start()
    peers = out.shape[0]
    parts = []
    for s in range(sectors):
        copies["g", s].wait()
        x = guess[s].astype(BF16)
        halves = []
        for k in range(ops):
            copies["l", k, s].wait()
            halves.append((dot(left[k, s], x) * pattern[k, s].astype(F32)).astype(BF16))
        total = None
        for k in range(ops):
            copies["r", k, s].wait()
            term = dot(halves[k], right[k, s])
            total = term if total is None else total + term
        parts.append(total.reshape(peers, -1, total.shape[1]))
    turned = [jnp.transpose(rot[s].astype(F32)) for s in range(sectors)]
    columns = jnp.stack(turned)
    columns = jnp.broadcast_to(columns[None], (peers // sectors,) + columns.shape).reshape((peers,) + turned[0].shape)
    out[...] = jnp.concatenate(parts + [columns], axis=1).astype(BF16)


def level_kernel(pattern, left, right, guess, precond, out):
    total = None
    for s in range(guess.shape[0]):
        d = guess[s] / precond[s]
        image = sigma_block(s, d.astype(BF16), pattern, left, right)
        term = jnp.sum(d * image, axis=0, keepdims=True)
        total = term if total is None else total + term
    out[...] = total


def rows_kernel(received, guess, precond, image_out, scaled_out, chunks):
    sectors, rows = guess.shape[:2]
    image = jnp.sum(received[:, : sectors * rows, :].astype(F32), axis=0)
    scaled = image / precond[...].reshape(image.shape)
    image_out[...] = image.reshape(guess.shape)
    scaled_out[...] = scaled.reshape(guess.shape)
    chunks[...] = jnp.broadcast_to(scaled[None].astype(BF16), chunks.shape)


def row_sums_kernel(guess, precond, image, scaled, sums):
    g, h, y = guess[...], image[...], scaled[...]
    d = g / precond[...]
    pairs = ((g, g), (g, h), (g, d), (d, d), (g, y), (d, y), (y, y), (h, y))
    sums[...] = jnp.concatenate([jnp.sum(a * b, axis=(0, 1)).reshape(1, -1) for a, b in pairs], axis=0)


def columns_kernel(received, out):
    width = received.shape[2]
    out[...] = received[:, received.shape[1] - width // received.shape[0] :, :].astype(F32).reshape(width, width).astype(BF16)


def renorm_kernel(core, left, mine, theirs, out):
    first = (core[0] == 0).astype(F32)
    a, b = mine[...].astype(F32), theirs[...].astype(F32)
    for s in range(left.shape[1]):
        turned = a * first + b * (1.0 - first) if s == 0 else b * first + a * (1.0 - first)
        rotation = jnp.transpose(turned).astype(BF16)
        turned = turned.astype(BF16)
        for k in range(left.shape[0]):
            rotated = dot(left[k, s], rotation).astype(BF16)
            out[k, s] = dot(turned, rotated).astype(BF16)


def second_kernel(pattern, received, left, right, guess, precond, row_sums, level, out):
    sectors, states = guess.shape[:2]
    rows = states // received.shape[0]
    y_hy, d_hy = None, None
    for s in range(sectors):
        y = received[:, s * rows : (s + 1) * rows, :].astype(F32).reshape(states, states)
        image = sigma_block(s, y.astype(BF16), pattern, left, right)
        d = guess[s] / precond[s]
        a, b = jnp.sum(y * image, axis=0, keepdims=True), jnp.sum(d * image, axis=0, keepdims=True)
        y_hy, d_hy = (a, b) if y_hy is None else (y_hy + a, d_hy + b)
    low = jnp.sum(row_sums[...], axis=1, keepdims=True)
    high = jnp.concatenate([y_hy, d_hy, level[...], jnp.zeros((5, states), F32)], axis=0)
    high = jnp.sum(high, axis=1, keepdims=True)
    lane = lax.broadcasted_iota(jnp.int32, out.shape[1:], 1)
    tile = jnp.where(lane == 0, low, jnp.where(lane == 1, high, 0.0))
    out[...] = jnp.broadcast_to(tile[None], out.shape)


def gather_kernel(received, out):
    total = jnp.sum(received[...], axis=0)
    out[...] = jnp.broadcast_to(total[None], out.shape)


def state_kernel(entries, received, guess, precond, scaled, state, energy_out):
    sums = jnp.sum(received[...], axis=0)
    lane = lax.broadcasted_iota(jnp.int32, sums.shape, 1)
    low = jnp.sum(jnp.where(lane == 0, sums, 0.0), axis=1, keepdims=True)
    high = jnp.sum(jnp.where(lane == 1, sums, 0.0), axis=1, keepdims=True)
    gg, gh, gd, dd, gy, dy, yy, hy = [low[i : i + 1] for i in range(8)]
    y_hy, d_hy, d_hd = [high[i : i + 1] for i in range(3)]
    inverse = 1.0 / entries
    first_square = 1.0 / (gg * inverse + 1e-06)
    rho = first_square * gh * inverse
    kappa = first_square * (gy - rho * gd) * inverse
    qq = yy - 2.0 * rho * dy + rho * rho * dd - 2.0 * kappa * (gy - rho * gd) + kappa * kappa * gg
    hq = hy - rho * gy - kappa * gh
    q_hq = y_hy - 2.0 * rho * d_hy + rho * rho * d_hd - 2.0 * kappa * (hy - rho * gy) + kappa * kappa * gh
    second_square = 1.0 / (first_square * qq * inverse + 1e-06)
    second_scale = jnp.sqrt(second_square)
    first_scale = jnp.sqrt(first_square)
    coupling = second_scale * first_square * hq * inverse
    rho_second = second_square * first_square * q_hq * inverse
    half_gap = (rho - rho_second) * 0.5
    energy = (rho + rho_second) * 0.5 - jnp.sqrt(half_gap * half_gap + coupling * coupling)
    weight_first = rho_second - energy
    weight_second = -coupling
    scaling = 1.0 / jnp.sqrt(weight_first * weight_first + weight_second * weight_second)
    on_second = weight_second * second_scale * scaling * first_scale
    on_first = weight_first * scaling * first_scale
    energy_out[...] = jnp.broadcast_to(energy, energy_out.shape)
    g = guess[...]
    d = g / precond[...]
    state[...] = on_first[None] * g + on_second[None] * (scaled[...] - rho[None] * d - kappa[None] * g)


def call(kernel, out_shape, in_specs, flops=0, scratch=(), out_specs=VMEM):
    return pl.pallas_call(
        kernel,
        out_shape=out_shape,
        in_specs=in_specs,
        out_specs=jax.tree.map(lambda _: out_specs, out_shape),
        scratch_shapes=scratch,
        cost_estimate=pl.CostEstimate(flops=flops, bytes_accessed=1 << 20, transcendentals=0),
        compiler_params=pltpu.CompilerParams(vmem_limit_bytes=16 << 20),
    )


def local(left, right, pattern, guess, precond, rotation):
    ops, sectors, states = left.shape[:3]
    peers = lax.axis_size(OPS)
    zones = lax.axis_size("sec")
    rows = states // peers
    me = lax.axis_index(OPS)
    entries = float(sectors * zones * states * states)
    shape = jax.ShapeDtypeStruct
    flops = 4 * ops * sectors * states**3

    parts = call(
        partial_kernel,
        shape((peers, (sectors + 1) * rows, states), BF16),
        [SMEM, HBM, HBM, HBM, VMEM],
        flops,
        [
            pltpu.VMEM(left.shape, BF16),
            pltpu.VMEM(right.shape, BF16),
            pltpu.VMEM(guess.shape, F32),
            pltpu.SemaphoreType.DMA((ops, sectors)),
            pltpu.SemaphoreType.DMA((ops, sectors)),
            pltpu.SemaphoreType.DMA((sectors,)),
        ],
    )(pattern, left, right, guess, rotation)
    received = lax.all_to_all(parts, OPS, 0, 0)

    level = call(level_kernel, shape((1, states), F32), [SMEM] + [VMEM] * 4, flops)(pattern, left, right, guess, precond)
    guess_rows = lax.dynamic_slice_in_dim(guess, me * rows, rows, 1)
    precond_rows = lax.dynamic_slice_in_dim(precond, me * rows, rows, 1)

    block = shape(guess_rows.shape, F32)
    image_rows, scaled_rows, chunks = call(
        rows_kernel, (block, block, shape((peers, sectors * rows, states), BF16)), [VMEM] * 3
    )(received, guess_rows, precond_rows)
    gathered = lax.all_to_all(chunks, OPS, 0, 0)

    mine = call(columns_kernel, shape((states, states), BF16), [VMEM])(received)
    theirs = lax.ppermute(mine, "core", [(0, 1), (1, 0)])
    row_sums = call(row_sums_kernel, shape((8, states), F32), [VMEM] * 4)(
        guess_rows, precond_rows, image_rows, scaled_rows
    )
    core = lax.axis_index("core").reshape(1)
    renormalized = call(renorm_kernel, shape(left.shape, BF16), [SMEM, VMEM, VMEM, VMEM], flops)(
        core, left, mine, theirs
    )

    sums = call(second_kernel, shape((peers, 8, 128), F32), [SMEM] + [VMEM] * 7, flops)(
        pattern, gathered, left, right, guess, precond, row_sums, level
    )
    sums = lax.all_to_all(sums, OPS, 0, 0)
    sums = call(gather_kernel, shape((zones, 8, 128), F32), [VMEM])(sums)
    sums = lax.all_to_all(sums, "sec", 0, 0)
    new_state, energy = call(
        lambda *refs: state_kernel(entries, *refs), (block, shape((1, 128), F32)), [VMEM] * 4
    )(sums, guess_rows, precond_rows, scaled_rows)
    return new_state, energy[0, :1], renormalized


def solution(mesh):
    cores = 2
    mesh = Mesh(mesh.devices.reshape(-1, cores, mesh.shape["sec"]), ("chip", "core", "sec"))
    return jax.shard_map(
        local,
        mesh=mesh,
        in_specs=(
            P(OPS, "sec", None, None),
            P(OPS, "sec", None, None),
            P(OPS, "sec"),
            P("sec", None, None),
            P("sec", None, None),
            P("sec", None, OPS),
        ),
        out_specs=(P("sec", OPS, None), P(), P(OPS, "sec", None, None)),
        check_vma=False,
    )
```

time: 661 us -> 83 us (0.13)
  blocking collectives: 406 us -> 0 us
  waiting for transfers between devices: 217 us -> 27.5 us
  starting transfers between devices: 0.08 us -> 25.6 us
  between operations: 20.7 us -> 0.83 us
  local copies, waits for them, and re-layouts: 1.34 us -> 15.1 us
  Pallas kernels: 0 us -> 13.1 us
  other arithmetic: 8.28 us -> 0 us
    psum x5 -> x0, blocking collectives: 382 us -> none  [the longest x1 81.4 us: local(): guess_sum = lax.psum(jnp.sum(guess_rows * guess_rows), ('ops', 'sec'))]
    psum x2 -> x0, waiting for transfers between devices: 217 us -> none  [apply_whole(): return lax.psum(local_sigma(vector, left_ops, right_ops, pattern), 'ops')]
    all_to_all x0 -> x4, waiting for transfers between devices: none -> 27.5 us  [the longest x1 9.51 us: local(): received = lax.all_to_all(parts, OPS, 0, 0)]
    all_to_all x0 -> x4, starting transfers between devices: none -> 25.2 us  [the longest x1 8.72 us: local(): received = lax.all_to_all(parts, OPS, 0, 0)]
    all_gather x1 -> x0, blocking collectives: 24 us -> none  [local(): rotate_full = lax.all_gather(rotation, 'ops', axis=2, tiled=True)]
    pallas_call x0 -> x9, Pallas kernels: none -> 13.1 us  [the longest x1 6.22 us: local(): call(partial_kernel, shape((peers, (sectors + 1) * rows, states), BF16),...]
    unnamed x11 -> x54, local copies, waits for them, and re-layouts: 1.34 us -> 14.5 us
  transfers between devices with their start and end apart: 2 -> 5, of which waited for: 2 -> 4; matrix products, arithmetic and copies ran while one was open for 0% -> 1% of each run, Pallas kernels for 0% -> 5%
where the time goes in v1:
time: 83 us; the launch traced here: 82.2 us
  waiting for transfers between devices  27.5 us (33%)
  starting transfers between devices  25.6 us (31%)
  local copies, waits for them, and re-layouts  15.1 us (18%)
  Pallas kernels  13.1 us (16%)
    unnamed x54, local copies, waits for them, and re-layouts  14.5 us
    all_to_all x1, waiting for transfers between devices, local(): received = lax.all_to_all(parts, OPS, 0, 0)  9.51 us
    all_to_all x1, starting transfers between devices, local(): received = lax.all_to_all(parts, OPS, 0, 0)  8.72 us
    all_to_all x1, starting transfers between devices, local(): sums = lax.all_to_all(sums, 'sec', 0, 0)  8.18 us
    all_to_all x1, waiting for transfers between devices, local(): sums = lax.all_to_all(sums, OPS, 0, 0)  7.29 us
    pallas_call x1, Pallas kernels, local(): call(partial_kernel, shape((peers, (sectors + 1) * rows, states), BF16),...  6.22 us
    all_to_all x1, waiting for transfers between devices, local(): gathered = lax.all_to_all(chunks, OPS, 0, 0)  5.72 us
    all_to_all x1, waiting for transfers between devices, local(): sums = lax.all_to_all(sums, 'sec', 0, 0)  5 us
  transfers between devices with their start and end apart: 5, of which 4 were waited for; matrix products, arithmetic and copies ran while one was open for 1% of the time, Pallas kernels for 5%

profile of v1, /device:TPU:1, one launch (start us, length us, event | category | flops | bytes accessed | tf_op | source)
XLA Modules:
  0.0 82.2 jit_solution(15938375950724998754)
XLA Ops:
  0.6 0.8 copy.12.pattern
  1.4 1.5 %copy.10.rot = bf16[2,256,8]{2,1,0:T(8,128)(2,1)} copy(bf16[2,256,8]{1,2,0:T(8,128)(2,1)} %param.11) | data formatting | bytes 16384 | tf_op args[5]
  2.9 0.0 copy-done.17
  2.9 1.2 %copy-done = bf16[4,2,256,256]{3,2,1,0:T(8,128)(2,1)S(1)} copy-done((bf16[4,2,256,256]{3,2,1,0:T(8,128)(2,1)S(1)}, bf16[4,2,256,256]{3,2,1,0:T(8,128)(2,1)}, u32[]{:S(2)}) %copy-start) | copy-done | bytes 1048600
  4.1 1.2 %copy-done.2 = bf16[4,2,256,256]{3,2,1,0:T(8,128)(2,1)S(1)} copy-done((bf16[4,2,256,256]{3,2,1,0:T(8,128)(2,1)S(1)}, bf16[4,2,256,256]{3,2,1,0:T(8,128)(2,1)}, u32[]{:S(2)}) %copy-start.2) | copy-done | bytes 1048600
  5.3 1.0 %copy-done.4 = f32[2,256,256]{2,1,0:T(8,128)S(1)} copy-done((f32[2,256,256]{2,1,0:T(8,128)S(1)}, f32[2,256,256]{2,1,0:T(8,128)}, u32[]{:S(2)}) %copy-start.4) | copy-done | bytes 524312
  6.4 0.9 %copy-done.9 = bf16[2,256,8]{2,1,0:T(8,128)(2,1)S(1)} copy-done((bf16[2,256,8]{2,1,0:T(8,128)(2,1)S(1)}, bf16[2,256,8]{2,1,0:T(8,128)(2,1)}, u32[]{:S(2)}) %copy-start.9) | copy-done | bytes 8216
  7.3 6.2 %shard_map.85 = bf16[32,24,256]{2,1,0:T(8,128)(2,1)S(1)} custom-call(s32[4,2]{1,0:T(4,128)S(1)} %copy.12.pattern, bf16[4,2,256,256]{3,2,1,0:T(8,128)(2,1)S(1)} %copy-done, bf16[4,2,256,256]{3,2,1,0:T(8,128)(2,1)S(1)} %copy-done.2, f32[2,256,256]{2,1,0:T(8,128)S(1)} %copy-done.4, bf16[2,256,8]{2,1,0:T(8,128)(2,1)S(1)} %copy-done.9), custom_call_target="tpu_custom_call" | custom-call | flops 536870912 | bytes 1048576 | tf_op jit(solution)/shard_map/pallas_call | solution.py:182
  13.5 0.0 copy-start.7
  13.5 0.7 copy-done.7
  14.3 8.7 %all-to-all-start = ((bf16[32,24,256]{2,1,0:T(8,128)(2,1)}), bf16[32,24,256]{2,1,0:T(8,128)(2,1)S(1)}, u32[]{:S(2)}, u32[]{:S(2)}) async-start(bf16[32,24,256]{2,1,0:T(8,128)(2,1)} %copy-done.7), calls=%async_computation | async-start | bytes 786432 | tf_op jit(solution)/shard_map/all_to_all | solution.py:196
  23.0 0.0 copy-done.5
  23.0 0.0 copy-done.6
  23.0 0.6 constant_dynamic-slice_fusion.precond.refs_2_
  23.7 9.5 %all-to-all-done.received = bf16[32,24,256]{2,1,0:T(8,128)(2,1)S(1)} async-done(((bf16[32,24,256]{2,1,0:T(8,128)(2,1)}), bf16[32,24,256]{2,1,0:T(8,128)(2,1)S(1)}, u32[]{:S(2)}, u32[]{:S(2)}) %all-to-all-start) | async-done | bytes 393248 | tf_op jit(solution)/shard_map/all_to_all | solution.py:196
  33.2 0.7 copy-done.11
  33.9 0.1 shard_map.86
  34.0 0.0 copy-start.10
  34.0 0.7 copy-done.10
  34.7 0.6 copy-done.14
  35.3 0.6 copy-done.22
  35.9 4.5 %all-to-all-start.1 = ((bf16[32,16,256]{2,1,0:T(8,128)(2,1)}), bf16[32,16,256]{2,1,0:T(8,128)(2,1)}, u32[]{:S(2)}, u32[]{:S(2)}) async-start(bf16[32,16,256]{2,1,0:T(8,128)(2,1)} %copy-done.10), calls=%async_computation.1 | async-start | bytes 524288 | tf_op jit(solution)/shard_map/all_to_all | solution.py:206
  40.4 0.0 copy-done.3
  40.4 0.0 copy-done.1
  40.4 0.0 copy-start.18
  40.4 0.7 copy-done.18
  41.1 1.5 %shard_map.88.level = f32[1,256]{1,0:T(1,128)S(1)} custom-call(s32[4,2]{1,0:T(4,128)S(1)} %copy-done.18, bf16[4,2,256,256]{3,2,1,0:T(8,128)(2,1)S(1)} %copy-done.1, bf16[4,2,256,256]{3,2,1,0:T(8,128)(2,1)S(1)} %copy-done.3, f32[2,256,256]{2,1,0:T(8,128)S(1)} %copy-done.5, f32[2,256,256]{2,1,0:T(8,128)S(1)} %copy-done.6), custom_call_target="tpu_custom_call" | custom-call | flops 536870912 | bytes 1048576 | tf_op jit(solution)/shard_map/pallas_call | solution.py:198
  42.6 0.5 copy-done.24
  43.1 0.0 copy-done.15
  43.2 0.6 copy-done.20
  43.8 5.7 %all-to-all-done.1.received = bf16[32,16,256]{2,1,0:T(8,128)(2,1)} async-done(((bf16[32,16,256]{2,1,0:T(8,128)(2,1)}), bf16[32,16,256]{2,1,0:T(8,128)(2,1)}, u32[]{:S(2)}, u32[]{:S(2)}) %all-to-all-start.1) | async-done | bytes 262176 | tf_op jit(solution)/shard_map/all_to_all | solution.py:206
  49.5 0.7 copy-done.19
  50.1 0.7 copy-done.21
  50.8 0.6 copy-done.25
  51.5 1.9 %shard_map.89 = f32[32,8,128]{2,1,0:T(8,128)S(1)} custom-call(s32[4,2]{1,0:T(4,128)S(1)} %copy-done.19, bf16[32,16,256]{2,1,0:T(8,128)(2,1)} %all-to-all-done.1.received, bf16[4,2,256,256]{3,2,1,0:T(8,128)(2,1)S(1)} %copy-done.1, bf16[4,2,256,256]{3,2,1,0:T(8,128)(2,1)S(1)} %copy-done.3, f32[2,256,256]{2,1,0:T(8,128)S(1)} %copy-done.5, ...), custom_call_target="tpu_custom_call" | custom-call | flops 536870912 | bytes 1048576 | tf_op jit(solution)/shard_map/pallas_call | solution.py:218
  53.4 0.0 copy-start.8
  53.4 0.6 copy-done.8
  54.1 3.8 %all-to-all-start.2 = ((f32[32,8,128]{2,1,0:T(8,128)}), f32[32,8,128]{2,1,0:T(8,128)S(1)}, u32[]{:S(2)}, u32[]{:S(2)}) async-start(f32[32,8,128]{2,1,0:T(8,128)} %copy-done.8), calls=%async_computation.2 | async-start | bytes 262144 | tf_op jit(solution)/shard_map/all_to_all | solution.py:221
  57.9 0.4 collective-permute-start
  58.3 7.3 %all-to-all-done.2.received = f32[32,8,128]{2,1,0:T(8,128)S(1)} async-done(((f32[32,8,128]{2,1,0:T(8,128)}), f32[32,8,128]{2,1,0:T(8,128)S(1)}, u32[]{:S(2)}, u32[]{:S(2)}) %all-to-all-start.2) | async-done | bytes 131104 | tf_op jit(solution)/shard_map/all_to_all | solution.py:221
  65.6 0.7 shard_map.90
  66.2 8.2 %all-to-all-start.3 = ((f32[8,8,128]{2,1,0:T(8,128)}), f32[8,8,128]{2,1,0:T(8,128)S(1)}, u32[]{:S(2)}, u32[]{:S(2)}) async-start(f32[8,8,128]{2,1,0:T(8,128)} %shard_map.90), calls=%async_computation.3 | async-start | bytes 65536 | tf_op jit(solution)/shard_map/all_to_all | solution.py:223
  74.4 0.0 collective-permute-done.theirs
  74.4 0.0 copy-start.13
  74.4 0.0 copy-start.16
  74.4 2.0 %shard_map.93 = bf16[4,2,256,256]{3,2,1,0:T(8,128)(2,1)} custom-call(s32[1]{0:T(128)} %bitcast.1.core, bf16[4,2,256,256]{3,2,1,0:T(8,128)(2,1)S(1)} %copy-done.1, bf16[256,256]{1,0:T(8,128)(2,1)S(1)} %shard_map.92.mine, bf16[256,256]{1,0:T(8,128)(2,1)S(1)} %collective-permute-done.theirs), custom_call_target="tpu_custom_call" | custom-call | flops 536870912 | bytes 1048576 | tf_op jit(solution)/shard_map/pallas_call | solution.py:214
  76.4 5.0 %all-to-all-done.3.refs_0_ = f32[8,8,128]{2,1,0:T(8,128)S(1)} async-done(((f32[8,8,128]{2,1,0:T(8,128)}), f32[8,8,128]{2,1,0:T(8,128)S(1)}, u32[]{:S(2)}, u32[]{:S(2)}) %all-to-all-start.3) | async-done | bytes 32800 | tf_op jit(solution)/shard_map/all_to_all | solution.py:223
  81.4 0.8 shard_map.91
  (27 shorter events, 0.1 us)
Async XLA Ops:
  1.4 1.5 %copy-start.17 = (s32[4,2]{1,0:T(4,128)}, s32[4,2]{1,0:T(4,128)S(1)}, u32[]{:S(2)}) copy-start(s32[4,2]{1,0:T(4,128)S(1)} %copy.12.pattern) | copy-start | bytes 100
  2.9 1.2 %copy-start = (bf16[4,2,256,256]{3,2,1,0:T(8,128)(2,1)S(1)}, bf16[4,2,256,256]{3,2,1,0:T(8,128)(2,1)}, u32[]{:S(2)}) copy-start(bf16[4,2,256,256]{3,2,1,0:T(8,128)(2,1)} %left.5) | copy-start | bytes 3145732
  4.1 1.2 %copy-start.2 = (bf16[4,2,256,256]{3,2,1,0:T(8,128)(2,1)S(1)}, bf16[4,2,256,256]{3,2,1,0:T(8,128)(2,1)}, u32[]{:S(2)}) copy-start(bf16[4,2,256,256]{3,2,1,0:T(8,128)(2,1)} %right.3) | copy-start | bytes 3145732
  5.3 1.0 %copy-start.4 = (f32[2,256,256]{2,1,0:T(8,128)S(1)}, f32[2,256,256]{2,1,0:T(8,128)}, u32[]{:S(2)}) copy-start(f32[2,256,256]{2,1,0:T(8,128)} %guess.3) | copy-start | bytes 1572868
  6.4 0.9 %copy-start.9 = (bf16[2,256,8]{2,1,0:T(8,128)(2,1)S(1)}, bf16[2,256,8]{2,1,0:T(8,128)(2,1)}, u32[]{:S(2)}) copy-start(bf16[2,256,8]{2,1,0:T(8,128)(2,1)} %copy.10.rot) | copy-start | bytes 24580
  7.3 15.7 %copy-start.5 = (f32[2,256,256]{2,1,0:T(8,128)S(1)}, f32[2,256,256]{2,1,0:T(8,128)}, u32[]{:S(2)}) copy-start(f32[2,256,256]{2,1,0:T(8,128)} %guess.3) | copy-start | bytes 1572868
  7.3 15.7 %copy-start.6 = (f32[2,256,256]{2,1,0:T(8,128)S(1)}, f32[2,256,256]{2,1,0:T(8,128)}, u32[]{:S(2)}) copy-start(f32[2,256,256]{2,1,0:T(8,128)} %precond.3) | copy-start | bytes 1572868
  7.3 33.1 %copy-start.3 = (bf16[4,2,256,256]{3,2,1,0:T(8,128)(2,1)S(1)}, bf16[4,2,256,256]{3,2,1,0:T(8,128)(2,1)}, u32[]{:S(2)}) copy-start(bf16[4,2,256,256]{3,2,1,0:T(8,128)(2,1)} %right.3) | copy-start | bytes 3145732
  13.5 0.7 copy-start.7
  14.3 26.2 %copy-start.1 = (bf16[4,2,256,256]{3,2,1,0:T(8,128)(2,1)S(1)}, bf16[4,2,256,256]{3,2,1,0:T(8,128)(2,1)}, u32[]{:S(2)}) copy-start(bf16[4,2,256,256]{3,2,1,0:T(8,128)(2,1)} %left.5) | copy-start | bytes 3145732
  14.3 18.9 %all-to-all-start = ((bf16[32,24,256]{2,1,0:T(8,128)(2,1)}), bf16[32,24,256]{2,1,0:T(8,128)(2,1)S(1)}, u32[]{:S(2)}, u32[]{:S(2)}) async-start(bf16[32,24,256]{2,1,0:T(8,128)(2,1)} %copy-done.7), calls=%async_computation | async-start | bytes 786432 | tf_op jit(solution)/shard_map/all_to_all | solution.py:196
  33.2 0.7 copy-start.11
  34.0 0.7 copy-start.10
  34.7 0.6 copy-start.14
  35.3 0.6 copy-start.22
  35.9 13.6 %all-to-all-start.1 = ((bf16[32,16,256]{2,1,0:T(8,128)(2,1)}), bf16[32,16,256]{2,1,0:T(8,128)(2,1)}, u32[]{:S(2)}, u32[]{:S(2)}) async-start(bf16[32,16,256]{2,1,0:T(8,128)(2,1)} %copy-done.10), calls=%async_computation.1 | async-start | bytes 524288 | tf_op jit(solution)/shard_map/all_to_all | solution.py:206
  40.4 0.7 copy-start.18
  41.1 2.0 %copy-start.12 = (f32[2,8,256]{2,1,0:T(8,128)S(1)}, f32[2,8,256]{2,1,0:T(8,128)}, u32[]{:S(2)}) copy-start(f32[2,8,256]{2,1,0:T(8,128)} %constant_dynamic-slice_fusion.precond.refs_2_) | copy-start | bytes 49156
  41.1 2.0 %copy-start.15 = (f32[2,8,256]{2,1,0:T(8,128)S(1)}, f32[2,8,256]{2,1,0:T(8,128)}, u32[]{:S(2)}) copy-start(f32[2,8,256]{2,1,0:T(8,128)} %copy-done.14) | copy-start | bytes 49156
  41.1 2.0 %copy-start.23 = (f32[2,8,256]{2,1,0:T(8,128)S(1)}, f32[2,8,256]{2,1,0:T(8,128)}, u32[]{:S(2)}) copy-start(f32[2,8,256]{2,1,0:T(8,128)} %copy-done.22) | copy-start | bytes 49156
  42.6 0.5 copy-start.24
  43.2 0.6 copy-start.20
  49.5 0.7 copy-start.19
  50.1 0.7 copy-start.21
  50.8 0.6 copy-start.25
  53.4 0.7 copy-start.8
  54.1 11.5 %all-to-all-start.2 = ((f32[32,8,128]{2,1,0:T(8,128)}), f32[32,8,128]{2,1,0:T(8,128)S(1)}, u32[]{:S(2)}, u32[]{:S(2)}) async-start(f32[32,8,128]{2,1,0:T(8,128)} %copy-done.8), calls=%async_computation.2 | async-start | bytes 262144 | tf_op jit(solution)/shard_map/all_to_all | solution.py:221
  57.9 16.6 %collective-permute-start = (bf16[256,256]{1,0:T(8,128)(2,1)S(1)}, bf16[256,256]{1,0:T(8,128)(2,1)S(1)}, u32[]{:S(2)}, u32[]{:S(2)}) collective-permute-start(bf16[256,256]{1,0:T(8,128)(2,1)S(1)} %shard_map.92.mine), channel_id=1, source_target_pairs={{0,8},{8,0},{1,9},{9,1},{2,10},{10,2},{3,11},{11,3},{4,12},{12,4},... | collective-permute-start | bytes 393224 | tf_op jit(solution)/shard_map/ppermute | solution.py:209
  66.2 15.2 %all-to-all-start.3 = ((f32[8,8,128]{2,1,0:T(8,128)}), f32[8,8,128]{2,1,0:T(8,128)S(1)}, u32[]{:S(2)}, u32[]{:S(2)}) async-start(f32[8,8,128]{2,1,0:T(8,128)} %shard_map.90), calls=%async_computation.3 | async-start | bytes 65536 | tf_op jit(solution)/shard_map/all_to_all | solution.py:223
  74.4 7.0 %copy-start.13 = (f32[2,8,256]{2,1,0:T(8,128)S(1)}, f32[2,8,256]{2,1,0:T(8,128)}, u32[]{:S(2)}) copy-start(f32[2,8,256]{2,1,0:T(8,128)} %constant_dynamic-slice_fusion.precond.refs_2_) | copy-start | bytes 49156
  74.4 7.0 %copy-start.16 = (f32[2,8,256]{2,1,0:T(8,128)S(1)}, f32[2,8,256]{2,1,0:T(8,128)}, u32[]{:S(2)}) copy-start(f32[2,8,256]{2,1,0:T(8,128)} %copy-done.14) | copy-start | bytes 49156

commit v2 on v1

v2 whole, which is shorter than its diff:
```python
import jax
import jax.numpy as jnp
from jax import lax
from jax.experimental import pallas as pl
from jax.experimental.pallas import tpu as pltpu
from jax.sharding import Mesh, PartitionSpec as P

F32 = jnp.float32
BF16 = jnp.bfloat16
OPS = ("chip", "core")
VMEM = pl.BlockSpec(memory_space=pltpu.VMEM)
SMEM = pl.BlockSpec(memory_space=pltpu.SMEM)
HBM = pl.BlockSpec(memory_space=pltpu.HBM)


def dot(a, b):
    return jnp.dot(a, b, preferred_element_type=F32)


def total_of(terms):
    total = terms[0]
    for term in terms[1:]:
        total = total + term
    return total


def partial_kernel(
    pattern, me, left_hbm, right_hbm, guess_hbm, precond_hbm, rot,
    chunks, left, right, level, rows_out,
    guess, precond, left_sem, right_sem, guess_sem, precond_sem,
):
    ops, sectors = left.shape[:2]
    peers = chunks.shape[0]
    rows = guess.shape[1] // peers
    copies = {}

    def start(name, source, target, sem):
        copies[name] = pltpu.make_async_copy(source, target, sem)
        copies[name].start()

    for s in range(sectors):
        start(("g", s), guess_hbm.at[s], guess.at[s], guess_sem.at[s])
        for k in range(ops):
            start(("l", k, s), left_hbm.at[k, s], left.at[k, s], left_sem.at[k, s])
        for k in range(ops):
            start(("r", k, s), right_hbm.at[k, s], right.at[k, s], right_sem.at[k, s])
    for s in range(sectors):
        start(("p", s), precond_hbm.at[s], precond.at[s], precond_sem.at[s])
    parts = []
    for s in range(sectors):
        copies["g", s].wait()
        g = guess[s]
        high = g.astype(BF16)
        low = (g - high.astype(F32)).astype(BF16)
        halves = []
        for k in range(ops):
            copies["l", k, s].wait()
            half = dot(left[k, s], high) + dot(left[k, s], low)
            halves.append((half * pattern[s, k].astype(F32)).astype(BF16))
        terms = []
        for k in range(ops):
            copies["r", k, s].wait()
            terms.append(dot(halves[k], right[k, s]))
        parts.append(total_of(terms).reshape(peers, rows, g.shape[1]))
    columns = rot[...].astype(F32)
    columns = jnp.broadcast_to(columns[None], (peers // sectors,) + columns.shape).reshape((peers,) + columns.shape[1:])
    chunks[...] = jnp.concatenate(parts + [columns], axis=1).astype(BF16)
    own = pl.ds(pl.multiple_of(me[0] * rows, rows), rows)
    for s in range(sectors):
        copies["p", s].wait()
        level[s] = guess[s] / precond[s]
        rows_out[0, s] = guess[s, own, :]
        rows_out[1, s] = level[s, own, :]
        rows_out[2, s] = precond[s, own, :]


def rows_kernel(received, rows_in, kept, chunks):
    g, d, p = rows_in[0], rows_in[1], rows_in[2]
    sectors, rows, states = g.shape
    image = jnp.sum(received[:, : sectors * rows, :].astype(F32), axis=0)
    h = image.reshape(g.shape)
    y = h / p
    pairs = ((g, g), (g, h), (g, d), (d, d), (g, y), (d, y), (y, y), (h, y))
    sums = jnp.concatenate([jnp.sum(a * b, axis=(0, 1)).reshape(1, -1) for a, b in pairs], axis=0)
    kept[...] = jnp.concatenate([y.reshape(-1, states), sums], axis=0)
    chunks[...] = jnp.broadcast_to(y.reshape(1, -1, states).astype(BF16), chunks.shape)


def second_kernel(pattern, received, left, right, level, kept, out):
    ops, sectors, states = left.shape[:3]
    rows = states // received.shape[0]
    y_hy, d_hy, d_hd = [], [], []
    for s in range(sectors):
        d = level[s]
        y = received[:, s * rows : (s + 1) * rows, :].astype(F32).reshape(states, states)
        low = jnp.concatenate([y.astype(BF16), d.astype(BF16)], axis=1)
        terms = []
        for k in range(ops):
            half = (dot(left[k, s], low) * pattern[s, k].astype(F32)).astype(BF16)
            half = jnp.concatenate([half[:, :states], half[:, states:]], axis=0)
            terms.append(dot(half, right[k, s]))
        image = total_of(terms)
        y_hy.append(jnp.sum(y * image[:states], axis=0, keepdims=True))
        d_hy.append(jnp.sum(d * image[:states], axis=0, keepdims=True))
        d_hd.append(jnp.sum(d * image[states:], axis=0, keepdims=True))
    low = jnp.sum(kept[sectors * rows :, :], axis=1, keepdims=True)
    high = jnp.concatenate([total_of(y_hy), total_of(d_hy), total_of(d_hd), jnp.zeros((5, states), F32)], axis=0)
    high = jnp.sum(high, axis=1, keepdims=True)
    lane = lax.broadcasted_iota(jnp.int32, out.shape[1:], 1)
    tile = jnp.where(lane == 0, low, jnp.where(lane == 1, high, 0.0))
    out[...] = jnp.broadcast_to(tile[None], out.shape)


def gather_kernel(received, out):
    out[...] = jnp.broadcast_to(jnp.sum(received[...], axis=0)[None], out.shape)


def columns_kernel(received, after, out):
    del after
    width = received.shape[2]
    out[...] = received[:, received.shape[1] - width // received.shape[0] :, :].astype(F32).reshape(width, width).astype(BF16)


def renorm_kernel(core, left, mine, theirs, out):
    first = (core[0] == 0).astype(F32)
    a, b = mine[...].astype(F32), theirs[...].astype(F32)
    for s in range(left.shape[1]):
        turned = a * first + b * (1.0 - first) if s == 0 else b * first + a * (1.0 - first)
        rotation = jnp.transpose(turned).astype(BF16)
        turned = turned.astype(BF16)
        for k in range(left.shape[0]):
            rotated = dot(left[k, s], rotation).astype(BF16)
            out[k, s] = dot(turned, rotated).astype(BF16)


def state_kernel(entries, received, rows_in, kept, state, energy_out):
    sums = jnp.sum(received[...], axis=0)
    lane = lax.broadcasted_iota(jnp.int32, sums.shape, 1)
    low = jnp.sum(jnp.where(lane == 0, sums, 0.0), axis=1, keepdims=True)
    high = jnp.sum(jnp.where(lane == 1, sums, 0.0), axis=1, keepdims=True)
    gg, gh, gd, dd, gy, dy, yy, hy = [low[i : i + 1] for i in range(8)]
    y_hy, d_hy, d_hd = [high[i : i + 1] for i in range(3)]
    inverse = 1.0 / entries
    first_square = 1.0 / (gg * inverse + 1e-06)
    rho = first_square * gh * inverse
    kappa = first_square * (gy - rho * gd) * inverse
    qq = yy - 2.0 * rho * dy + rho * rho * dd - 2.0 * kappa * (gy - rho * gd) + kappa * kappa * gg
    hq = hy - rho * gy - kappa * gh
    q_hq = y_hy - 2.0 * rho * d_hy + rho * rho * d_hd - 2.0 * kappa * (hy - rho * gy) + kappa * kappa * gh
    second_square = 1.0 / (first_square * qq * inverse + 1e-06)
    second_scale = jnp.sqrt(second_square)
    first_scale = jnp.sqrt(first_square)
    coupling = second_scale * first_square * hq * inverse
    rho_second = second_square * first_square * q_hq * inverse
    half_gap = (rho - rho_second) * 0.5
    energy = (rho + rho_second) * 0.5 - jnp.sqrt(half_gap * half_gap + coupling * coupling)
    weight_first = rho_second - energy
    weight_second = -coupling
    scaling = 1.0 / jnp.sqrt(weight_first * weight_first + weight_second * weight_second)
    on_second = weight_second * second_scale * scaling * first_scale
    on_first = weight_first * scaling * first_scale
    energy_out[...] = jnp.broadcast_to(energy, energy_out.shape)
    g, d = rows_in[0], rows_in[1]
    y = kept[: g.shape[0] * g.shape[1], :].reshape(g.shape)
    state[...] = on_first[None] * g + on_second[None] * (y - rho[None] * d - kappa[None] * g)


def call(kernel, out_shape, in_specs, flops=0, scratch=(), limit=16):
    return pl.pallas_call(
        kernel,
        out_shape=out_shape,
        in_specs=in_specs,
        out_specs=jax.tree.map(lambda _: VMEM, out_shape),
        scratch_shapes=scratch,
        cost_estimate=pl.CostEstimate(flops=flops, bytes_accessed=1 << 20, transcendentals=0),
        compiler_params=pltpu.CompilerParams(vmem_limit_bytes=limit << 20),
    )


def local(left_hbm, right_hbm, pattern, guess, precond, rotation):
    ops, sectors, states = left_hbm.shape[:3]
    chips, cores, zones = (lax.axis_size(axis) for axis in ("chip", "core", "sec"))
    peers = chips * cores
    rows = states // peers
    me = lax.axis_index(OPS).reshape(1)
    core = lax.axis_index("core").reshape(1)
    entries = float(sectors * zones * states * states)
    shape = jax.ShapeDtypeStruct
    flops = 4 * ops * sectors * states**3
    pattern = jnp.swapaxes(pattern, 0, 1)
    columns = jnp.swapaxes(rotation, 1, 2)

    def in_hbm(x):
        return pltpu.with_memory_space_constraint(x, pltpu.HBM)

    chunks, left, right, level, own = call(
        partial_kernel,
        (
            shape((peers, (sectors + 1) * rows, states), BF16),
            shape(left_hbm.shape, BF16),
            shape(right_hbm.shape, BF16),
            shape(guess.shape, F32),
            shape((3, sectors, rows, states), F32),
        ),
        [SMEM, SMEM, HBM, HBM, HBM, HBM, VMEM],
        flops,
        [
            pltpu.VMEM(guess.shape, F32),
            pltpu.VMEM(guess.shape, F32),
            pltpu.SemaphoreType.DMA((ops, sectors)),
            pltpu.SemaphoreType.DMA((ops, sectors)),
            pltpu.SemaphoreType.DMA((sectors,)),
            pltpu.SemaphoreType.DMA((sectors,)),
        ],
    )(pattern, me, in_hbm(left_hbm), in_hbm(right_hbm), in_hbm(guess), in_hbm(precond), columns)
    received = lax.all_to_all(chunks, OPS, 0, 0)
    kept, chunks = call(
        rows_kernel,
        (shape(((sectors + 1) * rows, states), F32), shape((peers, sectors * rows, states), BF16)),
        [VMEM] * 2,
    )(received, own)
    gathered = lax.all_to_all(chunks, OPS, 0, 0)
    sums = call(second_kernel, shape((chips, 8, 128), F32), [SMEM] + [VMEM] * 5, 2 * flops)(
        pattern, gathered, left, right, level, kept
    )
    over_chips = lax.all_to_all(sums, "chip", 0, 0)
    sums = call(gather_kernel, shape((cores * zones, 8, 128), F32), [VMEM])(over_chips)
    sums = lax.all_to_all(sums, ("core", "sec"), 0, 0)

    mine = call(columns_kernel, shape((states, states), BF16), [VMEM] * 2)(received, over_chips)
    theirs = lax.ppermute(mine, "core", [(0, 1), (1, 0)])
    renormalized = call(renorm_kernel, shape(left.shape, BF16), [SMEM, VMEM, VMEM, VMEM], flops)(
        core, left, mine, theirs
    )
    new_state, energy = call(
        lambda *refs: state_kernel(entries, *refs),
        (shape((sectors, rows, states), F32), shape((1, 128), F32)),
        [VMEM] * 3,
    )(sums, own, kept)
    return new_state, energy[0, :1], renormalized


def solution(mesh):
    cores = 2
    mesh = Mesh(mesh.devices.reshape(-1, cores, mesh.shape["sec"]), ("chip", "core", "sec"))
    return jax.shard_map(
        local,
        mesh=mesh,
        in_specs=(
            P(OPS, "sec", None, None),
            P(OPS, "sec", None, None),
            P(OPS, "sec"),
            P("sec", None, None),
            P("sec", None, None),
            P("sec", None, OPS),
        ),
        out_specs=(P("sec", OPS, None), P(), P(OPS, "sec", None, None)),
        check_vma=False,
    )
```

time: 83 us -> 70.3 us (0.85)
  blocking collectives: 0 us -> 56 us
  waiting for transfers between devices: 27.5 us -> 0.01 us
  starting transfers between devices: 25.6 us -> 1.82 us
  local copies, waits for them, and re-layouts: 15.1 us -> 0.68 us
  Pallas kernels: 13.1 us -> 10.8 us
    all_to_all x0 -> x4, blocking collectives: none -> 56 us  [the longest x1 18.6 us: local(): received = lax.all_to_all(chunks, OPS, 0, 0)]
    all_to_all x4 -> x0, waiting for transfers between devices: 27.5 us -> none  [the longest x1 9.51 us: local(): received = lax.all_to_all(parts, OPS, 0, 0)]
    all_to_all x4 -> x0, starting transfers between devices: 25.2 us -> none  [the longest x1 8.72 us: local(): received = lax.all_to_all(parts, OPS, 0, 0)]
    unnamed x54 -> x4, local copies, waits for them, and re-layouts: 14.5 us -> 0.68 us
    pallas_call x8 -> x6, Pallas kernels: 11.2 us -> 8.89 us  [the longest x1 5.72 us: local(): call(partial_kernel, (shape((peers, (sectors + 1) * rows, states), BF16),...]
    ppermute x1, starting transfers between devices: 0.43 us -> 1.82 us  [local(): theirs = lax.ppermute(mine, 'core', [(0, 1), (1, 0)])]
  transfers between devices with their start and end apart: 5 -> 1, of which waited for: 4 -> 0; matrix products, arithmetic and copies ran while one was open for 1% -> 0% of each run, Pallas kernels for 5% -> 1%
where the time goes in v2:
time: 70.3 us; the launch traced here: 70.1 us
  blocking collectives  56 us (80%)
  Pallas kernels  10.8 us (15%)
  starting transfers between devices  1.82 us (3%)
    all_to_all x1, blocking collectives, local(): received = lax.all_to_all(chunks, OPS, 0, 0)  18.6 us
    all_to_all x1, blocking collectives, local(): sums = lax.all_to_all(sums, ('core', 'sec'), 0, 0)  15.6 us
    all_to_all x1, blocking collectives, local(): gathered = lax.all_to_all(chunks, OPS, 0, 0)  12.5 us
    all_to_all x1, blocking collectives, local(): over_chips = lax.all_to_all(sums, 'chip', 0, 0)  9.43 us
    pallas_call x1, Pallas kernels, local(): call(partial_kernel, (shape((peers, (sectors + 1) * rows, states), BF16),...  5.72 us
    pallas_call x1, Pallas kernels, local(): call(second_kernel, shape((chips, 8, 128), F32), [SMEM] + [VMEM] * 5, 2 *...  2.25 us
    pallas_call x1, Pallas kernels, local(): call(renorm_kernel, shape(left.shape, BF16), [SMEM, VMEM, VMEM, VMEM], fl...  1.95 us
    ppermute x1, starting transfers between devices, local(): theirs = lax.ppermute(mine, 'core', [(0, 1), (1, 0)])  1.82 us
  transfers between devices with their start and end apart: 1, of which 0 were waited for; matrix products, arithmetic and copies ran while one was open for 0% of the time, Pallas kernels for 1%

profile of v2, /device:TPU:1, one launch (start us, length us, event | category | flops | bytes accessed | tf_op | source)
XLA Modules:
  0.0 70.1 jit_solution(14600098677995965769)
XLA Ops:
  0.6 0.0 copy-start
  0.6 0.0 copy-start.1
  0.7 0.7 copy-done
  1.3 0.0 copy-done.1
  1.3 5.7 %shard_map.85 = (bf16[32,24,256]{2,1,0:T(8,128)(2,1)S(1)}, bf16[4,2,256,256]{3,2,1,0:T(8,128)(2,1)S(1)}, bf16[4,2,256,256]{3,2,1,0:T(8,128)(2,1)S(1)}, f32[2,256,256]{2,1,0:T(8,128)S(1)}, f32[3,2,8,256]{3,2,1,0:T(8,128)S(1)}) custom-call(s32[2,4]{1,0:T(2,128)S(1)} %bitcast.7, s32[1]{0:T(128)} %bitcast.1.me, bf16[4,2,256,256]{3,2,1,0:T(8,128)(2,1)} %left_hbm.1, ...), custom_call_target="tpu_custom_call" | custom-call | flops 536870912 | bytes 1048576 | tf_op jit(solution)/shard_map/pallas_call | solution.py:196
  7.1 18.6 %all_to_all.20.received = bf16[32,24,256]{2,1,0:T(8,128)(2,1)S(1)} all-to-all(bf16[32,24,256]{2,1,0:T(8,128)(2,1)S(1)} %get-tuple-element.12), channel_id=1, replica_groups=mesh['chip'=16,'core'=2,'sec'=8] {'chip','core'}, dimensions={0} | all-to-all | bytes 786432 | tf_op jit(solution)/shard_map/all_to_all | solution.py:216
  25.6 0.1 shard_map.86
  25.7 12.5 %all_to_all.21.received = bf16[32,16,256]{2,1,0:T(8,128)(2,1)S(1)} all-to-all(bf16[32,16,256]{2,1,0:T(8,128)(2,1)S(1)} %get-tuple-element.14), channel_id=1, replica_groups=mesh['chip'=16,'core'=2,'sec'=8] {'chip','core'}, dimensions={0} | all-to-all | bytes 524288 | tf_op jit(solution)/shard_map/all_to_all | solution.py:222
  38.2 2.3 %shard_map.87 = f32[16,8,128]{2,1,0:T(8,128)S(1)} custom-call(s32[2,4]{1,0:T(2,128)S(1)} %bitcast.8, bf16[32,16,256]{2,1,0:T(8,128)(2,1)S(1)} %all_to_all.21.received, bf16[4,2,256,256]{3,2,1,0:T(8,128)(2,1)S(1)} %get-tuple-element.15.left, bf16[4,2,256,256]{3,2,1,0:T(8,128)(2,1)S(1)} %get-tuple-element.16.right, ...), custom_call_target="tpu_custom_call" | custom-call | flops 1073741824 | bytes 1048576 | tf_op jit(solution)/shard_map/pallas_call | solution.py:223
  40.4 9.4 %all_to_all.22.received.after = f32[16,8,128]{2,1,0:T(8,128)S(1)} all-to-all(f32[16,8,128]{2,1,0:T(8,128)S(1)} %shard_map.87), channel_id=1, replica_groups=mesh['chip'=16,'core'=2,'sec'=8] {'chip'}, dimensions={0} | all-to-all | bytes 131072 | tf_op jit(solution)/shard_map/all_to_all | solution.py:226
  49.9 1.8 %collective-permute-start = (bf16[256,256]{1,0:T(8,128)(2,1)S(1)}, bf16[256,256]{1,0:T(8,128)(2,1)S(1)}, u32[]{:S(2)}, u32[]{:S(2)}) collective-permute-start(bf16[256,256]{1,0:T(8,128)(2,1)S(1)} %shard_map.90.mine), channel_id=1, source_target_pairs={{0,8},{8,0},{1,9},{9,1},{2,10},{10,2},{3,11},{11,3},{4,12},{12,4},... | collective-permute-start | bytes 393224 | tf_op jit(solution)/shard_map/ppermute | solution.py:231
  51.7 15.6 %all_to_all.23.refs_0_ = f32[16,8,128]{2,1,0:T(8,128)S(1)} all-to-all(f32[16,8,128]{2,1,0:T(8,128)S(1)} %shard_map.88), channel_id=1, replica_groups=mesh['chip'=16,'core'=2,'sec'=8] {'core','sec'}, dimensions={0} | all-to-all | bytes 131072 | tf_op jit(solution)/shard_map/all_to_all | solution.py:228
  67.3 0.8 %shard_map.89 = (f32[2,8,256]{2,1,0:T(8,128)}, f32[1,128]{1,0:T(1,128)}) custom-call(f32[16,8,128]{2,1,0:T(8,128)S(1)} %all_to_all.23.refs_0_, f32[3,2,8,256]{3,2,1,0:T(8,128)S(1)} %get-tuple-element.13.rows_in.refs_1_, f32[24,256]{1,0:T(8,128)S(1)} %get-tuple-element.18.kept.refs_2_), custom_call_target="tpu_custom_call" | custom-call | bytes 1048576 | tf_op jit(solution)/shard_map/pallas_call | solution.py:235
  68.1 0.0 collective-permute-done.theirs
  68.1 2.0 %shard_map.91 = bf16[4,2,256,256]{3,2,1,0:T(8,128)(2,1)} custom-call(s32[1]{0:T(128)} %bitcast.4.core, bf16[4,2,256,256]{3,2,1,0:T(8,128)(2,1)S(1)} %get-tuple-element.15.left, bf16[256,256]{1,0:T(8,128)(2,1)S(1)} %shard_map.90.mine, bf16[256,256]{1,0:T(8,128)(2,1)S(1)} %collective-permute-done.theirs), custom_call_target="tpu_custom_call" | custom-call | flops 536870912 | bytes 1048576 | tf_op jit(solution)/shard_map/pallas_call | solution.py:232
  (2 shorter events, 0.0 us)
Async XLA Ops:
  0.6 0.7 copy-start
  0.6 0.7 copy-start.1
  49.9 18.2 %collective-permute-start = (bf16[256,256]{1,0:T(8,128)(2,1)S(1)}, bf16[256,256]{1,0:T(8,128)(2,1)S(1)}, u32[]{:S(2)}, u32[]{:S(2)}) collective-permute-start(bf16[256,256]{1,0:T(8,128)(2,1)S(1)} %shard_map.90.mine), channel_id=1, source_target_pairs={{0,8},{8,0},{1,9},{9,1},{2,10},{10,2},{3,11},{11,3},{4,12},{12,4},... | collective-permute-start | bytes 393224 | tf_op jit(solution)/shard_map/ppermute | solution.py:231

commit v3 on v2

v3 whole, which is shorter than its diff:
```python
import jax
import jax.numpy as jnp
from jax import lax
from jax.experimental import pallas as pl
from jax.experimental.pallas import tpu as pltpu
from jax.sharding import Mesh, PartitionSpec as P

F32 = jnp.float32
BF16 = jnp.bfloat16
OPS = ("chip", "core")
SWAP = [(0, 1), (1, 0)]
VMEM = pl.BlockSpec(memory_space=pltpu.VMEM)
SMEM = pl.BlockSpec(memory_space=pltpu.SMEM)
HBM = pl.BlockSpec(memory_space=pltpu.HBM)


def dot(a, b):
    return jnp.dot(a, b, preferred_element_type=F32)


def halves_of(left, s, flags, x):
    terms = x.shape[0] // left.shape[3]
    halves = []
    for k in range(left.shape[0]):
        block = left[k, s]
        half = dot(jnp.concatenate([block] * terms, axis=1), x)
        halves.append(half.astype(BF16) * flags(s, k))
    return halves


def in_rows(ref):
    return lambda s, k: ref[s, pl.ds(k, 1), :].astype(BF16)


def closed(halves, right, s):
    return dot(jnp.concatenate(halves, axis=1), right[:, s].reshape(-1, right.shape[3]))


def two_terms(x):
    high = x.astype(BF16)
    return jnp.concatenate([high, (x - high.astype(F32)).astype(BF16)], axis=0)


def other_kernel(
    core, chip, pattern_hbm, left_hbm, right_hbm, guess_hbm,
    part, left, right, guess, flags,
    pattern, pattern_sem, guess_sem, left_sem, right_sem,
):
    del chip
    mine = core[0]
    other = 1 - mine
    first = pltpu.make_async_copy(pattern_hbm, pattern, pattern_sem)
    first.start()
    copies = []
    for i, s in enumerate((other, mine)):
        copies.append(
            [
                pltpu.make_async_copy(guess_hbm.at[s], guess.at[s], guess_sem.at[i]),
                pltpu.make_async_copy(left_hbm.at[:, s], left.at[:, s], left_sem.at[i]),
                pltpu.make_async_copy(right_hbm.at[:, s], right.at[:, s], right_sem.at[i]),
            ]
        )
        for copy in copies[i]:
            copy.start()
    first.wait()
    for s in range(left.shape[1]):
        for k in range(left.shape[0]):
            flags[s, pl.ds(k, 1), :] = jnp.full((1, flags.shape[2]), pattern[s, k].astype(F32))
    copies[0][0].wait()
    copies[0][1].wait()
    halves = halves_of(left, other, in_rows(flags), two_terms(guess[other]))
    copies[0][2].wait()
    part[...] = closed(halves, right, other).astype(BF16)
    for copy in copies[1]:
        copy.wait()


def own_kernel(core, chip, flags, left, right, guess, precond_hbm, part, level, rows_out, state_rows, precond, precond_sem):
    mine = core[0]
    copy = pltpu.make_async_copy(precond_hbm, precond, precond_sem)
    copy.start()
    part[...] = closed(halves_of(left, mine, in_rows(flags), two_terms(guess[mine])), right, mine)
    copy.wait()
    level[...] = guess[...] / precond[...]
    count = rows_out.shape[1]
    own = pl.ds(pl.multiple_of(chip[0] * count, count), count)
    for i, ref in enumerate((guess, level, precond)):
        rows_out[i] = ref[mine, own, :]
    count = state_rows.shape[2]
    own = pl.ds(pl.multiple_of((chip[0] * 2 + mine) * count, count), count)
    for i, ref in enumerate((guess, level)):
        for s in range(ref.shape[0]):
            state_rows[i, s] = ref[s, own, :]


def chunks_kernel(core, own, theirs, columns, columns_theirs, chunks):
    mine = core[0]
    total = own[...] + theirs[...].astype(F32)
    a, b = columns[mine].astype(F32), columns_theirs[mine].astype(F32)
    first = (mine == 0).astype(F32)
    turned = jnp.concatenate([a * first + b * (1.0 - first), b * first + a * (1.0 - first)], axis=0)
    chips, count, states = chunks.shape
    turned = jnp.broadcast_to(turned[None], (chips,) + turned.shape)
    chunks[...] = jnp.concatenate([total.reshape(chips, -1, states), turned], axis=1).astype(BF16)


def rows_kernel(received, rows_in, kept, sums, rotation, chunks):
    g, d, p = rows_in[0], rows_in[1], rows_in[2]
    count, states = g.shape
    h = jnp.sum(received[:, :count, :].astype(F32), axis=0)
    rotation[...] = received[:, count:, :].reshape(states, states)
    y = h / p
    pairs = ((g, g), (g, h), (g, d), (d, d), (g, y), (d, y), (y, y), (h, y))
    sums[...] = jnp.concatenate([jnp.sum(a * b, axis=0, keepdims=True) for a, b in pairs], axis=0)
    kept[...] = y
    chunks[...] = jnp.broadcast_to(y[None].astype(BF16), chunks.shape)


def renorm_kernel(core, flags, left, right, level, mine, theirs, kept, kept_theirs, out, d_hd, state_y):
    count = state_y.shape[1]
    own = pl.ds(pl.multiple_of(core[0] * count, count), count)
    state_y[core[0]] = kept[own, :]
    state_y[1 - core[0]] = kept_theirs[own, :]
    first = (core[0] == 0).astype(F32)
    a, b = mine[...].astype(F32), theirs[...].astype(F32)
    dots = []
    for s in range(left.shape[1]):
        turned = a * first + b * (1.0 - first) if s == 0 else b * first + a * (1.0 - first)
        rotation = jnp.transpose(turned).astype(BF16)
        turned = turned.astype(BF16)
        for k in range(left.shape[0]):
            rotated = dot(left[k, s], rotation).astype(BF16)
            out[k, s] = dot(turned, rotated).astype(BF16)
        d = level[s]
        image = closed(halves_of(left, s, in_rows(flags), d.astype(BF16)), right, s)
        dots.append(jnp.sum(d * image, axis=0, keepdims=True))
    d_hd[...] = dots[0] + dots[1]


def dots_of(s, flags, y, left, right, level):
    image = closed(halves_of(left, s, in_rows(flags), y), right, s)
    y_hy = jnp.sum(y.astype(F32) * image, axis=0, keepdims=True)
    d_hy = jnp.sum(level[s] * image, axis=0, keepdims=True)
    return jnp.concatenate([y_hy, d_hy], axis=0)


def own_dots_kernel(core, flags, gathered, left, right, level, d_hd, out):
    y = gathered[...].reshape(left.shape[2:])
    out[...] = jnp.concatenate([dots_of(core[0], flags, y, left, right, level), d_hd[...]], axis=0)


def other_dots_kernel(core, flags, gathered, left, right, level, own_dots, row_sums, out):
    y = gathered[...].reshape(left.shape[2:])
    dots = dots_of(1 - core[0], flags, y, left, right, level)
    low = jnp.sum(row_sums[...], axis=1, keepdims=True)
    high = jnp.concatenate([own_dots[...], dots, jnp.zeros((3, y.shape[1]), F32)], axis=0)
    high = jnp.sum(high, axis=1, keepdims=True)
    lane = lax.broadcasted_iota(jnp.int32, out.shape[1:], 1)
    tile = jnp.where(lane == 0, low, jnp.where(lane == 1, high, 0.0))
    out[...] = jnp.broadcast_to(tile[None], out.shape)


def gather_kernel(received, out):
    out[...] = jnp.broadcast_to(jnp.sum(received[...], axis=0)[None], out.shape)


def state_kernel(entries, received, state_rows, state_y, state, energy_out):
    sums = jnp.sum(received[...], axis=0)
    lane = lax.broadcasted_iota(jnp.int32, sums.shape, 1)
    low = jnp.sum(jnp.where(lane == 0, sums, 0.0), axis=1, keepdims=True)
    high = jnp.sum(jnp.where(lane == 1, sums, 0.0), axis=1, keepdims=True)
    gg, gh, gd, dd, gy, dy, yy, hy = [low[i : i + 1] for i in range(8)]
    y_hy, d_hy, d_hd = high[0:1] + high[3:4], high[1:2] + high[4:5], high[2:3]
    inverse = 1.0 / entries
    first_square = 1.0 / (gg * inverse + 1e-06)
    rho = first_square * gh * inverse
    kappa = first_square * (gy - rho * gd) * inverse
    qq = yy - 2.0 * rho * dy + rho * rho * dd - 2.0 * kappa * (gy - rho * gd) + kappa * kappa * gg
    hq = hy - rho * gy - kappa * gh
    q_hq = y_hy - 2.0 * rho * d_hy + rho * rho * d_hd - 2.0 * kappa * (hy - rho * gy) + kappa * kappa * gh
    second_square = 1.0 / (first_square * qq * inverse + 1e-06)
    second_scale = jnp.sqrt(second_square)
    first_scale = jnp.sqrt(first_square)
    coupling = second_scale * first_square * hq * inverse
    rho_second = second_square * first_square * q_hq * inverse
    half_gap = (rho - rho_second) * 0.5
    energy = (rho + rho_second) * 0.5 - jnp.sqrt(half_gap * half_gap + coupling * coupling)
    weight_first = rho_second - energy
    weight_second = -coupling
    scaling = 1.0 / jnp.sqrt(weight_first * weight_first + weight_second * weight_second)
    on_second = weight_second * second_scale * scaling * first_scale
    on_first = weight_first * scaling * first_scale
    energy_out[...] = jnp.broadcast_to(energy, energy_out.shape)
    g, d, y = state_rows[0], state_rows[1], state_y[...]
    state[...] = on_first[None] * g + on_second[None] * (y - rho[None] * d - kappa[None] * g)


def call(kernel, out_shape, in_specs, flops=0, scratch=(), limit=16):
    return pl.pallas_call(
        kernel,
        out_shape=out_shape,
        in_specs=in_specs,
        out_specs=jax.tree.map(lambda _: VMEM, out_shape),
        scratch_shapes=scratch,
        cost_estimate=pl.CostEstimate(flops=flops, bytes_accessed=1 << 20, transcendentals=0),
        compiler_params=pltpu.CompilerParams(vmem_limit_bytes=limit << 20),
    )


def local(left_hbm, right_hbm, pattern, guess_hbm, precond_hbm, rotation):
    ops, sectors, states = left_hbm.shape[:3]
    chips, cores, zones = (lax.axis_size(axis) for axis in ("chip", "core", "sec"))
    count = states // chips
    core = lax.axis_index("core").reshape(1)
    chip = lax.axis_index("chip").reshape(1)
    entries = float(sectors * zones * states * states)
    shape = jax.ShapeDtypeStruct
    dma = pltpu.SemaphoreType.DMA
    block = (states, states)
    flops = 4 * ops * sectors * states**3
    pattern = jnp.swapaxes(pattern, 0, 1)
    columns = jnp.swapaxes(rotation, 1, 2)

    def in_hbm(x):
        return pltpu.with_memory_space_constraint(x, pltpu.HBM)

    def swapped(x):
        return lax.ppermute(x, "core", SWAP)

    columns_theirs = swapped(columns)
    part, left, right, guess, flags = call(
        other_kernel,
        (
            shape(block, BF16),
            shape(left_hbm.shape, BF16),
            shape(right_hbm.shape, BF16),
            shape(guess_hbm.shape, F32),
            shape((sectors, ops, states), F32),
        ),
        [SMEM] * 2 + [HBM] * 4,
        flops // 2,
        [pltpu.SMEM(pattern.shape, jnp.int32), dma, dma((2,)), dma((2,)), dma((2,))],
    )(core, chip, *(in_hbm(x) for x in (pattern, left_hbm, right_hbm, guess_hbm)))
    theirs = swapped(part)
    own, level, own_rows, state_rows = call(
        own_kernel,
        (
            shape(block, F32),
            shape(guess.shape, F32),
            shape((3, count, states), F32),
            shape((2, sectors, count // cores, states), F32),
        ),
        [SMEM] * 2 + [VMEM] * 4 + [HBM],
        flops // 2,
        [pltpu.VMEM(guess.shape, F32), dma],
    )(core, chip, flags, left, right, guess, in_hbm(precond_hbm))
    chunks = call(chunks_kernel, shape((chips, 2 * count, states), BF16), [SMEM] + [VMEM] * 4)(
        core, own, theirs, columns, columns_theirs
    )
    received = lax.all_to_all(chunks, "chip", 0, 0)
    kept, row_sums, mine, chunks = call(
        rows_kernel,
        (
            shape((count, states), F32),
            shape((8, states), F32),
            shape(block, BF16),
            shape((chips, count, states), BF16),
        ),
        [VMEM] * 2,
    )(received, own_rows)
    gathered = lax.all_to_all(chunks, "chip", 0, 0)
    renormalized, d_hd, state_y = call(
        renorm_kernel,
        (shape(left.shape, BF16), shape((1, states), F32), shape((sectors, count // cores, states), F32)),
        [SMEM] + [VMEM] * 8,
        2 * flops,
    )(core, flags, left, right, level, mine, swapped(mine), kept, swapped(kept))
    gathered, d_hd = lax.optimization_barrier((gathered, d_hd))
    gathered_theirs = swapped(gathered)
    dots = call(own_dots_kernel, shape((3, states), F32), [SMEM] + [VMEM] * 6, flops // 2)(
        core, flags, gathered, left, right, level, d_hd
    )
    sums = call(other_dots_kernel, shape((chips, 8, 128), F32), [SMEM] + [VMEM] * 7, flops // 2)(
        core, flags, gathered_theirs, left, right, level, dots, row_sums
    )
    sums = lax.all_to_all(sums, "chip", 0, 0)
    sums = call(gather_kernel, shape((cores * zones, 8, 128), F32), [VMEM])(sums)
    sums = lax.all_to_all(sums, ("core", "sec"), 0, 0)
    new_state, energy = call(
        lambda *refs: state_kernel(entries, *refs),
        (shape((sectors, count // cores, states), F32), shape((1, 128), F32)),
        [VMEM] * 3,
    )(sums, state_rows, state_y)
    return new_state, energy[0, :1], renormalized


def solution(mesh):
    cores = 2
    mesh = Mesh(mesh.devices.reshape(-1, cores, mesh.shape["sec"]), ("chip", "core", "sec"))
    return jax.shard_map(
        local,
        mesh=mesh,
        in_specs=(
            P(OPS, "sec", None, None),
            P(OPS, "sec", None, None),
            P(OPS, "sec"),
            P("sec", None, None),
            P("sec", None, None),
            P("sec", None, OPS),
        ),
        out_specs=(P("sec", OPS, None), P(), P(OPS, "sec", None, None)),
        check_vma=False,
    )
```

time: 70.3 us -> 63.7 us (0.906)
  blocking collectives: 56 us -> 39.4 us
  starting transfers between devices: 1.82 us -> 9.51 us
  waiting for transfers between devices: 0.01 us -> 4.94 us
  Pallas kernels: 10.8 us -> 8.72 us
    all_to_all x3 -> x2, blocking collectives: 40.5 us -> 22.2 us  [the longest x1 12.9 us: local(): received = lax.all_to_all(chunks, 'chip', 0, 0)]
    ppermute x1 -> x5, starting transfers between devices: 1.82 us -> 6 us  [swapped(): return lax.ppermute(x, 'core', SWAP)]
    all_to_all x0 -> x1, starting transfers between devices: none -> 3.51 us  [local(): gathered = lax.all_to_all(chunks, 'chip', 0, 0)]
    all_to_all x0 -> x1, waiting for transfers between devices: none -> 3.33 us  [local(): gathered = lax.all_to_all(chunks, 'chip', 0, 0)]
    pallas_call x7 -> x9, Pallas kernels: 10.8 us -> 8.72 us  [the longest x1 2.68 us: local(): call(renorm_kernel, (shape(left.shape, BF16), shape((1, states), F32), sh...]
    all_to_all x1, blocking collectives: 15.6 us -> 17.2 us  [local(): sums = lax.all_to_all(sums, ('core', 'sec'), 0, 0)]
    ppermute x1 -> x5, waiting for transfers between devices: 0.01 us -> 1.61 us  [swapped(): return lax.ppermute(x, 'core', SWAP)]
  transfers between devices with their start and end apart: 1 -> 6, of which waited for: 0 -> 3; matrix products, arithmetic and copies ran while one was open for 0% -> 0% of each run, Pallas kernels for 1% -> 7%
where the time goes in v3:
time: 63.7 us; the launch traced here: 63.3 us
  blocking collectives  39.4 us (62%)
  starting transfers between devices  9.51 us (15%)
  Pallas kernels  8.72 us (14%)
  waiting for transfers between devices  4.94 us (8%)
  between operations  0.72 us (1%)
    all_to_all x1, blocking collectives, local(): sums = lax.all_to_all(sums, ('core', 'sec'), 0, 0)  17.2 us
    all_to_all x1, blocking collectives, local(): received = lax.all_to_all(chunks, 'chip', 0, 0)  12.9 us
    all_to_all x1, blocking collectives, local(): sums = lax.all_to_all(sums, 'chip', 0, 0)  9.31 us
    ppermute x5, starting transfers between devices, swapped(): return lax.ppermute(x, 'core', SWAP)  6 us
    all_to_all x1, starting transfers between devices, local(): gathered = lax.all_to_all(chunks, 'chip', 0, 0)  3.51 us
    all_to_all x1, waiting for transfers between devices, local(): gathered = lax.all_to_all(chunks, 'chip', 0, 0)  3.33 us
    pallas_call x1, Pallas kernels, local(): call(renorm_kernel, (shape(left.shape, BF16), shape((1, states), F32), sh...  2.68 us
    pallas_call x1, Pallas kernels, local(): call(other_kernel, (shape(block, BF16), shape(left_hbm.shape, BF16), shap...  2.18 us
  transfers between devices with their start and end apart: 6, of which 3 were waited for; matrix products, arithmetic and copies ran while one was open for 0% of the time, Pallas kernels for 7%

profile of v3, /device:TPU:1, one launch (start us, length us, event | category | flops | bytes accessed | tf_op | source)
XLA Modules:
  0.0 63.3 jit_solution(14482896080854340101)
XLA Ops:
  0.6 0.0 copy-start
  0.6 2.2 %shard_map.85 = (bf16[256,256]{1,0:T(8,128)(2,1)S(1)}, bf16[4,2,256,256]{3,2,1,0:T(8,128)(2,1)S(1)}, bf16[4,2,256,256]{3,2,1,0:T(8,128)(2,1)S(1)}, f32[2,256,256]{2,1,0:T(8,128)S(1)}, f32[2,4,256]{2,1,0:T(4,128)S(1)}) custom-call(s32[1]{0:T(128)} %bitcast.core, s32[1]{0:T(128)} %bitcast.1.chip, s32[2,4]{1,0:T(2,128)} %bitcast.8, ...), custom_call_target="tpu_custom_call" | custom-call | flops 268435456 | bytes 1048576 | tf_op jit(solution)/shard_map/pallas_call | solution.py:231
  2.8 3.3 %collective-permute-start = (bf16[256,256]{1,0:T(8,128)(2,1)S(1)}, bf16[256,256]{1,0:T(8,128)(2,1)S(1)}, u32[]{:S(2)}, u32[]{:S(2)}) collective-permute-start(bf16[256,256]{1,0:T(8,128)(2,1)S(1)} %get-tuple-element.28), channel_id=1, source_target_pairs={{0,8},{8,0},{1,9},{9,1},{2,10},{10,2},{3,11},{11,3},{4,12},{12,4},... | collective-permute-start | bytes 393224 | tf_op jit(solution)/shard_map/ppermute | solution.py:228
  6.2 0.0 copy-done
  6.2 0.1 collective-permute-start.1
  6.3 1.1 %shard_map.86 = (f32[256,256]{1,0:T(8,128)S(1)}, f32[2,256,256]{2,1,0:T(8,128)S(1)}, f32[3,16,256]{2,1,0:T(8,128)S(1)}, f32[2,2,8,256]{3,2,1,0:T(8,128)S(1)}) custom-call(s32[1]{0:T(128)} %bitcast.core, s32[1]{0:T(128)} %bitcast.1.chip, f32[2,4,256]{2,1,0:T(4,128)S(1)} %get-tuple-element.23.flags, bf16[4,2,256,256]{3,2,1,0:T(8,128)(2,1)S(1)} %get-tuple-element.24.left, ...), custom_call_target="tpu_custom_call" | custom-call | flops 268435456 | bytes 1048576 | tf_op jit(solution)/shard_map/pallas_call | solution.py:245
  7.4 0.0 collective-permute-done.1.columns_theirs
  7.4 0.0 collective-permute-done.theirs
  7.5 12.9 %all_to_all.20.received = bf16[16,32,256]{2,1,0:T(8,128)(2,1)S(1)} all-to-all(bf16[16,32,256]{2,1,0:T(8,128)(2,1)S(1)} %shard_map.87), channel_id=1, replica_groups=mesh['chip'=16,'core'=2,'sec'=8] {'chip'}, dimensions={0} | all-to-all | bytes 524288 | tf_op jit(solution)/shard_map/all_to_all | solution.py:260
  20.4 0.7 %shard_map.88 = (f32[16,256]{1,0:T(8,128)S(1)}, f32[8,256]{1,0:T(8,128)S(1)}, bf16[256,256]{1,0:T(8,128)(2,1)S(1)}, bf16[16,16,256]{2,1,0:T(8,128)(2,1)}) custom-call(bf16[16,32,256]{2,1,0:T(8,128)(2,1)S(1)} %all_to_all.20.received, f32[3,16,256]{2,1,0:T(8,128)S(1)} %get-tuple-element.29.rows_in), custom_call_target="tpu_custom_call" | custom-call | bytes 1048576 | tf_op jit(solution)/shard_map/pallas_call | solution.py:261
  21.1 1.6 %collective-permute-start.2 = (bf16[256,256]{1,0:T(8,128)(2,1)S(1)}, bf16[256,256]{1,0:T(8,128)(2,1)S(1)}, u32[]{:S(2)}, u32[]{:S(2)}) collective-permute-start(bf16[256,256]{1,0:T(8,128)(2,1)S(1)} %get-tuple-element.32.mine), channel_id=1, source_target_pairs={{0,8},{8,0},{1,9},{9,1},{2,10},{10,2},{3,11},{11,3},{4,12},{12,4},... | collective-permute-start | bytes 393224 | tf_op jit(solution)/shard_map/ppermute | solution.py:228
  22.6 3.5 %all-to-all-start.1 = ((bf16[16,16,256]{2,1,0:T(8,128)(2,1)}), bf16[16,16,256]{2,1,0:T(8,128)(2,1)S(1)}, u32[]{:S(2)}, u32[]{:S(2)}) async-start(bf16[16,16,256]{2,1,0:T(8,128)(2,1)} %get-tuple-element.30), calls=%async_computation.1 | async-start | bytes 262144 | tf_op jit(solution)/shard_map/all_to_all | solution.py:271
  26.1 0.1 collective-permute-start.3
  26.2 1.2 %collective-permute-done.3.kept_theirs = f32[16,256]{1,0:T(8,128)S(1)} collective-permute-done((f32[16,256]{1,0:T(8,128)S(1)}, f32[16,256]{1,0:T(8,128)S(1)}, u32[]{:S(2)}, u32[]{:S(2)}) %collective-permute-start.3) | collective-permute-done | bytes 16416 | tf_op jit(solution)/shard_map/ppermute | solution.py:228
  27.4 0.0 collective-permute-done.2.theirs
  27.4 2.7 %shard_map.89 = (bf16[4,2,256,256]{3,2,1,0:T(8,128)(2,1)}, f32[1,256]{1,0:T(1,128)S(1)}, f32[2,8,256]{2,1,0:T(8,128)S(1)}) custom-call(s32[1]{0:T(128)} %bitcast.core, f32[2,4,256]{2,1,0:T(4,128)S(1)} %get-tuple-element.23.flags, bf16[4,2,256,256]{3,2,1,0:T(8,128)(2,1)S(1)} %get-tuple-element.24.left, bf16[4,2,256,256]{3,2,1,0:T(8,128)(2,1)S(1)} %get-tuple-element.25.right, ...), custom_call_target="tpu_custom_call" | custom-call | flops 1073741824 | bytes 1048576 | tf_op jit(solution)/shard_map/pallas_call | solution.py:272
  30.1 3.3 %all-to-all-done.1.gathered = bf16[16,16,256]{2,1,0:T(8,128)(2,1)S(1)} async-done(((bf16[16,16,256]{2,1,0:T(8,128)(2,1)}), bf16[16,16,256]{2,1,0:T(8,128)(2,1)S(1)}, u32[]{:S(2)}, u32[]{:S(2)}) %all-to-all-start.1) | async-done | bytes 131104 | tf_op jit(solution)/shard_map/all_to_all | solution.py:271
  33.4 0.9 %collective-permute-start.4 = (bf16[16,16,256]{2,1,0:T(8,128)(2,1)S(1)}, bf16[16,16,256]{2,1,0:T(8,128)(2,1)S(1)}, u32[]{:S(2)}, u32[]{:S(2)}) collective-permute-start(bf16[16,16,256]{2,1,0:T(8,128)(2,1)S(1)} %all-to-all-done.1.gathered), channel_id=1, source_target_pairs={{0,8},{8,0},{1,9},{9,1},{2,10},{10,2},{3,11},{11,3},{4,12},{12,4},... | collective-permute-start | bytes 393224 | tf_op jit(solution)/shard_map/ppermute | solution.py:228
  34.3 0.6 shard_map.90.own_dots
  34.9 0.4 collective-permute-done.4.gathered
  35.3 0.6 shard_map.91
  35.9 9.3 %all_to_all.21.received = f32[16,8,128]{2,1,0:T(8,128)S(1)} all-to-all(f32[16,8,128]{2,1,0:T(8,128)S(1)} %shard_map.91), channel_id=1, replica_groups=mesh['chip'=16,'core'=2,'sec'=8] {'chip'}, dimensions={0} | all-to-all | bytes 131072 | tf_op jit(solution)/shard_map/all_to_all | solution.py:286
  45.3 17.2 %all_to_all.22.refs_0_ = f32[16,8,128]{2,1,0:T(8,128)S(1)} all-to-all(f32[16,8,128]{2,1,0:T(8,128)S(1)} %shard_map.92), channel_id=1, replica_groups=mesh['chip'=16,'core'=2,'sec'=8] {'core','sec'}, dimensions={0} | all-to-all | bytes 131072 | tf_op jit(solution)/shard_map/all_to_all | solution.py:288
  62.5 0.8 %shard_map.93 = (f32[2,8,256]{2,1,0:T(8,128)}, f32[1,128]{1,0:T(1,128)}) custom-call(f32[16,8,128]{2,1,0:T(8,128)S(1)} %all_to_all.22.refs_0_, f32[2,2,8,256]{3,2,1,0:T(8,128)S(1)} %get-tuple-element.38.refs_1_, f32[2,8,256]{2,1,0:T(8,128)S(1)} %get-tuple-element.39.refs_2_), custom_call_target="tpu_custom_call" | custom-call | bytes 1048576 | tf_op jit(solution)/shard_map/pallas_call | solution.py:289
  (2 shorter events, 0.1 us)
Async XLA Ops:
  0.6 5.5 %copy-start = (bf16[2,256,8]{1,2,0:T(8,128)(2,1)S(1)}, bf16[2,256,8]{1,2,0:T(8,128)(2,1)}, u32[]{:S(2)}) copy-start(bf16[2,256,8]{1,2,0:T(8,128)(2,1)} %param.11) | copy-start | bytes 24580
  2.8 4.6 %collective-permute-start = (bf16[256,256]{1,0:T(8,128)(2,1)S(1)}, bf16[256,256]{1,0:T(8,128)(2,1)S(1)}, u32[]{:S(2)}, u32[]{:S(2)}) collective-permute-start(bf16[256,256]{1,0:T(8,128)(2,1)S(1)} %get-tuple-element.28), channel_id=1, source_target_pairs={{0,8},{8,0},{1,9},{9,1},{2,10},{10,2},{3,11},{11,3},{4,12},{12,4},... | collective-permute-start | bytes 393224 | tf_op jit(solution)/shard_map/ppermute | solution.py:228
  6.2 1.2 %collective-permute-start.1 = (bf16[2,8,256]{2,1,0:T(8,128)(2,1)S(1)}, bf16[2,8,256]{2,1,0:T(8,128)(2,1)S(1)}, u32[]{:S(2)}, u32[]{:S(2)}) collective-permute-start(bf16[2,8,256]{2,1,0:T(8,128)(2,1)S(1)} %bitcast.6), channel_id=1, source_target_pairs={{0,8},{8,0},{1,9},{9,1},{2,10},{10,2},{3,11},{11,3},{4,12},{12,4},... | collective-permute-start | bytes 24584 | tf_op jit(solution)/shard_map/ppermute | solution.py:228
  21.1 6.3 %collective-permute-start.2 = (bf16[256,256]{1,0:T(8,128)(2,1)S(1)}, bf16[256,256]{1,0:T(8,128)(2,1)S(1)}, u32[]{:S(2)}, u32[]{:S(2)}) collective-permute-start(bf16[256,256]{1,0:T(8,128)(2,1)S(1)} %get-tuple-element.32.mine), channel_id=1, source_target_pairs={{0,8},{8,0},{1,9},{9,1},{2,10},{10,2},{3,11},{11,3},{4,12},{12,4},... | collective-permute-start | bytes 393224 | tf_op jit(solution)/shard_map/ppermute | solution.py:228
  22.6 10.8 %all-to-all-start.1 = ((bf16[16,16,256]{2,1,0:T(8,128)(2,1)}), bf16[16,16,256]{2,1,0:T(8,128)(2,1)S(1)}, u32[]{:S(2)}, u32[]{:S(2)}) async-start(bf16[16,16,256]{2,1,0:T(8,128)(2,1)} %get-tuple-element.30), calls=%async_computation.1 | async-start | bytes 262144 | tf_op jit(solution)/shard_map/all_to_all | solution.py:271
  26.1 1.3 %collective-permute-start.3 = (f32[16,256]{1,0:T(8,128)S(1)}, f32[16,256]{1,0:T(8,128)S(1)}, u32[]{:S(2)}, u32[]{:S(2)}) collective-permute-start(f32[16,256]{1,0:T(8,128)S(1)} %get-tuple-element.33.kept), channel_id=1, source_target_pairs={{0,8},{8,0},{1,9},{9,1},{2,10},{10,2},{3,11},{11,3},{4,12},{12,4},... | collective-permute-start | bytes 49160 | tf_op jit(solution)/shard_map/ppermute | solution.py:228
  33.4 1.9 %collective-permute-start.4 = (bf16[16,16,256]{2,1,0:T(8,128)(2,1)S(1)}, bf16[16,16,256]{2,1,0:T(8,128)(2,1)S(1)}, u32[]{:S(2)}, u32[]{:S(2)}) collective-permute-start(bf16[16,16,256]{2,1,0:T(8,128)(2,1)S(1)} %all-to-all-done.1.gathered), channel_id=1, source_target_pairs={{0,8},{8,0},{1,9},{9,1},{2,10},{10,2},{3,11},{11,3},{4,12},{12,4},... | collective-permute-start | bytes 393224 | tf_op jit(solution)/shard_map/ppermute | solution.py:228

commit v4 on v3

v4 whole, which is shorter than its diff:
```python
import jax
import jax.numpy as jnp
from jax import lax
from jax.experimental import pallas as pl
from jax.experimental.pallas import tpu as pltpu
from jax.sharding import Mesh, PartitionSpec as P

F32 = jnp.float32
BF16 = jnp.bfloat16
OPS = ("chip", "core")
SWAP = [(0, 1), (1, 0)]
VMEM = pl.BlockSpec(memory_space=pltpu.VMEM)
SMEM = pl.BlockSpec(memory_space=pltpu.SMEM)
HBM = pl.BlockSpec(memory_space=pltpu.HBM)


def dot(a, b):
    return jnp.dot(a, b, preferred_element_type=F32)


def halves_of(left, s, flags, x):
    terms = x.shape[0] // left.shape[3]
    halves = []
    for k in range(left.shape[0]):
        block = left[k, s]
        half = dot(jnp.concatenate([block] * terms, axis=1), x)
        halves.append(half.astype(BF16) * flags(s, k))
    return halves


def in_rows(ref):
    return lambda s, k: ref[s, pl.ds(k, 1), :].astype(BF16)


def closed(halves, right, s):
    return dot(jnp.concatenate(halves, axis=1), right[:, s].reshape(-1, right.shape[3]))


def two_terms(x):
    high = x.astype(BF16)
    return jnp.concatenate([high, (x - high.astype(F32)).astype(BF16)], axis=0)


def other_kernel(
    pattern_hbm, left_hbm, right_hbm, guess_hbm, precond_hbm, columns_hbm,
    part, left, right, guess, precond, columns, flags,
    pattern, pattern_sem, columns_sem, guess_sem, left_sem, right_sem, precond_sem,
):
    mine = lax.axis_index("core")
    other = 1 - mine
    small = [
        pltpu.make_async_copy(pattern_hbm, pattern, pattern_sem),
        pltpu.make_async_copy(columns_hbm, columns, columns_sem),
    ]
    copies = []
    for i, s in enumerate((other, mine)):
        copies.append(
            [
                pltpu.make_async_copy(guess_hbm.at[s], guess.at[s], guess_sem.at[i]),
                pltpu.make_async_copy(left_hbm.at[:, s], left.at[:, s], left_sem.at[i]),
                pltpu.make_async_copy(right_hbm.at[:, s], right.at[:, s], right_sem.at[i]),
            ]
        )
    last = pltpu.make_async_copy(precond_hbm, precond, precond_sem)
    for copy in small + copies[0] + copies[1] + [last]:
        copy.start()
    for copy in small:
        copy.wait()
    for s in range(left.shape[1]):
        for k in range(left.shape[0]):
            flags[s, pl.ds(k, 1), :] = jnp.full((1, flags.shape[2]), pattern[s, k].astype(F32))
    copies[0][0].wait()
    copies[0][1].wait()
    halves = halves_of(left, other, in_rows(flags), two_terms(guess[other]))
    copies[0][2].wait()
    turned = columns[other].astype(F32)
    rest = part.shape[0] - right.shape[2] - turned.shape[0]
    rest = jnp.zeros((rest, turned.shape[1]), F32)
    part[...] = jnp.concatenate([closed(halves, right, other), turned, rest], axis=0).astype(BF16)
    for copy in copies[1] + [last]:
        copy.wait()


def own_kernel(flags, left, right, guess, precond, part, level, rows_out, state_rows):
    mine, chip = lax.axis_index("core"), lax.axis_index("chip")
    part[...] = closed(halves_of(left, mine, in_rows(flags), two_terms(guess[mine])), right, mine)
    level[...] = guess[...] / precond[...]
    count = rows_out.shape[1]
    own = pl.ds(pl.multiple_of(chip * count, count), count)
    for i, ref in enumerate((guess, level, precond)):
        rows_out[i] = ref[mine, own, :]
    count = state_rows.shape[2]
    own = pl.ds(pl.multiple_of((chip * 2 + mine) * count, count), count)
    for i, ref in enumerate((guess, level)):
        for s in range(ref.shape[0]):
            state_rows[i, s] = ref[s, own, :]


def chunks_kernel(own, theirs, columns, chunks):
    mine = lax.axis_index("core")
    chips, count, states = chunks.shape
    theirs = theirs[...].astype(F32)
    total = own[...] + theirs[:states]
    a, b = columns[mine].astype(F32), theirs[states : states + columns.shape[1]]
    first = mine == 0
    turned = jnp.concatenate([jnp.where(first, a, b), jnp.where(first, b, a)], axis=0)
    turned = jnp.broadcast_to(turned[None], (chips,) + turned.shape)
    chunks[...] = jnp.concatenate([total.reshape(chips, -1, states), turned], axis=1).astype(BF16)


def rows_kernel(received, rows_in, packed, sums, chunks):
    g, d, p = rows_in[0], rows_in[1], rows_in[2]
    count, states = g.shape
    h = jnp.sum(received[:, :count, :].astype(F32), axis=0)
    y = h / p
    high = y.astype(BF16).astype(F32)
    middle = (y - high).astype(BF16).astype(F32)
    packed[:states, :] = received[:, count:, :].reshape(states, states)
    packed[states:, :] = jnp.concatenate([high, middle, y - high - middle], axis=0).astype(BF16)
    chunks[...] = jnp.broadcast_to(y[None].astype(BF16), chunks.shape)
    pairs = ((g, g), (g, h), (g, d), (d, d), (g, y), (d, y), (y, y), (h, y))
    sums[...] = jnp.concatenate([jnp.sum(a * b, axis=0, keepdims=True) for a, b in pairs], axis=0)


def renorm_kernel(flags, left, right, level, mine, theirs, out, d_hd, state_y):
    first = lax.axis_index("core") == 0
    states = left.shape[2]
    a, b = mine[...].astype(F32), theirs[...].astype(F32)
    count = state_y.shape[1]
    y = []
    for x in (a, b):
        terms = [x[i : i + count] for i in range(states, x.shape[0], count)]
        terms = terms[0::2], terms[1::2]
        low, high = [c[0] + c[1] + c[2] for c in terms]
        y.append(jnp.where(first, low, high))
    a, b = a[:states], b[:states]
    dots = []
    for s in range(left.shape[1]):
        is_mine = first if s == 0 else jnp.logical_not(first)
        state_y[s] = jnp.where(is_mine, y[0], y[1])
        turned = jnp.where(is_mine, a, b)
        rotation = jnp.transpose(turned).astype(BF16)
        turned = turned.astype(BF16)
        for k in range(left.shape[0]):
            rotated = dot(left[k, s], rotation).astype(BF16)
            out[k, s] = dot(turned, rotated).astype(BF16)
        d = level[s]
        image = closed(halves_of(left, s, in_rows(flags), d.astype(BF16)), right, s)
        dots.append(jnp.sum(d * image, axis=0, keepdims=True))
    d_hd[...] = dots[0] + dots[1]


def dots_of(s, flags, y, left, right, level):
    image = closed(halves_of(left, s, in_rows(flags), y), right, s)
    y_hy = jnp.sum(y.astype(F32) * image, axis=0, keepdims=True)
    d_hy = jnp.sum(level[s] * image, axis=0, keepdims=True)
    return jnp.concatenate([y_hy, d_hy], axis=0)


def own_dots_kernel(flags, gathered, left, right, level, d_hd, out):
    y = gathered[...].reshape(left.shape[2:])
    out[...] = jnp.concatenate([dots_of(lax.axis_index("core"), flags, y, left, right, level), d_hd[...]], axis=0)


def other_dots_kernel(flags, gathered, left, right, level, own_dots, row_sums, out):
    y = gathered[...].reshape(left.shape[2:])
    dots = dots_of(1 - lax.axis_index("core"), flags, y, left, right, level)
    sums = jnp.concatenate([row_sums[...], own_dots[...], dots, jnp.zeros((3, y.shape[1]), F32)], axis=0)
    sums = jnp.sum(sums, axis=1, keepdims=True)
    extent = (sums.shape[0], out.shape[2])
    here = lax.broadcasted_iota(jnp.int32, extent, 0) == lax.broadcasted_iota(jnp.int32, extent, 1)
    line = jnp.sum(jnp.where(here, sums, 0.0), axis=0, keepdims=True)
    out[...] = jnp.broadcast_to(line[None], out.shape)


def gather_kernel(received, out):
    out[...] = jnp.broadcast_to(jnp.sum(received[...], axis=0)[None], out.shape)


def state_kernel(entries, received, state_rows, state_y, state, energy_out):
    sums = jnp.sum(received[...], axis=0)
    lanes = [sums[:, i : i + 1] for i in range(13)]
    gg, gh, gd, dd, gy, dy, yy, hy = lanes[:8]
    y_hy, d_hy, d_hd = lanes[8] + lanes[11], lanes[9] + lanes[12], lanes[10]
    inverse = 1.0 / entries
    first_square = 1.0 / (gg * inverse + 1e-06)
    rho = first_square * gh * inverse
    kappa = first_square * (gy - rho * gd) * inverse
    qq = yy - 2.0 * rho * dy + rho * rho * dd - 2.0 * kappa * (gy - rho * gd) + kappa * kappa * gg
    hq = hy - rho * gy - kappa * gh
    q_hq = y_hy - 2.0 * rho * d_hy + rho * rho * d_hd - 2.0 * kappa * (hy - rho * gy) + kappa * kappa * gh
    second_square = 1.0 / (first_square * qq * inverse + 1e-06)
    second_scale = jnp.sqrt(second_square)
    first_scale = jnp.sqrt(first_square)
    coupling = second_scale * first_square * hq * inverse
    rho_second = second_square * first_square * q_hq * inverse
    half_gap = (rho - rho_second) * 0.5
    energy = (rho + rho_second) * 0.5 - jnp.sqrt(half_gap * half_gap + coupling * coupling)
    weight_first = rho_second - energy
    weight_second = -coupling
    scaling = 1.0 / jnp.sqrt(weight_first * weight_first + weight_second * weight_second)
    on_second = weight_second * second_scale * scaling * first_scale
    on_first = weight_first * scaling * first_scale
    energy_out[...] = jnp.broadcast_to(energy, energy_out.shape)
    g, d, y = state_rows[0], state_rows[1], state_y[...]
    state[...] = on_first[None] * g + on_second[None] * (y - rho[None] * d - kappa[None] * g)


def call(kernel, out_shape, in_specs, flops=0, scratch=(), limit=16):
    return pl.pallas_call(
        kernel,
        out_shape=out_shape,
        in_specs=in_specs,
        out_specs=jax.tree.map(lambda _: VMEM, out_shape),
        scratch_shapes=scratch,
        cost_estimate=pl.CostEstimate(flops=flops, bytes_accessed=1 << 20, transcendentals=0),
        compiler_params=pltpu.CompilerParams(vmem_limit_bytes=limit << 20),
    )


def local(left_hbm, right_hbm, pattern, guess_hbm, precond_hbm, rotation):
    ops, sectors, states = left_hbm.shape[:3]
    chips, cores, zones = (lax.axis_size(axis) for axis in ("chip", "core", "sec"))
    count = states // chips
    entries = float(sectors * zones * states * states)
    shape = jax.ShapeDtypeStruct
    dma = pltpu.SemaphoreType.DMA
    block = (states, states)
    flops = 4 * ops * sectors * states**3
    pattern = jnp.swapaxes(pattern, 0, 1)
    columns = jnp.swapaxes(rotation, 1, 2)

    def in_hbm(x):
        return pltpu.with_memory_space_constraint(x, pltpu.HBM)

    def swapped(x):
        return lax.ppermute(x, "core", SWAP)

    part, left, right, guess, precond, columns, flags = call(
        other_kernel,
        (
            shape((states + 16, states), BF16),
            shape(left_hbm.shape, BF16),
            shape(right_hbm.shape, BF16),
            shape(guess_hbm.shape, F32),
            shape(guess_hbm.shape, F32),
            shape(columns.shape, BF16),
            shape((sectors, ops, states), F32),
        ),
        [HBM] * 6,
        flops // 2,
        [pltpu.SMEM(pattern.shape, jnp.int32), dma, dma, dma((2,)), dma((2,)), dma((2,)), dma],
    )(*(in_hbm(x) for x in (pattern, left_hbm, right_hbm, guess_hbm, precond_hbm, columns)))
    theirs = swapped(part)
    own, level, own_rows, state_rows = call(
        own_kernel,
        (
            shape(block, F32),
            shape(guess.shape, F32),
            shape((3, count, states), F32),
            shape((2, sectors, count // cores, states), F32),
        ),
        [VMEM] * 5,
        flops // 2,
    )(flags, left, right, guess, precond)
    chunks = call(chunks_kernel, shape((chips, 2 * count, states), BF16), [VMEM] * 3)(own, theirs, columns)
    received = lax.all_to_all(chunks, "chip", 0, 0)
    packed, row_sums, chunks = call(
        rows_kernel,
        (shape((states + 3 * count, states), BF16), shape((8, states), F32), shape((chips, count, states), BF16)),
        [VMEM] * 2,
    )(received, own_rows)
    gathered = lax.all_to_all(chunks, "chip", 0, 0)
    renormalized, d_hd, state_y = call(
        renorm_kernel,
        (shape(left.shape, BF16), shape((1, states), F32), shape((sectors, count // cores, states), F32)),
        [VMEM] * 6,
        2 * flops,
    )(flags, left, right, level, packed, swapped(packed))
    gathered, d_hd = lax.optimization_barrier((gathered, d_hd))
    gathered_theirs = swapped(gathered)
    dots = call(own_dots_kernel, shape((3, states), F32), [VMEM] * 6, flops // 2)(
        flags, gathered, left, right, level, d_hd
    )
    sums = call(other_dots_kernel, shape((chips, 1, 128), F32), [VMEM] * 7, flops // 2)(
        flags, gathered_theirs, left, right, level, dots, row_sums
    )
    sums = lax.all_to_all(sums, "chip", 0, 0)
    sums = call(gather_kernel, shape((cores * zones, 1, 128), F32), [VMEM])(sums)
    sums = lax.all_to_all(sums, ("core", "sec"), 0, 0)
    new_state, energy = call(
        lambda *refs: state_kernel(entries, *refs),
        (shape((sectors, count // cores, states), F32), shape((1, 128), F32)),
        [VMEM] * 3,
    )(sums, state_rows, state_y)
    return new_state, energy[0, :1], renormalized


def solution(mesh):
    cores = 2
    mesh = Mesh(mesh.devices.reshape(-1, cores, mesh.shape["sec"]), ("chip", "core", "sec"))
    return jax.shard_map(
        local,
        mesh=mesh,
        in_specs=(
            P(OPS, "sec", None, None),
            P(OPS, "sec", None, None),
            P(OPS, "sec"),
            P("sec", None, None),
            P("sec", None, None),
            P("sec", None, OPS),
        ),
        out_specs=(P("sec", OPS, None), P(), P(OPS, "sec", None, None)),
        check_vma=False,
    )
```

time: 63.7 us -> 63.5 us (level)
    all_to_all x1, waiting for transfers between devices: 3.33 us -> 4.58 us  [local(): gathered = lax.all_to_all(chunks, 'chip', 0, 0)]
    ppermute x5 -> x3, waiting for transfers between devices: 1.61 us -> 0.7 us  [swapped(): return lax.ppermute(x, 'core', SWAP)]
    ppermute x5 -> x3, starting transfers between devices: 6 us -> 5.75 us  [swapped(): return lax.ppermute(x, 'core', SWAP)]
  transfers between devices with their start and end apart: 6 -> 4, of which waited for: 3 -> 3; matrix products, arithmetic and copies ran while one was open for 0% -> 0% of each run, Pallas kernels for 7% -> 6%
where the time goes in v4:
time: 63.5 us; the launch traced here: 63.2 us
  blocking collectives  39.2 us (62%)
  starting transfers between devices  9.26 us (15%)
  Pallas kernels  8.77 us (14%)
  waiting for transfers between devices  5.28 us (8%)
  between operations  0.68 us (1%)
    all_to_all x1, blocking collectives, local(): sums = lax.all_to_all(sums, ('core', 'sec'), 0, 0)  17 us
    all_to_all x1, blocking collectives, local(): received = lax.all_to_all(chunks, 'chip', 0, 0)  12.9 us
    all_to_all x1, blocking collectives, local(): sums = lax.all_to_all(sums, 'chip', 0, 0)  9.2 us
    ppermute x3, starting transfers between devices, swapped(): return lax.ppermute(x, 'core', SWAP)  5.75 us
    all_to_all x1, waiting for transfers between devices, local(): gathered = lax.all_to_all(chunks, 'chip', 0, 0)  4.58 us
    all_to_all x1, starting transfers between devices, local(): gathered = lax.all_to_all(chunks, 'chip', 0, 0)  3.51 us
    pallas_call x1, Pallas kernels, local(): call(renorm_kernel, (shape(left.shape, BF16), shape((1, states), F32), sh...  2.69 us
    pallas_call x1, Pallas kernels, local(): call(other_kernel, (shape((states + 16, states), BF16), shape(left_hbm.sh...  2.37 us
  transfers between devices with their start and end apart: 4, of which 3 were waited for; matrix products, arithmetic and copies ran while one was open for 0% of the time, Pallas kernels for 6%

profile of v4, /device:TPU:1, one launch (start us, length us, event | category | flops | bytes accessed | tf_op | source)
XLA Modules:
  0.0 63.2 jit_solution(11209751682533580007)
XLA Ops:
  0.6 2.4 %shard_map.85 = (bf16[272,256]{1,0:T(8,128)(2,1)S(1)}, bf16[4,2,256,256]{3,2,1,0:T(8,128)(2,1)S(1)}, bf16[4,2,256,256]{3,2,1,0:T(8,128)(2,1)S(1)}, f32[2,256,256...) custom-call(s32[2,4]{1,0:T(2,128)} %bitcast.5, ...), custom_call_target="tpu_custom_call" | custom-call | flops 268435456 | bytes 1048576 | tf_op jit(solution)/shard_map/pallas_call | solution.py:239
  3.0 3.3 %collective-permute-start = (bf16[272,256]{1,0:T(8,128)(2,1)S(1)}, bf16[272,256]{1,0:T(8,128)(2,1)S(1)}, u32[]{:S(2)}, u32[]{:S(2)}) collective-permute-start(bf16[272,256]{1,0:T(8,128)(2,1)S(1)} %get-tuple-element.30), channel_id=1, source_target_pairs={{0,8},{8,0},{1,9},{9,1},{2,10},{10,2},{3,11},{11,3},{4,12},{12,4},... | collective-permute-start | bytes 417800 | tf_op jit(solution)/shard_map/ppermute | solution.py:237
  6.3 0.7 %shard_map.86 = (f32[256,256]{1,0:T(8,128)S(1)}, f32[2,256,256]{2,1,0:T(8,128)S(1)}, f32[3,16,256]{2,1,0:T(8,128)S(1)}, f32[2,2,8,256]{3,2,1,0:T(8,128)S(1)}) custom-call(f32[2,4,256]{2,1,0:T(4,128)S(1)} %get-tuple-element.24.flags, bf16[4,2,256,256]{3,2,1,0:T(8,128)(2,1)S(1)} %get-tuple-element.25.left, ...), custom_call_target="tpu_custom_call" | custom-call | flops 268435456 | bytes 1048576 | tf_op jit(solution)/shard_map/pallas_call | solution.py:255
  7.1 0.3 collective-permute-done.theirs
  7.4 12.9 %all_to_all.20.received = bf16[16,32,256]{2,1,0:T(8,128)(2,1)S(1)} all-to-all(bf16[16,32,256]{2,1,0:T(8,128)(2,1)S(1)} %shard_map.87), channel_id=1, replica_groups=mesh['chip'=16,'core'=2,'sec'=8] {'chip'}, dimensions={0} | all-to-all | bytes 524288 | tf_op jit(solution)/shard_map/all_to_all | solution.py:267
  20.3 0.7 %shard_map.88 = (bf16[304,256]{1,0:T(8,128)(2,1)S(1)}, f32[8,256]{1,0:T(8,128)S(1)}, bf16[16,16,256]{2,1,0:T(8,128)(2,1)}) custom-call(bf16[16,32,256]{2,1,0:T(8,128)(2,1)S(1)} %all_to_all.20.received, f32[3,16,256]{2,1,0:T(8,128)S(1)} %get-tuple-element.32.rows_in), custom_call_target="tpu_custom_call" | custom-call | bytes 1048576 | tf_op jit(solution)/shard_map/pallas_call | solution.py:268
  21.0 1.5 %collective-permute-start.1 = (bf16[304,256]{1,0:T(8,128)(2,1)S(1)}, bf16[304,256]{1,0:T(8,128)(2,1)S(1)}, u32[]{:S(2)}, u32[]{:S(2)}) collective-permute-start(bf16[304,256]{1,0:T(8,128)(2,1)S(1)} %get-tuple-element.35.mine), channel_id=1, source_target_pairs={{0,8},{8,0},{1,9},{9,1},{2,10},{10,2},{3,11},{11,3},{4,12},{12,4},... | collective-permute-start | bytes 466952 | tf_op jit(solution)/shard_map/ppermute | solution.py:237
  22.5 3.5 %all-to-all-start.1 = ((bf16[16,16,256]{2,1,0:T(8,128)(2,1)}), bf16[16,16,256]{2,1,0:T(8,128)(2,1)S(1)}, u32[]{:S(2)}, u32[]{:S(2)}) async-start(bf16[16,16,256]{2,1,0:T(8,128)(2,1)} %get-tuple-element.33), calls=%async_computation.1 | async-start | bytes 262144 | tf_op jit(solution)/shard_map/all_to_all | solution.py:273
  26.0 0.0 collective-permute-done.1.theirs
  26.0 2.7 %shard_map.89 = (bf16[4,2,256,256]{3,2,1,0:T(8,128)(2,1)}, f32[1,256]{1,0:T(1,128)S(1)}, f32[2,8,256]{2,1,0:T(8,128)S(1)}) custom-call(f32[2,4,256]{2,1,0:T(4,128)S(1)} %get-tuple-element.24.flags, bf16[4,2,256,256]{3,2,1,0:T(8,128)(2,1)S(1)} %get-tuple-element.25.left, bf16[4,2,256,256]{3,2,1,0:T(8,128)(2,1)S(1)} %get-tuple-element.26.right, ...), custom_call_target="tpu_custom_call" | custom-call | flops 1073741824 | bytes 1048576 | tf_op jit(solution)/shard_map/pallas_call | solution.py:274
  28.7 4.6 %all-to-all-done.1.gathered = bf16[16,16,256]{2,1,0:T(8,128)(2,1)S(1)} async-done(((bf16[16,16,256]{2,1,0:T(8,128)(2,1)}), bf16[16,16,256]{2,1,0:T(8,128)(2,1)S(1)}, u32[]{:S(2)}, u32[]{:S(2)}) %all-to-all-start.1) | async-done | bytes 131104 | tf_op jit(solution)/shard_map/all_to_all | solution.py:273
  33.3 0.9 %collective-permute-start.2 = (bf16[16,16,256]{2,1,0:T(8,128)(2,1)S(1)}, bf16[16,16,256]{2,1,0:T(8,128)(2,1)S(1)}, u32[]{:S(2)}, u32[]{:S(2)}) collective-permute-start(bf16[16,16,256]{2,1,0:T(8,128)(2,1)S(1)} %all-to-all-done.1.gathered), channel_id=1, source_target_pairs={{0,8},{8,0},{1,9},{9,1},{2,10},{10,2},{3,11},{11,3},{4,12},{12,4},... | collective-permute-start | bytes 393224 | tf_op jit(solution)/shard_map/ppermute | solution.py:237
  34.2 0.6 shard_map.90.own_dots
  34.8 0.4 collective-permute-done.2.gathered
  35.2 0.6 %shard_map.91 = f32[16,1,128]{2,1,0:T(1,128)S(1)} custom-call(f32[2,4,256]{2,1,0:T(4,128)S(1)} %get-tuple-element.24.flags, bf16[16,16,256]{2,1,0:T(8,128)(2,1)S(1)} %collective-permute-done.2.gathered, bf16[4,2,256,256]{3,2,1,0:T(8,128)(2,1)S(1)} %get-tuple-element.25.left, bf16[4,2,256,256]{3,2,1,0:T(8,128)(2,1)S(1)} %get-tuple-element.26.right, ...), custom_call_target="tpu_custom_call" | custom-call | flops 268435456 | bytes 1048576 | tf_op jit(solution)/shard_map/pallas_call | solution.py:285
  35.8 9.2 %all_to_all.21.received = f32[16,1,128]{2,1,0:T(1,128)S(1)} all-to-all(f32[16,1,128]{2,1,0:T(1,128)S(1)} %shard_map.91), channel_id=1, replica_groups=mesh['chip'=16,'core'=2,'sec'=8] {'chip'}, dimensions={0} | all-to-all | bytes 16384 | tf_op jit(solution)/shard_map/all_to_all | solution.py:288
  45.1 17.0 %all_to_all.22.refs_0_ = f32[16,1,128]{2,1,0:T(1,128)S(1)} all-to-all(f32[16,1,128]{2,1,0:T(1,128)S(1)} %shard_map.92), channel_id=1, replica_groups=mesh['chip'=16,'core'=2,'sec'=8] {'core','sec'}, dimensions={0} | all-to-all | bytes 16384 | tf_op jit(solution)/shard_map/all_to_all | solution.py:290
  62.1 1.1 %shard_map.93 = (f32[2,8,256]{2,1,0:T(8,128)}, f32[1,128]{1,0:T(1,128)}) custom-call(f32[16,1,128]{2,1,0:T(1,128)S(1)} %all_to_all.22.refs_0_, f32[2,2,8,256]{3,2,1,0:T(8,128)S(1)} %get-tuple-element.40.refs_1_, f32[2,8,256]{2,1,0:T(8,128)S(1)} %get-tuple-element.41.refs_2_), custom_call_target="tpu_custom_call" | custom-call | bytes 1048576 | tf_op jit(solution)/shard_map/pallas_call | solution.py:291
  (2 shorter events, 0.1 us)
Async XLA Ops:
  3.0 4.3 %collective-permute-start = (bf16[272,256]{1,0:T(8,128)(2,1)S(1)}, bf16[272,256]{1,0:T(8,128)(2,1)S(1)}, u32[]{:S(2)}, u32[]{:S(2)}) collective-permute-start(bf16[272,256]{1,0:T(8,128)(2,1)S(1)} %get-tuple-element.30), channel_id=1, source_target_pairs={{0,8},{8,0},{1,9},{9,1},{2,10},{10,2},{3,11},{11,3},{4,12},{12,4},... | collective-permute-start | bytes 417800 | tf_op jit(solution)/shard_map/ppermute | solution.py:237
  21.0 5.0 %collective-permute-start.1 = (bf16[304,256]{1,0:T(8,128)(2,1)S(1)}, bf16[304,256]{1,0:T(8,128)(2,1)S(1)}, u32[]{:S(2)}, u32[]{:S(2)}) collective-permute-start(bf16[304,256]{1,0:T(8,128)(2,1)S(1)} %get-tuple-element.35.mine), channel_id=1, source_target_pairs={{0,8},{8,0},{1,9},{9,1},{2,10},{10,2},{3,11},{11,3},{4,12},{12,4},... | collective-permute-start | bytes 466952 | tf_op jit(solution)/shard_map/ppermute | solution.py:237
  22.5 10.8 %all-to-all-start.1 = ((bf16[16,16,256]{2,1,0:T(8,128)(2,1)}), bf16[16,16,256]{2,1,0:T(8,128)(2,1)S(1)}, u32[]{:S(2)}, u32[]{:S(2)}) async-start(bf16[16,16,256]{2,1,0:T(8,128)(2,1)} %get-tuple-element.33), calls=%async_computation.1 | async-start | bytes 262144 | tf_op jit(solution)/shard_map/all_to_all | solution.py:273
  33.3 1.9 %collective-permute-start.2 = (bf16[16,16,256]{2,1,0:T(8,128)(2,1)S(1)}, bf16[16,16,256]{2,1,0:T(8,128)(2,1)S(1)}, u32[]{:S(2)}, u32[]{:S(2)}) collective-permute-start(bf16[16,16,256]{2,1,0:T(8,128)(2,1)S(1)} %all-to-all-done.1.gathered), channel_id=1, source_target_pairs={{0,8},{8,0},{1,9},{9,1},{2,10},{10,2},{3,11},{11,3},{4,12},{12,4},... | collective-permute-start | bytes 393224 | tf_op jit(solution)/shard_map/ppermute | solution.py:237

commit v5 on v4

v5 whole, which is shorter than its diff:
```python
import jax
import jax.numpy as jnp
from jax import lax
from jax.experimental import pallas as pl
from jax.experimental.pallas import tpu as pltpu
from jax.sharding import Mesh, PartitionSpec as P

F32 = jnp.float32
BF16 = jnp.bfloat16
OPS = ("chip", "core")
SWAP = [(0, 1), (1, 0)]
VMEM = pl.BlockSpec(memory_space=pltpu.VMEM)
SMEM = pl.BlockSpec(memory_space=pltpu.SMEM)
HBM = pl.BlockSpec(memory_space=pltpu.HBM)


def dot(a, b):
    return jnp.dot(a, b, preferred_element_type=F32)


def image_of(x, left, right, flags):
    count, states = left.shape[:2]
    terms = x.shape[0] // states
    halves = []
    for k in range(count):
        block = left[k]
        half = dot(jnp.concatenate([block] * terms, axis=1), x).astype(BF16)
        halves.append(half * flags[k : k + 1, :].astype(BF16))
    return dot(jnp.concatenate(halves, axis=1), right[...].reshape(count * states, states))


def chip_image(x, flags, left, right, left_swapped, right_swapped):
    count = left.shape[0]
    own = image_of(x, left, right, flags.at[pl.ds(0, count)])
    return own + image_of(x, left_swapped, right_swapped, flags.at[pl.ds(count, count)])


def two_terms(x):
    high = x.astype(BF16)
    return jnp.concatenate([high, (x - high.astype(F32)).astype(BF16)], axis=0)


def other_kernel(
    pattern_hbm, left_hbm, right_hbm, guess_hbm, precond_hbm, columns_hbm,
    part, left, left_other, right, right_other, guess, precond, rows_other, columns, flags,
    pattern, pattern_sem, columns_sem, rows_sem, guess_sem, left_sem, right_sem, precond_sem,
):
    mine, chip = lax.axis_index("core"), lax.axis_index("chip")
    other = 1 - mine
    count = rows_other.shape[0]
    own = pl.ds(pl.multiple_of((chip * 2 + mine) * count, count), count)
    small = [
        pltpu.make_async_copy(pattern_hbm, pattern, pattern_sem),
        pltpu.make_async_copy(columns_hbm, columns, columns_sem),
    ]
    copies = []
    for i, (s, l, r) in enumerate(((other, left_other, right_other), (mine, left, right))):
        copies.append(
            [
                pltpu.make_async_copy(guess_hbm.at[s], guess.at[s], guess_sem.at[i]),
                pltpu.make_async_copy(left_hbm.at[:, s], l, left_sem.at[i]),
                pltpu.make_async_copy(right_hbm.at[:, s], r, right_sem.at[i]),
            ]
        )
    last = [
        pltpu.make_async_copy(precond_hbm.at[mine], precond, precond_sem),
        pltpu.make_async_copy(precond_hbm.at[other, own], rows_other, rows_sem),
    ]
    for copy in small + copies[0] + copies[1] + last:
        copy.start()
    for copy in small:
        copy.wait()
    for s in range(flags.shape[0]):
        for k in range(flags.shape[1]):
            flags[s, pl.ds(k, 1), :] = jnp.full((1, flags.shape[2]), pattern[s, k].astype(F32))
    turned = columns[other].astype(F32)
    ones = flags[other]
    rest = jnp.zeros((part.shape[0] - guess.shape[1] - turned.shape[0] - ones.shape[0], turned.shape[1]), F32)
    for copy in copies[0]:
        copy.wait()
    image = image_of(two_terms(guess[other]), left_other, right_other, flags.at[other])
    part[...] = jnp.concatenate([image, turned, ones, rest], axis=0).astype(BF16)
    for copy in copies[1] + last:
        copy.wait()


def own_kernel(flags, left, right, guess, precond, rows_other, part, level, rows_out, state_rows):
    mine, chip = lax.axis_index("core"), lax.axis_index("chip")
    other = 1 - mine
    part[...] = image_of(two_terms(guess[mine]), left, right, flags.at[mine])
    level[...] = guess[mine] / precond[...]
    count = rows_out.shape[1]
    own = pl.ds(pl.multiple_of(chip * count, count), count)
    rows_out[0] = guess[mine, own, :]
    rows_out[1] = level[own, :]
    rows_out[2] = precond[own, :]
    count = state_rows.shape[2]
    own = pl.ds(pl.multiple_of((chip * 2 + mine) * count, count), count)
    state_rows[0, mine] = guess[mine, own, :]
    state_rows[1, mine] = level[own, :]
    state_rows[0, other] = guess[other, own, :]
    state_rows[1, other] = guess[other, own, :] / rows_other[...]


def chunks_kernel(own, theirs, columns, flags, chunks, all_flags):
    mine = lax.axis_index("core")
    chips, count, states = chunks.shape
    theirs = theirs[...].astype(F32)
    total = own[...] + theirs[:states]
    a, b = columns[mine].astype(F32), theirs[states : states + columns.shape[1]]
    first = mine == 0
    turned = jnp.concatenate([jnp.where(first, a, b), jnp.where(first, b, a)], axis=0)
    turned = jnp.broadcast_to(turned[None], (chips,) + turned.shape)
    ones = theirs[states + columns.shape[1] :][: flags.shape[1]]
    all_flags[...] = jnp.concatenate([flags[mine], ones], axis=0)
    chunks[...] = jnp.concatenate([total.reshape(chips, -1, states), turned], axis=1).astype(BF16)


def rows_kernel(received, rows_in, packed, sums, chunks):
    g, d, p = rows_in[0], rows_in[1], rows_in[2]
    count, states = g.shape
    h = jnp.sum(received[:, :count, :].astype(F32), axis=0)
    y = h / p
    high = y.astype(BF16).astype(F32)
    middle = (y - high).astype(BF16).astype(F32)
    packed[:states, :] = received[:, count:, :].reshape(states, states)
    packed[states:, :] = jnp.concatenate([high, middle, y - high - middle], axis=0).astype(BF16)
    chunks[...] = jnp.broadcast_to(y[None].astype(BF16), chunks.shape)
    pairs = ((g, g), (g, h), (g, d), (d, d), (g, y), (d, y), (y, y), (h, y))
    sums[...] = jnp.concatenate([jnp.sum(a * b, axis=0, keepdims=True) for a, b in pairs], axis=0)


def renorm_kernel(flags, left, left_other, right, left_swapped, right_swapped, level, packed, packed_theirs, out, d_hd, state_y):
    mine = lax.axis_index("core")
    first = mine == 0
    states = left.shape[2]
    a, b = packed[...].astype(F32), packed_theirs[...].astype(F32)
    count = state_y.shape[1]
    y = []
    for x in (a, b):
        terms = [x[i : i + count] for i in range(states, x.shape[0], count)]
        terms = terms[0::2], terms[1::2]
        low, high = [c[0] + c[1] + c[2] for c in terms]
        y.append(jnp.where(first, low, high))
    state_y[mine] = y[0]
    state_y[1 - mine] = y[1]
    for s, turned, blocks in ((mine, a[:states], left), (1 - mine, b[:states], left_other)):
        rotation = jnp.transpose(turned).astype(BF16)
        turned = turned.astype(BF16)
        for k in range(blocks.shape[0]):
            rotated = dot(blocks[k], rotation).astype(BF16)
            out[k, s] = dot(turned, rotated).astype(BF16)
    low = level[...].astype(BF16)
    image = chip_image(low, flags, left, right, left_swapped, right_swapped)
    d_hd[...] = jnp.sum(level[...] * image, axis=0, keepdims=True)


def dots_kernel(flags, gathered, left, right, left_swapped, right_swapped, level, row_sums, d_hd, out):
    y = gathered[...].reshape(level.shape)
    image = chip_image(y, flags, left, right, left_swapped, right_swapped)
    y_hy = jnp.sum(y.astype(F32) * image, axis=0, keepdims=True)
    d_hy = jnp.sum(level[...] * image, axis=0, keepdims=True)
    rest = jnp.zeros((5, y.shape[1]), F32)
    sums = jnp.concatenate([row_sums[...], y_hy, d_hy, d_hd[...], rest], axis=0)
    sums = jnp.sum(sums, axis=1, keepdims=True)
    extent = (sums.shape[0], out.shape[2])
    here = lax.broadcasted_iota(jnp.int32, extent, 0) == lax.broadcasted_iota(jnp.int32, extent, 1)
    line = jnp.sum(jnp.where(here, sums, 0.0), axis=0, keepdims=True)
    out[...] = jnp.broadcast_to(line[None], out.shape)


def gather_kernel(received, out):
    out[...] = jnp.broadcast_to(jnp.sum(received[...], axis=0)[None], out.shape)


def state_kernel(entries, received, state_rows, state_y, state, energy_out):
    sums = jnp.sum(received[...], axis=0)
    extent = (16, sums.shape[1])
    here = lax.broadcasted_iota(jnp.int32, extent, 0) == lax.broadcasted_iota(jnp.int32, extent, 1)
    sums = jnp.sum(jnp.where(here, jnp.broadcast_to(sums, extent), 0.0), axis=1, keepdims=True)
    sums = jnp.broadcast_to(sums, (extent[0], state.shape[2]))
    gg, gh, gd, dd, gy, dy, yy, hy, y_hy, d_hy, d_hd = [sums[i : i + 1] for i in range(11)]
    inverse = 1.0 / entries
    first_square = 1.0 / (gg * inverse + 1e-06)
    rho = first_square * gh * inverse
    kappa = first_square * (gy - rho * gd) * inverse
    qq = yy - 2.0 * rho * dy + rho * rho * dd - 2.0 * kappa * (gy - rho * gd) + kappa * kappa * gg
    hq = hy - rho * gy - kappa * gh
    q_hq = y_hy - 2.0 * rho * d_hy + rho * rho * d_hd - 2.0 * kappa * (hy - rho * gy) + kappa * kappa * gh
    second_square = 1.0 / (first_square * qq * inverse + 1e-06)
    second_scale = jnp.sqrt(second_square)
    first_scale = jnp.sqrt(first_square)
    coupling = second_scale * first_square * hq * inverse
    rho_second = second_square * first_square * q_hq * inverse
    half_gap = (rho - rho_second) * 0.5
    energy = (rho + rho_second) * 0.5 - jnp.sqrt(half_gap * half_gap + coupling * coupling)
    weight_first = rho_second - energy
    weight_second = -coupling
    scaling = 1.0 / jnp.sqrt(weight_first * weight_first + weight_second * weight_second)
    on_second = weight_second * second_scale * scaling * first_scale
    on_first = weight_first * scaling * first_scale
    energy_out[...] = energy[:, : energy_out.shape[1]]
    g, d, y = state_rows[0], state_rows[1], state_y[...]
    state[...] = on_first[None] * g + on_second[None] * (y - rho[None] * d - kappa[None] * g)


def call(kernel, out_shape, in_specs, flops=0, scratch=(), limit=16):
    return pl.pallas_call(
        kernel,
        out_shape=out_shape,
        in_specs=in_specs,
        out_specs=jax.tree.map(lambda _: VMEM, out_shape),
        scratch_shapes=scratch,
        cost_estimate=pl.CostEstimate(flops=flops, bytes_accessed=1 << 20, transcendentals=0),
        compiler_params=pltpu.CompilerParams(vmem_limit_bytes=limit << 20),
    )


def local(left_hbm, right_hbm, pattern, guess_hbm, precond_hbm, rotation):
    ops, sectors, states = left_hbm.shape[:3]
    chips, cores, zones = (lax.axis_size(axis) for axis in ("chip", "core", "sec"))
    count = states // chips
    entries = float(sectors * zones * states * states)
    shape = jax.ShapeDtypeStruct
    dma = pltpu.SemaphoreType.DMA
    block = (states, states)
    flops = 4 * ops * sectors * states**3
    pattern = jnp.swapaxes(pattern, 0, 1)
    columns = jnp.swapaxes(rotation, 1, 2)

    def in_hbm(x):
        return pltpu.with_memory_space_constraint(x, pltpu.HBM)

    def swap(x):
        return lax.ppermute(x, "core", SWAP)

    operators = shape((ops,) + block, BF16)
    part, left, left_other, right, right_other, guess, precond, rows_other, columns, flags = call(
        other_kernel,
        (
            shape((states + 16, states), BF16),
            operators,
            operators,
            operators,
            operators,
            shape(guess_hbm.shape, F32),
            shape(block, F32),
            shape((count // cores, states), F32),
            shape(columns.shape, BF16),
            shape((sectors, ops, states), F32),
        ),
        [HBM] * 6,
        flops // 2,
        [pltpu.SMEM(pattern.shape, jnp.int32), dma, dma, dma, dma((2,)), dma((2,)), dma((2,)), dma],
    )(*(in_hbm(x) for x in (pattern, left_hbm, right_hbm, guess_hbm, precond_hbm, columns)))
    theirs = swap(part)
    own, level, own_rows, state_rows = call(
        own_kernel,
        (
            shape(block, F32),
            shape(block, F32),
            shape((3, count, states), F32),
            shape((2, sectors, count // cores, states), F32),
        ),
        [VMEM] * 6,
        flops // 2,
    )(flags, left, right, guess, precond, rows_other)
    chunks, flags = call(
        chunks_kernel,
        (shape((chips, 2 * count, states), BF16), shape((2 * ops, states), F32)),
        [VMEM] * 4,
    )(own, theirs, columns, flags)
    chunks, left_other, right_other = lax.optimization_barrier((chunks, left_other, right_other))
    left_swapped, right_swapped = swap(left_other), swap(right_other)
    received = lax.all_to_all(chunks, "chip", 0, 0)
    received, left_swapped, right_swapped = lax.optimization_barrier((received, left_swapped, right_swapped))
    packed, row_sums, chunks = call(
        rows_kernel,
        (shape((states + 3 * count, states), BF16), shape((8, states), F32), shape((chips, count, states), BF16)),
        [VMEM] * 2,
    )(received, own_rows)
    gathered = lax.all_to_all(chunks, "chip", 0, 0)
    renormalized, d_hd, state_y = call(
        renorm_kernel,
        (shape(left_hbm.shape, BF16), shape((1, states), F32), shape((sectors, count // cores, states), F32)),
        [VMEM] * 9,
        2 * flops,
    )(flags, left, left_other, right, left_swapped, right_swapped, level, packed, swap(packed))
    gathered, d_hd = lax.optimization_barrier((gathered, d_hd))
    sums = call(dots_kernel, shape((chips, 1, 128), F32), [VMEM] * 9, flops)(
        flags, gathered, left, right, left_swapped, right_swapped, level, row_sums, d_hd
    )
    sums = lax.all_to_all(sums, "chip", 0, 0)
    sums = call(gather_kernel, shape((cores * zones, 1, 128), F32), [VMEM])(sums)
    sums = lax.all_to_all(sums, ("core", "sec"), 0, 0)
    new_state, energy = call(
        lambda *refs: state_kernel(entries, *refs),
        (shape((sectors, count // cores, states), F32), shape((1, 128), F32)),
        [VMEM] * 3,
    )(sums, state_rows, state_y)
    return new_state, energy[0, :1], renormalized


def solution(mesh):
    cores = 2
    mesh = Mesh(mesh.devices.reshape(-1, cores, mesh.shape["sec"]), ("chip", "core", "sec"))
    return jax.shard_map(
        local,
        mesh=mesh,
        in_specs=(
            P(OPS, "sec", None, None),
            P(OPS, "sec", None, None),
            P(OPS, "sec"),
            P("sec", None, None),
            P("sec", None, None),
            P("sec", None, OPS),
        ),
        out_specs=(P("sec", OPS, None), P(), P(OPS, "sec", None, None)),
        check_vma=False,
    )
```

time: 63.5 us -> 62.7 us (0.987)
  waiting for transfers between devices: 5.28 us -> 4.44 us
    ppermute x3 -> x4, starting transfers between devices: 5.75 us -> 5.44 us  [swap(): return lax.ppermute(x, 'core', SWAP)]
    pallas_call x6 -> x5, Pallas kernels: 7 us -> 7.16 us  [the longest x1 3.1 us: local(): call(renorm_kernel, (shape(left_hbm.shape, BF16), shape((1, states), F32)...]
  transfers between devices with their start and end apart: 4 -> 5, of which waited for: 3 -> 2; matrix products, arithmetic and copies ran while one was open for 0% -> 0% of each run, Pallas kernels for 6% -> 6%
where the time goes in v5:
time: 62.7 us; the launch traced here: 62.4 us
  blocking collectives  39.7 us (63%)
  starting transfers between devices  8.95 us (14%)
  Pallas kernels  8.63 us (14%)
  waiting for transfers between devices  4.44 us (7%)
  between operations  0.67 us (1%)
    all_to_all x1, blocking collectives, local(): sums = lax.all_to_all(sums, ('core', 'sec'), 0, 0)  17.6 us
    all_to_all x1, blocking collectives, local(): received = lax.all_to_all(chunks, 'chip', 0, 0)  12.9 us
    all_to_all x1, blocking collectives, local(): sums = lax.all_to_all(sums, 'chip', 0, 0)  9.15 us
    ppermute x4, starting transfers between devices, swap(): return lax.ppermute(x, 'core', SWAP)  5.44 us
    all_to_all x1, waiting for transfers between devices, local(): gathered = lax.all_to_all(chunks, 'chip', 0, 0)  4.17 us
    all_to_all x1, starting transfers between devices, local(): gathered = lax.all_to_all(chunks, 'chip', 0, 0)  3.51 us
    pallas_call x1, Pallas kernels, local(): call(renorm_kernel, (shape(left_hbm.shape, BF16), shape((1, states), F32)...  3.1 us
    pallas_call x1, Pallas kernels, local(): call(other_kernel, (shape((states + 16, states), BF16), operators, operat...  2.11 us
  transfers between devices with their start and end apart: 5, of which 2 were waited for; matrix products, arithmetic and copies ran while one was open for 0% of the time, Pallas kernels for 6%

profile of v5, /device:TPU:1, one launch (start us, length us, event | category | flops | bytes accessed | tf_op | source)
XLA Modules:
  0.0 62.4 jit_solution(14186529451604925733)
XLA Ops:
  0.6 2.1 %shard_map.85 = (bf16[272,256]{1,0:T(8,128)(2,1)S(1)}, bf16[4,256,256]{2,1,0:T(8,128)(2,1)S(1)}, bf16[4,256,256]{2,1,0:T(8,128)(2,1)S(1)}, bf16[4,256,256]{2,1,0...) custom-call(s32[2,4]{1,0:T(2,128)} %bitcast.5, ...), custom_call_target="tpu_custom_call" | custom-call | flops 268435456 | bytes 1048576 | tf_op jit(solution)/shard_map/pallas_call | solution.py:238
  2.7 3.3 %collective-permute-start = (bf16[272,256]{1,0:T(8,128)(2,1)S(1)}, bf16[272,256]{1,0:T(8,128)(2,1)S(1)}, u32[]{:S(2)}, u32[]{:S(2)}) collective-permute-start(bf16[272,256]{1,0:T(8,128)(2,1)S(1)} %get-tuple-element.42), channel_id=1, source_target_pairs={{0,8},{8,0},{1,9},{9,1},{2,10},{10,2},{3,11},{11,3},{4,12},{12,4},... | collective-permute-start | bytes 417800 | tf_op jit(solution)/shard_map/ppermute | solution.py:235
  6.1 0.7 %shard_map.86 = (f32[256,256]{1,0:T(8,128)S(1)}, f32[256,256]{1,0:T(8,128)S(1)}, f32[3,16,256]{2,1,0:T(8,128)S(1)}, f32[2,2,8,256]{3,2,1,0:T(8,128)S(1)}) custom-call(f32[2,4,256]{2,1,0:T(4,128)S(1)} %get-tuple-element.35.flags, bf16[4,256,256]{2,1,0:T(8,128)(2,1)S(1)} %get-tuple-element.36.left, bf16[4,256,256]{2,1,0:T(8,128)(2,1)S(1)} %get-tuple-element.37.right, ...), custom_call_target="tpu_custom_call" | custom-call | flops 268435456 | bytes 1048576 | tf_op jit(solution)/shard_map/pallas_call | solution.py:257
  6.8 0.3 collective-permute-done.theirs
  7.1 0.5 collective-permute-start.2
  7.6 0.1 collective-permute-start.1
  7.7 12.9 %all_to_all.20.received = bf16[16,32,256]{2,1,0:T(8,128)(2,1)S(1)} all-to-all(bf16[16,32,256]{2,1,0:T(8,128)(2,1)S(1)} %get-tuple-element.48), channel_id=1, replica_groups=mesh['chip'=16,'core'=2,'sec'=8] {'chip'}, dimensions={0} | all-to-all | bytes 524288 | tf_op jit(solution)/shard_map/all_to_all | solution.py:275
  20.6 0.0 collective-permute-done.2.right_swapped
  20.6 0.0 collective-permute-done.1.left_swapped
  20.6 0.7 %shard_map.88 = (bf16[304,256]{1,0:T(8,128)(2,1)S(1)}, f32[8,256]{1,0:T(8,128)S(1)}, bf16[16,16,256]{2,1,0:T(8,128)(2,1)}) custom-call(bf16[16,32,256]{2,1,0:T(8,128)(2,1)S(1)} %all_to_all.20.received, f32[3,16,256]{2,1,0:T(8,128)S(1)} %get-tuple-element.52.rows_in), custom_call_target="tpu_custom_call" | custom-call | bytes 1048576 | tf_op jit(solution)/shard_map/pallas_call | solution.py:277
  21.3 1.5 %collective-permute-start.3 = (bf16[304,256]{1,0:T(8,128)(2,1)S(1)}, bf16[304,256]{1,0:T(8,128)(2,1)S(1)}, u32[]{:S(2)}, u32[]{:S(2)}) collective-permute-start(bf16[304,256]{1,0:T(8,128)(2,1)S(1)} %get-tuple-element.57.packed), channel_id=1, source_target_pairs={{0,8},{8,0},{1,9},{9,1},{2,10},{10,2},{3,11},{11,3},{4,12},{12,4},... | collective-permute-start | bytes 466952 | tf_op jit(solution)/shard_map/ppermute | solution.py:235
  22.8 3.5 %all-to-all-start.1 = ((bf16[16,16,256]{2,1,0:T(8,128)(2,1)}), bf16[16,16,256]{2,1,0:T(8,128)(2,1)S(1)}, u32[]{:S(2)}, u32[]{:S(2)}) async-start(bf16[16,16,256]{2,1,0:T(8,128)(2,1)} %get-tuple-element.53), calls=%async_computation.1 | async-start | bytes 262144 | tf_op jit(solution)/shard_map/all_to_all | solution.py:282
  26.4 0.0 collective-permute-done.3.packed_theirs
  26.4 3.1 %shard_map.89 = (bf16[4,2,256,256]{3,2,1,0:T(8,128)(2,1)}, f32[1,256]{1,0:T(1,128)S(1)}, f32[2,8,256]{2,1,0:T(8,128)S(1)}) custom-call(f32[8,256]{1,0:T(8,128)S(1)} %get-tuple-element.44.flags, bf16[4,256,256]{2,1,0:T(8,128)(2,1)S(1)} %get-tuple-element.36.left, bf16[4,256,256]{2,1,0:T(8,128)(2,1)S(1)} %get-tuple-element.49.left_other, ...), custom_call_target="tpu_custom_call" | custom-call | flops 1073741824 | bytes 1048576 | tf_op jit(solution)/shard_map/pallas_call | solution.py:283
  29.5 4.2 %all-to-all-done.1.gathered = bf16[16,16,256]{2,1,0:T(8,128)(2,1)S(1)} async-done(((bf16[16,16,256]{2,1,0:T(8,128)(2,1)}), bf16[16,16,256]{2,1,0:T(8,128)(2,1)S(1)}, u32[]{:S(2)}, u32[]{:S(2)}) %all-to-all-start.1) | async-done | bytes 131104 | tf_op jit(solution)/shard_map/all_to_all | solution.py:282
  33.6 1.2 %shard_map.90 = f32[16,1,128]{2,1,0:T(1,128)S(1)} custom-call(f32[8,256]{1,0:T(8,128)S(1)} %get-tuple-element.44.flags, bf16[16,16,256]{2,1,0:T(8,128)(2,1)S(1)} %all-to-all-done.1.gathered, bf16[4,256,256]{2,1,0:T(8,128)(2,1)S(1)} %get-tuple-element.36.left, bf16[4,256,256]{2,1,0:T(8,128)(2,1)S(1)} %get-tuple-element.37.right, ...), custom_call_target="tpu_custom_call" | custom-call | flops 536870912 | bytes 1048576 | tf_op jit(solution)/shard_map/pallas_call | solution.py:290
  34.8 9.2 %all_to_all.21.received = f32[16,1,128]{2,1,0:T(1,128)S(1)} all-to-all(f32[16,1,128]{2,1,0:T(1,128)S(1)} %shard_map.90), channel_id=1, replica_groups=mesh['chip'=16,'core'=2,'sec'=8] {'chip'}, dimensions={0} | all-to-all | bytes 16384 | tf_op jit(solution)/shard_map/all_to_all | solution.py:293
  44.0 17.6 %all_to_all.22.refs_0_ = f32[16,1,128]{2,1,0:T(1,128)S(1)} all-to-all(f32[16,1,128]{2,1,0:T(1,128)S(1)} %shard_map.91), channel_id=1, replica_groups=mesh['chip'=16,'core'=2,'sec'=8] {'core','sec'}, dimensions={0} | all-to-all | bytes 16384 | tf_op jit(solution)/shard_map/all_to_all | solution.py:295
  61.6 0.8 %shard_map.92 = (f32[2,8,256]{2,1,0:T(8,128)}, f32[1,128]{1,0:T(1,128)}) custom-call(f32[16,1,128]{2,1,0:T(1,128)S(1)} %all_to_all.22.refs_0_, f32[2,2,8,256]{3,2,1,0:T(8,128)S(1)} %get-tuple-element.62.refs_1_, f32[2,8,256]{2,1,0:T(8,128)S(1)} %get-tuple-element.63.refs_2_), custom_call_target="tpu_custom_call" | custom-call | bytes 1048576 | tf_op jit(solution)/shard_map/pallas_call | solution.py:296
  (2 shorter events, 0.1 us)
Async XLA Ops:
  2.7 4.3 %collective-permute-start = (bf16[272,256]{1,0:T(8,128)(2,1)S(1)}, bf16[272,256]{1,0:T(8,128)(2,1)S(1)}, u32[]{:S(2)}, u32[]{:S(2)}) collective-permute-start(bf16[272,256]{1,0:T(8,128)(2,1)S(1)} %get-tuple-element.42), channel_id=1, source_target_pairs={{0,8},{8,0},{1,9},{9,1},{2,10},{10,2},{3,11},{11,3},{4,12},{12,4},... | collective-permute-start | bytes 417800 | tf_op jit(solution)/shard_map/ppermute | solution.py:235
  7.1 13.5 %collective-permute-start.2 = (bf16[4,256,256]{2,1,0:T(8,128)(2,1)S(1)}, bf16[4,256,256]{2,1,0:T(8,128)(2,1)S(1)}, u32[]{:S(2)}, u32[]{:S(2)}) collective-permute-start(bf16[4,256,256]{2,1,0:T(8,128)(2,1)S(1)} %get-tuple-element.50), channel_id=1, source_target_pairs={{0,8},{8,0},{1,9},{9,1},{2,10},{10,2},{3,11},{11,3},{4,12},{12,4},... | collective-permute-start | bytes 1572872 | tf_op jit(solution)/shard_map/ppermute | solution.py:235
  7.6 13.1 %collective-permute-start.1 = (bf16[4,256,256]{2,1,0:T(8,128)(2,1)S(1)}, bf16[4,256,256]{2,1,0:T(8,128)(2,1)S(1)}, u32[]{:S(2)}, u32[]{:S(2)}) collective-permute-start(bf16[4,256,256]{2,1,0:T(8,128)(2,1)S(1)} %get-tuple-element.49.left_other), channel_id=1, source_target_pairs={{0,8},{8,0},{1,9},{9,1},{2,10},{10,2},{3,11},{11,3},{4,12},{12,4},... | collective-permute-start | bytes 1572872 | tf_op jit(solution)/shard_map/ppermute | solution.py:235
  21.3 5.0 %collective-permute-start.3 = (bf16[304,256]{1,0:T(8,128)(2,1)S(1)}, bf16[304,256]{1,0:T(8,128)(2,1)S(1)}, u32[]{:S(2)}, u32[]{:S(2)}) collective-permute-start(bf16[304,256]{1,0:T(8,128)(2,1)S(1)} %get-tuple-element.57.packed), channel_id=1, source_target_pairs={{0,8},{8,0},{1,9},{9,1},{2,10},{10,2},{3,11},{11,3},{4,12},{12,4},... | collective-permute-start | bytes 466952 | tf_op jit(solution)/shard_map/ppermute | solution.py:235
  22.8 10.8 %all-to-all-start.1 = ((bf16[16,16,256]{2,1,0:T(8,128)(2,1)}), bf16[16,16,256]{2,1,0:T(8,128)(2,1)S(1)}, u32[]{:S(2)}, u32[]{:S(2)}) async-start(bf16[16,16,256]{2,1,0:T(8,128)(2,1)} %get-tuple-element.53), calls=%async_computation.1 | async-start | bytes 262144 | tf_op jit(solution)/shard_map/all_to_all | solution.py:282

commit v6 on v5

--- a/solution.py
+++ b/solution.py
@@ -25,14 +25,15 @@
     for k in range(count):
         block = left[k]
         half = dot(jnp.concatenate([block] * terms, axis=1), x).astype(BF16)
-        halves.append(half * flags[k : k + 1, :].astype(BF16))
+        parts = [half[:, i : i + states] for i in range(0, half.shape[1], states)]
+        halves.append(jnp.concatenate(parts, axis=0) * flags[k : k + 1, :].astype(BF16))
     return dot(jnp.concatenate(halves, axis=1), right[...].reshape(count * states, states))
 
 
-def chip_image(x, flags, left, right, left_swapped, right_swapped):
+def chip_image(x, flags, left, right, swapped):
     count = left.shape[0]
     own = image_of(x, left, right, flags.at[pl.ds(0, count)])
-    return own + image_of(x, left_swapped, right_swapped, flags.at[pl.ds(count, count)])
+    return own + image_of(x, swapped.at[0], swapped.at[1], flags.at[pl.ds(count, count)])
 
 
 def two_terms(x):
@@ -42,7 +43,7 @@
 
 def other_kernel(
     pattern_hbm, left_hbm, right_hbm, guess_hbm, precond_hbm, columns_hbm,
-    part, left, left_other, right, right_other, guess, precond, rows_other, columns, flags,
+    part, left, right, operators, guess, precond, rows_other, columns, flags,
     pattern, pattern_sem, columns_sem, rows_sem, guess_sem, left_sem, right_sem, precond_sem,
 ):
     mine, chip = lax.axis_index("core"), lax.axis_index("chip")
@@ -54,7 +55,7 @@
         pltpu.make_async_copy(columns_hbm, columns, columns_sem),
     ]
     copies = []
-    for i, (s, l, r) in enumerate(((other, left_other, right_other), (mine, left, right))):
+    for i, (s, l, r) in enumerate(((other, operators.at[0], operators.at[1]), (mine, left, right))):
         copies.append(
             [
                 pltpu.make_async_copy(guess_hbm.at[s], guess.at[s], guess_sem.at[i]),
@@ -78,7 +79,7 @@
     rest = jnp.zeros((part.shape[0] - guess.shape[1] - turned.shape[0] - ones.shape[0], turned.shape[1]), F32)
     for copy in copies[0]:
         copy.wait()
-    image = image_of(two_terms(guess[other]), left_other, right_other, flags.at[other])
+    image = image_of(two_terms(guess[other]), operators.at[0], operators.at[1], flags.at[other])
     part[...] = jnp.concatenate([image, turned, ones, rest], axis=0).astype(BF16)
     for copy in copies[1] + last:
         copy.wait()
@@ -130,7 +131,7 @@
     sums[...] = jnp.concatenate([jnp.sum(a * b, axis=0, keepdims=True) for a, b in pairs], axis=0)
 
 
-def renorm_kernel(flags, left, left_other, right, left_swapped, right_swapped, level, packed, packed_theirs, out, d_hd, state_y):
+def renorm_kernel(left, operators, packed, packed_theirs, out, state_y):
     mine = lax.axis_index("core")
     first = mine == 0
     states = left.shape[2]
@@ -144,37 +145,33 @@
         y.append(jnp.where(first, low, high))
     state_y[mine] = y[0]
     state_y[1 - mine] = y[1]
-    for s, turned, blocks in ((mine, a[:states], left), (1 - mine, b[:states], left_other)):
+    for s, turned, blocks in ((mine, a[:states], left), (1 - mine, b[:states], operators.at[0])):
         rotation = jnp.transpose(turned).astype(BF16)
         turned = turned.astype(BF16)
         for k in range(blocks.shape[0]):
             rotated = dot(blocks[k], rotation).astype(BF16)
             out[k, s] = dot(turned, rotated).astype(BF16)
-    low = level[...].astype(BF16)
-    image = chip_image(low, flags, left, right, left_swapped, right_swapped)
-    d_hd[...] = jnp.sum(level[...] * image, axis=0, keepdims=True)
-
-
-def dots_kernel(flags, gathered, left, right, left_swapped, right_swapped, level, row_sums, d_hd, out):
+
+
+def dots_kernel(flags, gathered, left, right, swapped, level, row_sums, out):
     y = gathered[...].reshape(level.shape)
-    image = chip_image(y, flags, left, right, left_swapped, right_swapped)
+    states = y.shape[1]
+    images = chip_image(jnp.concatenate([y, level[...].astype(BF16)], axis=1), flags, left, right, swapped)
+    image = images[:states]
+    d_hd = jnp.sum(level[...] * images[states:], axis=0, keepdims=True)
     y_hy = jnp.sum(y.astype(F32) * image, axis=0, keepdims=True)
     d_hy = jnp.sum(level[...] * image, axis=0, keepdims=True)
     rest = jnp.zeros((5, y.shape[1]), F32)
-    sums = jnp.concatenate([row_sums[...], y_hy, d_hy, d_hd[...], rest], axis=0)
+    sums = jnp.concatenate([row_sums[...], y_hy, d_hy, d_hd, rest], axis=0)
     sums = jnp.sum(sums, axis=1, keepdims=True)
-    extent = (sums.shape[0], out.shape[2])
+    extent = (sums.shape[0], out.shape[1])
     here = lax.broadcasted_iota(jnp.int32, extent, 0) == lax.broadcasted_iota(jnp.int32, extent, 1)
     line = jnp.sum(jnp.where(here, sums, 0.0), axis=0, keepdims=True)
-    out[...] = jnp.broadcast_to(line[None], out.shape)
-
-
-def gather_kernel(received, out):
-    out[...] = jnp.broadcast_to(jnp.sum(received[...], axis=0)[None], out.shape)
+    out[...] = jnp.broadcast_to(line, out.shape)
 
 
 def state_kernel(entries, received, state_rows, state_y, state, energy_out):
-    sums = jnp.sum(received[...], axis=0)
+    sums = jnp.sum(received[...], axis=0, keepdims=True)
     extent = (16, sums.shape[1])
     here = lax.broadcasted_iota(jnp.int32, extent, 0) == lax.broadcasted_iota(jnp.int32, extent, 1)
     sums = jnp.sum(jnp.where(here, jnp.broadcast_to(sums, extent), 0.0), axis=1, keepdims=True)
@@ -235,14 +232,13 @@
         return lax.ppermute(x, "core", SWAP)
 
     operators = shape((ops,) + block, BF16)
-    part, left, left_other, right, right_other, guess, precond, rows_other, columns, flags = call(
+    part, left, right, others, guess, precond, rows_other, columns, flags = call(
         other_kernel,
         (
             shape((states + 16, states), BF16),
             operators,
             operators,
-            operators,
-            operators,
+            shape((2, ops) + block, BF16),
             shape(guess_hbm.shape, F32),
             shape(block, F32),
             shape((count // cores, states), F32),
@@ -270,29 +266,27 @@
         (shape((chips, 2 * count, states), BF16), shape((2 * ops, states), F32)),
         [VMEM] * 4,
     )(own, theirs, columns, flags)
-    chunks, left_other, right_other = lax.optimization_barrier((chunks, left_other, right_other))
-    left_swapped, right_swapped = swap(left_other), swap(right_other)
+    chunks, others = lax.optimization_barrier((chunks, others))
+    swapped = swap(others)
     received = lax.all_to_all(chunks, "chip", 0, 0)
-    received, left_swapped, right_swapped = lax.optimization_barrier((received, left_swapped, right_swapped))
+    received, swapped = lax.optimization_barrier((received, swapped))
     packed, row_sums, chunks = call(
         rows_kernel,
         (shape((states + 3 * count, states), BF16), shape((8, states), F32), shape((chips, count, states), BF16)),
         [VMEM] * 2,
     )(received, own_rows)
     gathered = lax.all_to_all(chunks, "chip", 0, 0)
-    renormalized, d_hd, state_y = call(
+    sums = call(dots_kernel, shape((chips * cores * zones, 128), F32), [VMEM] * 7, flops)(
+        flags, gathered, left, right, swapped, level, row_sums
+    )
+    sums, packed = lax.optimization_barrier((sums, packed))
+    sums = lax.all_to_all(sums, OPS + ("sec",), 0, 0)
+    renormalized, state_y = call(
         renorm_kernel,
-        (shape(left_hbm.shape, BF16), shape((1, states), F32), shape((sectors, count // cores, states), F32)),
-        [VMEM] * 9,
+        (shape(left_hbm.shape, BF16), shape((sectors, count // cores, states), F32)),
+        [VMEM] * 4,
         2 * flops,
-    )(flags, left, left_other, right, left_swapped, right_swapped, level, packed, swap(packed))
-    gathered, d_hd = lax.optimization_barrier((gathered, d_hd))
-    sums = call(dots_kernel, shape((chips, 1, 128), F32), [VMEM] * 9, flops)(
-        flags, gathered, left, right, left_swapped, right_swapped, level, row_sums, d_hd
-    )
-    sums = lax.all_to_all(sums, "chip", 0, 0)
-    sums = call(gather_kernel, shape((cores * zones, 1, 128), F32), [VMEM])(sums)
-    sums = lax.all_to_all(sums, ("core", "sec"), 0, 0)
+    )(left, others, packed, swap(packed))
     new_state, energy = call(
         lambda *refs: state_kernel(entries, *refs),
         (shape((sectors, count // cores, states), F32), shape((1, 128), F32)),

time: 62.7 us -> 59.4 us (0.947)
  blocking collectives: 39.7 us -> 22.7 us
  starting transfers between devices: 8.95 us -> 19 us
  waiting for transfers between devices: 4.44 us -> 9.13 us
  Pallas kernels: 8.63 us -> 7.66 us
    all_to_all x2 -> x1, blocking collectives: 26.8 us -> 9.57 us  [local(): gathered = lax.all_to_all(chunks, 'chip', 0, 0)]
    all_to_all x1, starting transfers between devices: 3.51 us -> 13 us  [local(): sums = lax.all_to_all(sums, OPS + ('sec',), 0, 0)]
    all_to_all x1, waiting for transfers between devices: 4.17 us -> 7.84 us  [local(): sums = lax.all_to_all(sums, OPS + ('sec',), 0, 0)]
    ppermute x4 -> x3, waiting for transfers between devices: 0.28 us -> 1.29 us  [swap(): return lax.ppermute(x, 'core', SWAP)]
    ppermute x4 -> x3, starting transfers between devices: 5.44 us -> 6.01 us  [swap(): return lax.ppermute(x, 'core', SWAP)]
    pallas_call x3 -> x2, Pallas kernels: 4.31 us -> 3.94 us  [the longest x1 2 us: local(): call(dots_kernel, shape((chips * cores * zones, 128), F32), [VMEM] * 7, f...]
  transfers between devices with their start and end apart: 5 -> 4, of which waited for: 2 -> 3; matrix products, arithmetic and copies ran while one was open for 0% -> 0% of each run, Pallas kernels for 6% -> 5%
where the time goes in v6:
time: 59.4 us; the launch traced here: 59.2 us
  blocking collectives  22.7 us (38%)
  starting transfers between devices  19 us (32%)
  waiting for transfers between devices  9.13 us (15%)
  Pallas kernels  7.66 us (13%)
  between operations  0.66 us (1%)
    all_to_all x1, blocking collectives, local(): received = lax.all_to_all(chunks, 'chip', 0, 0)  13.2 us
    all_to_all x1, starting transfers between devices, local(): sums = lax.all_to_all(sums, OPS + ('sec',), 0, 0)  13 us
    all_to_all x1, blocking collectives, local(): gathered = lax.all_to_all(chunks, 'chip', 0, 0)  9.57 us
    all_to_all x1, waiting for transfers between devices, local(): sums = lax.all_to_all(sums, OPS + ('sec',), 0, 0)  7.84 us
    ppermute x3, starting transfers between devices, swap(): return lax.ppermute(x, 'core', SWAP)  6.01 us
    pallas_call x1, Pallas kernels, local(): call(other_kernel, (shape((states + 16, states), BF16), operators, operat...  2.11 us
    pallas_call x1, Pallas kernels, local(): call(dots_kernel, shape((chips * cores * zones, 128), F32), [VMEM] * 7, f...  2 us
    pallas_call x1, Pallas kernels, local(): call(renorm_kernel, (shape(left_hbm.shape, BF16), shape((sectors, count /...  1.94 us
  transfers between devices with their start and end apart: 4, of which 3 were waited for; matrix products, arithmetic and copies ran while one was open for 0% of the time, Pallas kernels for 5%

profile of v6, /device:TPU:1, one launch (start us, length us, event | category | flops | bytes accessed | tf_op | source)
XLA Modules:
  0.0 59.2 jit_solution(10055804152316807854)
XLA Ops:
  0.6 2.1 %shard_map.85 = (bf16[272,256]{1,0:T(8,128)(2,1)S(1)}, bf16[4,256,256]{2,1,0:T(8,128)(2,1)S(1)}, bf16[4,256,256]{2,1,0:T(8,128)(2,1)S(1)}, bf16[2,4,256,256]{3,2...) custom-call(s32[2,4]{1,0:T(2,128)} %bitcast.10, ...), custom_call_target="tpu_custom_call" | custom-call | flops 268435456 | bytes 1048576 | tf_op jit(solution)/shard_map/pallas_call | solution.py:235
  2.7 3.3 %collective-permute-start = (bf16[272,256]{1,0:T(8,128)(2,1)S(1)}, bf16[272,256]{1,0:T(8,128)(2,1)S(1)}, u32[]{:S(2)}, u32[]{:S(2)}) collective-permute-start(bf16[272,256]{1,0:T(8,128)(2,1)S(1)} %get-tuple-element.38), channel_id=1, source_target_pairs={{0,8},{8,0},{1,9},{9,1},{2,10},{10,2},{3,11},{11,3},{4,12},{12,4},... | collective-permute-start | bytes 417800 | tf_op jit(solution)/shard_map/ppermute | solution.py:232
  6.1 0.7 %shard_map.86 = (f32[256,256]{1,0:T(8,128)S(1)}, f32[256,256]{1,0:T(8,128)S(1)}, f32[3,16,256]{2,1,0:T(8,128)S(1)}, f32[2,2,8,256]{3,2,1,0:T(8,128)S(1)}) custom-call(f32[2,4,256]{2,1,0:T(4,128)S(1)} %get-tuple-element.31.flags, bf16[4,256,256]{2,1,0:T(8,128)(2,1)S(1)} %get-tuple-element.32.left, bf16[4,256,256]{2,1,0:T(8,128)(2,1)S(1)} %get-tuple-element.33.right, ...), custom_call_target="tpu_custom_call" | custom-call | flops 268435456 | bytes 1048576 | tf_op jit(solution)/shard_map/pallas_call | solution.py:253
  6.8 0.3 collective-permute-done.theirs
  7.1 0.4 collective-permute-start.1
  7.6 13.2 %all_to_all.21.received = bf16[16,32,256]{2,1,0:T(8,128)(2,1)S(1)} all-to-all(bf16[16,32,256]{2,1,0:T(8,128)(2,1)S(1)} %get-tuple-element.43), channel_id=1, replica_groups=mesh['chip'=16,'core'=2,'sec'=8] {'chip'}, dimensions={0} | all-to-all | bytes 524288 | tf_op jit(solution)/shard_map/all_to_all | solution.py:271
  20.7 0.0 collective-permute-done.1.swapped
  20.7 0.1 shard_map.88
  20.8 9.6 %all_to_all.22.gathered = bf16[16,16,256]{2,1,0:T(8,128)(2,1)S(1)} all-to-all(bf16[16,16,256]{2,1,0:T(8,128)(2,1)S(1)} %get-tuple-element.47), channel_id=1, replica_groups=mesh['chip'=16,'core'=2,'sec'=8] {'chip'}, dimensions={0} | all-to-all | bytes 262144 | tf_op jit(solution)/shard_map/all_to_all | solution.py:278
  30.3 2.0 %shard_map.89 = f32[256,128]{1,0:T(8,128)} custom-call(f32[8,256]{1,0:T(8,128)S(1)} %get-tuple-element.40.flags, bf16[16,16,256]{2,1,0:T(8,128)(2,1)S(1)} %all_to_all.22.gathered, bf16[4,256,256]{2,1,0:T(8,128)(2,1)S(1)} %get-tuple-element.32.left, bf16[4,256,256]{2,1,0:T(8,128)(2,1)S(1)} %get-tuple-element.33.right, ...), custom_call_target="tpu_custom_call" | custom-call | flops 536870912 | bytes 1048576 | tf_op jit(solution)/shard_map/pallas_call | solution.py:279
  32.4 13.0 %all-to-all-start.2 = ((f32[256,1,128]{2,1,0:T(1,128)}), f32[256,1,128]{2,1,0:T(1,128)S(1)}, u32[]{:S(2)}, u32[]{:S(2)}) async-start(f32[256,1,128]{2,1,0:T(1,128)} %bitcast.3), calls=%async_computation.2 | async-start | bytes 262144 | tf_op jit(solution)/shard_map/all_to_all | solution.py:283
  45.4 2.2 %collective-permute-start.2 = (bf16[304,256]{1,0:T(8,128)(2,1)S(1)}, bf16[304,256]{1,0:T(8,128)(2,1)S(1)}, u32[]{:S(2)}, u32[]{:S(2)}) collective-permute-start(bf16[304,256]{1,0:T(8,128)(2,1)S(1)} %get-tuple-element.54.packed), channel_id=1, source_target_pairs={{0,8},{8,0},{1,9},{9,1},{2,10},{10,2},{3,11},{11,3},{4,12},{12,4},... | collective-permute-start | bytes 466952 | tf_op jit(solution)/shard_map/ppermute | solution.py:232
  47.6 1.0 %collective-permute-done.2.packed_theirs = bf16[304,256]{1,0:T(8,128)(2,1)S(1)} collective-permute-done((bf16[304,256]{1,0:T(8,128)(2,1)S(1)}, bf16[304,256]{1,0:T(8,128)(2,1)S(1)}, u32[]{:S(2)}, u32[]{:S(2)}) %collective-permute-start.2) | collective-permute-done | bytes 155680 | tf_op jit(solution)/shard_map/ppermute | solution.py:232
  48.6 1.9 %shard_map.90 = (bf16[4,2,256,256]{3,2,1,0:T(8,128)(2,1)}, f32[2,8,256]{2,1,0:T(8,128)S(1)}) custom-call(bf16[4,256,256]{2,1,0:T(8,128)(2,1)S(1)} %get-tuple-element.32.left, bf16[2,4,256,256]{3,2,1,0:T(8,128)(2,1)S(1)} %get-tuple-element.44.operators, bf16[304,256]{1,0:T(8,128)(2,1)S(1)} %get-tuple-element.54.packed, ...), custom_call_target="tpu_custom_call" | custom-call | flops 1073741824 | bytes 1048576 | tf_op jit(solution)/shard_map/pallas_call | solution.py:284
  50.5 7.8 %all-to-all-done.2 = f32[256,1,128]{2,1,0:T(1,128)S(1)} async-done(((f32[256,1,128]{2,1,0:T(1,128)}), f32[256,1,128]{2,1,0:T(1,128)S(1)}, u32[]{:S(2)}, u32[]{:S(2)}) %all-to-all-start.2) | async-done | bytes 131104 | tf_op jit(solution)/shard_map/all_to_all | solution.py:283
  58.4 0.8 %shard_map.91 = (f32[2,8,256]{2,1,0:T(8,128)}, f32[1,128]{1,0:T(1,128)}) custom-call(f32[256,128]{1,0:T(8,128)S(1)} %bitcast.8, f32[2,2,8,256]{3,2,1,0:T(8,128)S(1)} %get-tuple-element.53.refs_1_, f32[2,8,256]{2,1,0:T(8,128)S(1)} %get-tuple-element.55.refs_2_), custom_call_target="tpu_custom_call" | custom-call | bytes 1048576 | tf_op jit(solution)/shard_map/pallas_call | solution.py:290
  (1 shorter events, 0.0 us)
Async XLA Ops:
  2.7 4.3 %collective-permute-start = (bf16[272,256]{1,0:T(8,128)(2,1)S(1)}, bf16[272,256]{1,0:T(8,128)(2,1)S(1)}, u32[]{:S(2)}, u32[]{:S(2)}) collective-permute-start(bf16[272,256]{1,0:T(8,128)(2,1)S(1)} %get-tuple-element.38), channel_id=1, source_target_pairs={{0,8},{8,0},{1,9},{9,1},{2,10},{10,2},{3,11},{11,3},{4,12},{12,4},... | collective-permute-start | bytes 417800 | tf_op jit(solution)/shard_map/ppermute | solution.py:232
  7.1 13.6 %collective-permute-start.1 = (bf16[2,4,256,256]{3,2,1,0:T(8,128)(2,1)S(1)}, bf16[2,4,256,256]{3,2,1,0:T(8,128)(2,1)S(1)}, u32[]{:S(2)}, u32[]{:S(2)}) collective-permute-start(bf16[2,4,256,256]{3,2,1,0:T(8,128)(2,1)S(1)} %get-tuple-element.44.operators), channel_id=1, source_target_pairs={{0,8},{8,0},{1,9},{9,1},{2,10},{10,2},{3,11},{11,3},{4,12},{12,4},... | collective-permute-start | bytes 3145736 | tf_op jit(solution)/shard_map/ppermute | solution.py:232
  32.4 26.0 %all-to-all-start.2 = ((f32[256,1,128]{2,1,0:T(1,128)}), f32[256,1,128]{2,1,0:T(1,128)S(1)}, u32[]{:S(2)}, u32[]{:S(2)}) async-start(f32[256,1,128]{2,1,0:T(1,128)} %bitcast.3), calls=%async_computation.2 | async-start | bytes 262144 | tf_op jit(solution)/shard_map/all_to_all | solution.py:283
  45.4 3.3 %collective-permute-start.2 = (bf16[304,256]{1,0:T(8,128)(2,1)S(1)}, bf16[304,256]{1,0:T(8,128)(2,1)S(1)}, u32[]{:S(2)}, u32[]{:S(2)}) collective-permute-start(bf16[304,256]{1,0:T(8,128)(2,1)S(1)} %get-tuple-element.54.packed), channel_id=1, source_target_pairs={{0,8},{8,0},{1,9},{9,1},{2,10},{10,2},{3,11},{11,3},{4,12},{12,4},... | collective-permute-start | bytes 466952 | tf_op jit(solution)/shard_map/ppermute | solution.py:232

commit v7 on v6

--- a/solution.py
+++ b/solution.py
@@ -266,10 +266,9 @@
         (shape((chips, 2 * count, states), BF16), shape((2 * ops, states), F32)),
         [VMEM] * 4,
     )(own, theirs, columns, flags)
-    chunks, others = lax.optimization_barrier((chunks, others))
+    received = lax.all_to_all(chunks, "chip", 0, 0)
+    received, others = lax.optimization_barrier((received, others))
     swapped = swap(others)
-    received = lax.all_to_all(chunks, "chip", 0, 0)
-    received, swapped = lax.optimization_barrier((received, swapped))
     packed, row_sums, chunks = call(
         rows_kernel,
         (shape((states + 3 * count, states), BF16), shape((8, states), F32), shape((chips, count, states), BF16)),

time: 59.4 us -> 59 us (level)
    all_to_all x1, starting transfers between devices: 13 us -> 11.5 us  [local(): sums = lax.all_to_all(sums, OPS + ('sec',), 0, 0)]
    ppermute x3, starting transfers between devices: 6.01 us -> 7.07 us  [swap(): return lax.ppermute(x, 'core', SWAP)]
where the time goes in v7:
time: 59 us; the launch traced here: 58.8 us
  blocking collectives  22.7 us (38%)
  starting transfers between devices  18.6 us (32%)
  waiting for transfers between devices  9.13 us (15%)
  Pallas kernels  7.66 us (13%)
  between operations  0.66 us (1%)
    all_to_all x1, blocking collectives, local(): received = lax.all_to_all(chunks, 'chip', 0, 0)  12.9 us
    all_to_all x1, starting transfers between devices, local(): sums = lax.all_to_all(sums, OPS + ('sec',), 0, 0)  11.5 us
    all_to_all x1, blocking collectives, local(): gathered = lax.all_to_all(chunks, 'chip', 0, 0)  9.75 us
    all_to_all x1, waiting for transfers between devices, local(): sums = lax.all_to_all(sums, OPS + ('sec',), 0, 0)  7.84 us
    ppermute x3, starting transfers between devices, swap(): return lax.ppermute(x, 'core', SWAP)  7.07 us
    pallas_call x1, Pallas kernels, local(): call(other_kernel, (shape((states + 16, states), BF16), operators, operat...  2.11 us
    pallas_call x1, Pallas kernels, local(): call(dots_kernel, shape((chips * cores * zones, 128), F32), [VMEM] * 7, f...  2 us
    pallas_call x1, Pallas kernels, local(): call(renorm_kernel, (shape(left_hbm.shape, BF16), shape((sectors, count /...  1.94 us
  transfers between devices with their start and end apart: 4, of which 3 were waited for; matrix products, arithmetic and copies ran while one was open for 0% of the time, Pallas kernels for 5%

profile of v7, /device:TPU:1, one launch (start us, length us, event | category | flops | bytes accessed | tf_op | source)
XLA Modules:
  0.0 58.8 jit_solution(5312803105408238833)
XLA Ops:
  0.6 2.1 %shard_map.85 = (bf16[272,256]{1,0:T(8,128)(2,1)S(1)}, bf16[4,256,256]{2,1,0:T(8,128)(2,1)S(1)}, bf16[4,256,256]{2,1,0:T(8,128)(2,1)S(1)}, bf16[2,4,256,256]{3,2...) custom-call(s32[2,4]{1,0:T(2,128)} %bitcast.10, ...), custom_call_target="tpu_custom_call" | custom-call | flops 268435456 | bytes 1048576 | tf_op jit(solution)/shard_map/pallas_call | solution.py:235
  2.7 3.3 %collective-permute-start = (bf16[272,256]{1,0:T(8,128)(2,1)S(1)}, bf16[272,256]{1,0:T(8,128)(2,1)S(1)}, u32[]{:S(2)}, u32[]{:S(2)}) collective-permute-start(bf16[272,256]{1,0:T(8,128)(2,1)S(1)} %get-tuple-element.36), channel_id=1, source_target_pairs={{0,8},{8,0},{1,9},{9,1},{2,10},{10,2},{3,11},{11,3},{4,12},{12,4},... | collective-permute-start | bytes 417800 | tf_op jit(solution)/shard_map/ppermute | solution.py:232
  6.1 0.7 %shard_map.86 = (f32[256,256]{1,0:T(8,128)S(1)}, f32[256,256]{1,0:T(8,128)S(1)}, f32[3,16,256]{2,1,0:T(8,128)S(1)}, f32[2,2,8,256]{3,2,1,0:T(8,128)S(1)}) custom-call(f32[2,4,256]{2,1,0:T(4,128)S(1)} %get-tuple-element.29.flags, bf16[4,256,256]{2,1,0:T(8,128)(2,1)S(1)} %get-tuple-element.30.left, bf16[4,256,256]{2,1,0:T(8,128)(2,1)S(1)} %get-tuple-element.31.right, ...), custom_call_target="tpu_custom_call" | custom-call | flops 268435456 | bytes 1048576 | tf_op jit(solution)/shard_map/pallas_call | solution.py:253
  6.8 0.3 collective-permute-done.theirs
  7.1 12.9 %all_to_all.21.received = bf16[16,32,256]{2,1,0:T(8,128)(2,1)S(1)} all-to-all(bf16[16,32,256]{2,1,0:T(8,128)(2,1)S(1)} %get-tuple-element.39), channel_id=1, replica_groups=mesh['chip'=16,'core'=2,'sec'=8] {'chip'}, dimensions={0} | all-to-all | bytes 524288 | tf_op jit(solution)/shard_map/all_to_all | solution.py:269
  20.1 1.5 %collective-permute-start.1 = (bf16[2,4,256,256]{3,2,1,0:T(8,128)(2,1)S(1)}, bf16[2,4,256,256]{3,2,1,0:T(8,128)(2,1)S(1)}, u32[]{:S(2)}, u32[]{:S(2)}) collective-permute-start(bf16[2,4,256,256]{3,2,1,0:T(8,128)(2,1)S(1)} %get-tuple-element.44.operators), channel_id=1, source_target_pairs={{0,8},{8,0},{1,9},{9,1},{2,10},{10,2},{3,11},{11,3},{4,12},{12,4},... | collective-permute-start | bytes 3145736 | tf_op jit(solution)/shard_map/ppermute | solution.py:232
  21.6 0.1 shard_map.88
  21.6 9.8 %all_to_all.22.gathered = bf16[16,16,256]{2,1,0:T(8,128)(2,1)S(1)} all-to-all(bf16[16,16,256]{2,1,0:T(8,128)(2,1)S(1)} %get-tuple-element.43), channel_id=1, replica_groups=mesh['chip'=16,'core'=2,'sec'=8] {'chip'}, dimensions={0} | all-to-all | bytes 262144 | tf_op jit(solution)/shard_map/all_to_all | solution.py:277
  31.4 0.0 collective-permute-done.1.swapped
  31.4 2.0 %shard_map.89 = f32[256,128]{1,0:T(8,128)} custom-call(f32[8,256]{1,0:T(8,128)S(1)} %get-tuple-element.38.flags, bf16[16,16,256]{2,1,0:T(8,128)(2,1)S(1)} %all_to_all.22.gathered, bf16[4,256,256]{2,1,0:T(8,128)(2,1)S(1)} %get-tuple-element.30.left, bf16[4,256,256]{2,1,0:T(8,128)(2,1)S(1)} %get-tuple-element.31.right, ...), custom_call_target="tpu_custom_call" | custom-call | flops 536870912 | bytes 1048576 | tf_op jit(solution)/shard_map/pallas_call | solution.py:278
  33.4 11.5 %all-to-all-start.2 = ((f32[256,1,128]{2,1,0:T(1,128)}), f32[256,1,128]{2,1,0:T(1,128)S(1)}, u32[]{:S(2)}, u32[]{:S(2)}) async-start(f32[256,1,128]{2,1,0:T(1,128)} %bitcast.3), calls=%async_computation.2 | async-start | bytes 262144 | tf_op jit(solution)/shard_map/all_to_all | solution.py:282
  44.9 2.2 %collective-permute-start.2 = (bf16[304,256]{1,0:T(8,128)(2,1)S(1)}, bf16[304,256]{1,0:T(8,128)(2,1)S(1)}, u32[]{:S(2)}, u32[]{:S(2)}) collective-permute-start(bf16[304,256]{1,0:T(8,128)(2,1)S(1)} %get-tuple-element.50.packed), channel_id=1, source_target_pairs={{0,8},{8,0},{1,9},{9,1},{2,10},{10,2},{3,11},{11,3},{4,12},{12,4},... | collective-permute-start | bytes 466952 | tf_op jit(solution)/shard_map/ppermute | solution.py:232
  47.2 1.0 %collective-permute-done.2.packed_theirs = bf16[304,256]{1,0:T(8,128)(2,1)S(1)} collective-permute-done((bf16[304,256]{1,0:T(8,128)(2,1)S(1)}, bf16[304,256]{1,0:T(8,128)(2,1)S(1)}, u32[]{:S(2)}, u32[]{:S(2)}) %collective-permute-start.2) | collective-permute-done | bytes 155680 | tf_op jit(solution)/shard_map/ppermute | solution.py:232
  48.2 1.9 %shard_map.90 = (bf16[4,2,256,256]{3,2,1,0:T(8,128)(2,1)}, f32[2,8,256]{2,1,0:T(8,128)S(1)}) custom-call(bf16[4,256,256]{2,1,0:T(8,128)(2,1)S(1)} %get-tuple-element.30.left, bf16[2,4,256,256]{3,2,1,0:T(8,128)(2,1)S(1)} %get-tuple-element.44.operators, bf16[304,256]{1,0:T(8,128)(2,1)S(1)} %get-tuple-element.50.packed, ...), custom_call_target="tpu_custom_call" | custom-call | flops 1073741824 | bytes 1048576 | tf_op jit(solution)/shard_map/pallas_call | solution.py:283
  50.1 7.8 %all-to-all-done.2 = f32[256,1,128]{2,1,0:T(1,128)S(1)} async-done(((f32[256,1,128]{2,1,0:T(1,128)}), f32[256,1,128]{2,1,0:T(1,128)S(1)}, u32[]{:S(2)}, u32[]{:S(2)}) %all-to-all-start.2) | async-done | bytes 131104 | tf_op jit(solution)/shard_map/all_to_all | solution.py:282
  58.0 0.8 %shard_map.91 = (f32[2,8,256]{2,1,0:T(8,128)}, f32[1,128]{1,0:T(1,128)}) custom-call(f32[256,128]{1,0:T(8,128)S(1)} %bitcast.8, f32[2,2,8,256]{3,2,1,0:T(8,128)S(1)} %get-tuple-element.49.refs_1_, f32[2,8,256]{2,1,0:T(8,128)S(1)} %get-tuple-element.51.refs_2_), custom_call_target="tpu_custom_call" | custom-call | bytes 1048576 | tf_op jit(solution)/shard_map/pallas_call | solution.py:289
  (1 shorter events, 0.0 us)
Async XLA Ops:
  2.7 4.3 %collective-permute-start = (bf16[272,256]{1,0:T(8,128)(2,1)S(1)}, bf16[272,256]{1,0:T(8,128)(2,1)S(1)}, u32[]{:S(2)}, u32[]{:S(2)}) collective-permute-start(bf16[272,256]{1,0:T(8,128)(2,1)S(1)} %get-tuple-element.36), channel_id=1, source_target_pairs={{0,8},{8,0},{1,9},{9,1},{2,10},{10,2},{3,11},{11,3},{4,12},{12,4},... | collective-permute-start | bytes 417800 | tf_op jit(solution)/shard_map/ppermute | solution.py:232
  20.1 11.3 %collective-permute-start.1 = (bf16[2,4,256,256]{3,2,1,0:T(8,128)(2,1)S(1)}, bf16[2,4,256,256]{3,2,1,0:T(8,128)(2,1)S(1)}, u32[]{:S(2)}, u32[]{:S(2)}) collective-permute-start(bf16[2,4,256,256]{3,2,1,0:T(8,128)(2,1)S(1)} %get-tuple-element.44.operators), channel_id=1, source_target_pairs={{0,8},{8,0},{1,9},{9,1},{2,10},{10,2},{3,11},{11,3},{4,12},{12,4},... | collective-permute-start | bytes 3145736 | tf_op jit(solution)/shard_map/ppermute | solution.py:232
  33.4 24.6 %all-to-all-start.2 = ((f32[256,1,128]{2,1,0:T(1,128)}), f32[256,1,128]{2,1,0:T(1,128)S(1)}, u32[]{:S(2)}, u32[]{:S(2)}) async-start(f32[256,1,128]{2,1,0:T(1,128)} %bitcast.3), calls=%async_computation.2 | async-start | bytes 262144 | tf_op jit(solution)/shard_map/all_to_all | solution.py:282
  44.9 3.3 %collective-permute-start.2 = (bf16[304,256]{1,0:T(8,128)(2,1)S(1)}, bf16[304,256]{1,0:T(8,128)(2,1)S(1)}, u32[]{:S(2)}, u32[]{:S(2)}) collective-permute-start(bf16[304,256]{1,0:T(8,128)(2,1)S(1)} %get-tuple-element.50.packed), channel_id=1, source_target_pairs={{0,8},{8,0},{1,9},{9,1},{2,10},{10,2},{3,11},{11,3},{4,12},{12,4},... | collective-permute-start | bytes 466952 | tf_op jit(solution)/shard_map/ppermute | solution.py:232

commit v8 on v7

--- a/solution.py
+++ b/solution.py
@@ -39,6 +39,12 @@
 def two_terms(x):
     high = x.astype(BF16)
     return jnp.concatenate([high, (x - high.astype(F32)).astype(BF16)], axis=0)
+
+
+def columns_of(columns, s):
+    both = columns[...].astype(F32)
+    count = both.shape[0] // 2
+    return jnp.where(s == 0, both[:count], both[count:])
 
 
 def other_kernel(
@@ -74,7 +80,7 @@
     for s in range(flags.shape[0]):
         for k in range(flags.shape[1]):
             flags[s, pl.ds(k, 1), :] = jnp.full((1, flags.shape[2]), pattern[s, k].astype(F32))
-    turned = columns[other].astype(F32)
+    turned = columns_of(columns, other)
     ones = flags[other]
     rest = jnp.zeros((part.shape[0] - guess.shape[1] - turned.shape[0] - ones.shape[0], turned.shape[1]), F32)
     for copy in copies[0]:
@@ -108,11 +114,12 @@
     chips, count, states = chunks.shape
     theirs = theirs[...].astype(F32)
     total = own[...] + theirs[:states]
-    a, b = columns[mine].astype(F32), theirs[states : states + columns.shape[1]]
+    a = columns_of(columns, mine)
+    b = theirs[states : states + a.shape[0]]
     first = mine == 0
     turned = jnp.concatenate([jnp.where(first, a, b), jnp.where(first, b, a)], axis=0)
     turned = jnp.broadcast_to(turned[None], (chips,) + turned.shape)
-    ones = theirs[states + columns.shape[1] :][: flags.shape[1]]
+    ones = theirs[states + a.shape[0] :][: flags.shape[1]]
     all_flags[...] = jnp.concatenate([flags[mine], ones], axis=0)
     chunks[...] = jnp.concatenate([total.reshape(chips, -1, states), turned], axis=1).astype(BF16)
 
@@ -223,7 +230,7 @@
     block = (states, states)
     flops = 4 * ops * sectors * states**3
     pattern = jnp.swapaxes(pattern, 0, 1)
-    columns = jnp.swapaxes(rotation, 1, 2)
+    columns = jnp.swapaxes(rotation, 1, 2).reshape(-1, states)
 
     def in_hbm(x):
         return pltpu.with_memory_space_constraint(x, pltpu.HBM)

time: 59 us -> 59 us (level)
  no operation moved by 1% of the time
where the time goes in v8:
time: 59 us; the launch traced here: 58.8 us
  blocking collectives  22.7 us (38%)
  starting transfers between devices  18.6 us (32%)
  waiting for transfers between devices  9.13 us (15%)
  Pallas kernels  7.66 us (13%)
  between operations  0.66 us (1%)
    all_to_all x1, blocking collectives, local(): received = lax.all_to_all(chunks, 'chip', 0, 0)  12.9 us
    all_to_all x1, starting transfers between devices, local(): sums = lax.all_to_all(sums, OPS + ('sec',), 0, 0)  11.5 us
    all_to_all x1, blocking collectives, local(): gathered = lax.all_to_all(chunks, 'chip', 0, 0)  9.75 us
    all_to_all x1, waiting for transfers between devices, local(): sums = lax.all_to_all(sums, OPS + ('sec',), 0, 0)  7.84 us
    ppermute x3, starting transfers between devices, swap(): return lax.ppermute(x, 'core', SWAP)  7.07 us
    pallas_call x1, Pallas kernels, local(): call(other_kernel, (shape((states + 16, states), BF16), operators, operat...  2.11 us
    pallas_call x1, Pallas kernels, local(): call(dots_kernel, shape((chips * cores * zones, 128), F32), [VMEM] * 7, f...  2 us
    pallas_call x1, Pallas kernels, local(): call(renorm_kernel, (shape(left_hbm.shape, BF16), shape((sectors, count /...  1.94 us
  transfers between devices with their start and end apart: 4, of which 3 were waited for; matrix products, arithmetic and copies ran while one was open for 0% of the time, Pallas kernels for 5%

profile of v8, /device:TPU:1, one launch (start us, length us, event | category | flops | bytes accessed | tf_op | source)
XLA Modules:
  0.0 58.8 jit_solution(10526751999349190474)
XLA Ops:
  0.6 2.1 %shard_map.85 = (bf16[272,256]{1,0:T(8,128)(2,1)S(1)}, bf16[4,256,256]{2,1,0:T(8,128)(2,1)S(1)}, bf16[4,256,256]{2,1,0:T(8,128)(2,1)S(1)}, bf16[2,4,256,256]{3,2...) custom-call(s32[2,4]{1,0:T(2,128)} %bitcast.12, ...), custom_call_target="tpu_custom_call" | custom-call | flops 268435456 | bytes 1048576 | tf_op jit(solution)/shard_map/pallas_call | solution.py:242
  2.7 3.3 %collective-permute-start = (bf16[272,256]{1,0:T(8,128)(2,1)S(1)}, bf16[272,256]{1,0:T(8,128)(2,1)S(1)}, u32[]{:S(2)}, u32[]{:S(2)}) collective-permute-start(bf16[272,256]{1,0:T(8,128)(2,1)S(1)} %get-tuple-element.36), channel_id=1, source_target_pairs={{0,8},{8,0},{1,9},{9,1},{2,10},{10,2},{3,11},{11,3},{4,12},{12,4},... | collective-permute-start | bytes 417800 | tf_op jit(solution)/shard_map/ppermute | solution.py:239
  6.1 0.7 %shard_map.86 = (f32[256,256]{1,0:T(8,128)S(1)}, f32[256,256]{1,0:T(8,128)S(1)}, f32[3,16,256]{2,1,0:T(8,128)S(1)}, f32[2,2,8,256]{3,2,1,0:T(8,128)S(1)}) custom-call(f32[2,4,256]{2,1,0:T(4,128)S(1)} %get-tuple-element.29.flags, bf16[4,256,256]{2,1,0:T(8,128)(2,1)S(1)} %get-tuple-element.30.left, bf16[4,256,256]{2,1,0:T(8,128)(2,1)S(1)} %get-tuple-element.31.right, ...), custom_call_target="tpu_custom_call" | custom-call | flops 268435456 | bytes 1048576 | tf_op jit(solution)/shard_map/pallas_call | solution.py:260
  6.8 0.3 collective-permute-done.theirs
  7.1 12.9 %all_to_all.21.received = bf16[16,32,256]{2,1,0:T(8,128)(2,1)S(1)} all-to-all(bf16[16,32,256]{2,1,0:T(8,128)(2,1)S(1)} %get-tuple-element.39), channel_id=1, replica_groups=mesh['chip'=16,'core'=2,'sec'=8] {'chip'}, dimensions={0} | all-to-all | bytes 524288 | tf_op jit(solution)/shard_map/all_to_all | solution.py:276
  20.1 1.5 %collective-permute-start.1 = (bf16[2,4,256,256]{3,2,1,0:T(8,128)(2,1)S(1)}, bf16[2,4,256,256]{3,2,1,0:T(8,128)(2,1)S(1)}, u32[]{:S(2)}, u32[]{:S(2)}) collective-permute-start(bf16[2,4,256,256]{3,2,1,0:T(8,128)(2,1)S(1)} %get-tuple-element.44.operators), channel_id=1, source_target_pairs={{0,8},{8,0},{1,9},{9,1},{2,10},{10,2},{3,11},{11,3},{4,12},{12,4},... | collective-permute-start | bytes 3145736 | tf_op jit(solution)/shard_map/ppermute | solution.py:239
  21.6 0.1 shard_map.88
  21.6 9.8 %all_to_all.22.gathered = bf16[16,16,256]{2,1,0:T(8,128)(2,1)S(1)} all-to-all(bf16[16,16,256]{2,1,0:T(8,128)(2,1)S(1)} %get-tuple-element.43), channel_id=1, replica_groups=mesh['chip'=16,'core'=2,'sec'=8] {'chip'}, dimensions={0} | all-to-all | bytes 262144 | tf_op jit(solution)/shard_map/all_to_all | solution.py:284
  31.4 0.0 collective-permute-done.1.swapped
  31.4 2.0 %shard_map.89 = f32[256,128]{1,0:T(8,128)} custom-call(f32[8,256]{1,0:T(8,128)S(1)} %get-tuple-element.38.flags, bf16[16,16,256]{2,1,0:T(8,128)(2,1)S(1)} %all_to_all.22.gathered, bf16[4,256,256]{2,1,0:T(8,128)(2,1)S(1)} %get-tuple-element.30.left, bf16[4,256,256]{2,1,0:T(8,128)(2,1)S(1)} %get-tuple-element.31.right, ...), custom_call_target="tpu_custom_call" | custom-call | flops 536870912 | bytes 1048576 | tf_op jit(solution)/shard_map/pallas_call | solution.py:285
  33.4 11.5 %all-to-all-start.2 = ((f32[256,1,128]{2,1,0:T(1,128)}), f32[256,1,128]{2,1,0:T(1,128)S(1)}, u32[]{:S(2)}, u32[]{:S(2)}) async-start(f32[256,1,128]{2,1,0:T(1,128)} %bitcast.4), calls=%async_computation.2 | async-start | bytes 262144 | tf_op jit(solution)/shard_map/all_to_all | solution.py:289
  44.9 2.2 %collective-permute-start.2 = (bf16[304,256]{1,0:T(8,128)(2,1)S(1)}, bf16[304,256]{1,0:T(8,128)(2,1)S(1)}, u32[]{:S(2)}, u32[]{:S(2)}) collective-permute-start(bf16[304,256]{1,0:T(8,128)(2,1)S(1)} %get-tuple-element.50.packed), channel_id=1, source_target_pairs={{0,8},{8,0},{1,9},{9,1},{2,10},{10,2},{3,11},{11,3},{4,12},{12,4},... | collective-permute-start | bytes 466952 | tf_op jit(solution)/shard_map/ppermute | solution.py:239
  47.2 1.0 %collective-permute-done.2.packed_theirs = bf16[304,256]{1,0:T(8,128)(2,1)S(1)} collective-permute-done((bf16[304,256]{1,0:T(8,128)(2,1)S(1)}, bf16[304,256]{1,0:T(8,128)(2,1)S(1)}, u32[]{:S(2)}, u32[]{:S(2)}) %collective-permute-start.2) | collective-permute-done | bytes 155680 | tf_op jit(solution)/shard_map/ppermute | solution.py:239
  48.2 1.9 %shard_map.90 = (bf16[4,2,256,256]{3,2,1,0:T(8,128)(2,1)}, f32[2,8,256]{2,1,0:T(8,128)S(1)}) custom-call(bf16[4,256,256]{2,1,0:T(8,128)(2,1)S(1)} %get-tuple-element.30.left, bf16[2,4,256,256]{3,2,1,0:T(8,128)(2,1)S(1)} %get-tuple-element.44.operators, bf16[304,256]{1,0:T(8,128)(2,1)S(1)} %get-tuple-element.50.packed, ...), custom_call_target="tpu_custom_call" | custom-call | flops 1073741824 | bytes 1048576 | tf_op jit(solution)/shard_map/pallas_call | solution.py:290
  50.1 7.8 %all-to-all-done.2 = f32[256,1,128]{2,1,0:T(1,128)S(1)} async-done(((f32[256,1,128]{2,1,0:T(1,128)}), f32[256,1,128]{2,1,0:T(1,128)S(1)}, u32[]{:S(2)}, u32[]{:S(2)}) %all-to-all-start.2) | async-done | bytes 131104 | tf_op jit(solution)/shard_map/all_to_all | solution.py:289
  58.0 0.8 %shard_map.91 = (f32[2,8,256]{2,1,0:T(8,128)}, f32[1,128]{1,0:T(1,128)}) custom-call(f32[256,128]{1,0:T(8,128)S(1)} %bitcast.10, f32[2,2,8,256]{3,2,1,0:T(8,128)S(1)} %get-tuple-element.49.refs_1_, f32[2,8,256]{2,1,0:T(8,128)S(1)} %get-tuple-element.51.refs_2_), custom_call_target="tpu_custom_call" | custom-call | bytes 1048576 | tf_op jit(solution)/shard_map/pallas_call | solution.py:296
  (1 shorter events, 0.0 us)
Async XLA Ops:
  2.7 4.3 %collective-permute-start = (bf16[272,256]{1,0:T(8,128)(2,1)S(1)}, bf16[272,256]{1,0:T(8,128)(2,1)S(1)}, u32[]{:S(2)}, u32[]{:S(2)}) collective-permute-start(bf16[272,256]{1,0:T(8,128)(2,1)S(1)} %get-tuple-element.36), channel_id=1, source_target_pairs={{0,8},{8,0},{1,9},{9,1},{2,10},{10,2},{3,11},{11,3},{4,12},{12,4},... | collective-permute-start | bytes 417800 | tf_op jit(solution)/shard_map/ppermute | solution.py:239
  20.1 11.3 %collective-permute-start.1 = (bf16[2,4,256,256]{3,2,1,0:T(8,128)(2,1)S(1)}, bf16[2,4,256,256]{3,2,1,0:T(8,128)(2,1)S(1)}, u32[]{:S(2)}, u32[]{:S(2)}) collective-permute-start(bf16[2,4,256,256]{3,2,1,0:T(8,128)(2,1)S(1)} %get-tuple-element.44.operators), channel_id=1, source_target_pairs={{0,8},{8,0},{1,9},{9,1},{2,10},{10,2},{3,11},{11,3},{4,12},{12,4},... | collective-permute-start | bytes 3145736 | tf_op jit(solution)/shard_map/ppermute | solution.py:239
  33.4 24.6 %all-to-all-start.2 = ((f32[256,1,128]{2,1,0:T(1,128)}), f32[256,1,128]{2,1,0:T(1,128)S(1)}, u32[]{:S(2)}, u32[]{:S(2)}) async-start(f32[256,1,128]{2,1,0:T(1,128)} %bitcast.4), calls=%async_computation.2 | async-start | bytes 262144 | tf_op jit(solution)/shard_map/all_to_all | solution.py:289
  44.9 3.3 %collective-permute-start.2 = (bf16[304,256]{1,0:T(8,128)(2,1)S(1)}, bf16[304,256]{1,0:T(8,128)(2,1)S(1)}, u32[]{:S(2)}, u32[]{:S(2)}) collective-permute-start(bf16[304,256]{1,0:T(8,128)(2,1)S(1)} %get-tuple-element.50.packed), channel_id=1, source_target_pairs={{0,8},{8,0},{1,9},{9,1},{2,10},{10,2},{3,11},{11,3},{4,12},{12,4},... | collective-permute-start | bytes 466952 | tf_op jit(solution)/shard_map/ppermute | solution.py:239

commit v9 on v8

--- a/solution.py
+++ b/solution.py
@@ -49,13 +49,11 @@
 
 def other_kernel(
     pattern_hbm, left_hbm, right_hbm, guess_hbm, precond_hbm, columns_hbm,
-    part, left, right, operators, guess, precond, rows_other, columns, flags,
-    pattern, pattern_sem, columns_sem, rows_sem, guess_sem, left_sem, right_sem, precond_sem,
+    part, left, right, operators, guess, precond, columns, flags,
+    pattern, pattern_sem, columns_sem, guess_sem, left_sem, right_sem, precond_sem,
 ):
-    mine, chip = lax.axis_index("core"), lax.axis_index("chip")
+    mine = lax.axis_index("core")
     other = 1 - mine
-    count = rows_other.shape[0]
-    own = pl.ds(pl.multiple_of((chip * 2 + mine) * count, count), count)
     small = [
         pltpu.make_async_copy(pattern_hbm, pattern, pattern_sem),
         pltpu.make_async_copy(columns_hbm, columns, columns_sem),
@@ -69,11 +67,8 @@
                 pltpu.make_async_copy(right_hbm.at[:, s], r, right_sem.at[i]),
             ]
         )
-    last = [
-        pltpu.make_async_copy(precond_hbm.at[mine], precond, precond_sem),
-        pltpu.make_async_copy(precond_hbm.at[other, own], rows_other, rows_sem),
-    ]
-    for copy in small + copies[0] + copies[1] + last:
+    last = [pltpu.make_async_copy(precond_hbm, precond, precond_sem)]
+    for copy in copies[0] + small + copies[1] + last:
         copy.start()
     for copy in small:
         copy.wait()
@@ -91,22 +86,26 @@
         copy.wait()
 
 
-def own_kernel(flags, left, right, guess, precond, rows_other, part, level, rows_out, state_rows):
+def own_kernel(flags, left, right, operators, guess, precond, part, level, rows_out, state_rows, d_hd):
     mine, chip = lax.axis_index("core"), lax.axis_index("chip")
     other = 1 - mine
     part[...] = image_of(two_terms(guess[mine]), left, right, flags.at[mine])
-    level[...] = guess[mine] / precond[...]
+    level[...] = guess[...] / precond[...]
+    dots = []
+    for s, l, r in ((mine, left, right), (other, operators.at[0], operators.at[1])):
+        d = level[s]
+        image = image_of(d.astype(BF16), l, r, flags.at[s])
+        dots.append(jnp.sum((d * image).reshape(-1, 8, d.shape[1]), axis=0))
+    d_hd[...] = dots[0] + dots[1]
     count = rows_out.shape[1]
     own = pl.ds(pl.multiple_of(chip * count, count), count)
-    rows_out[0] = guess[mine, own, :]
-    rows_out[1] = level[own, :]
-    rows_out[2] = precond[own, :]
+    for i, ref in enumerate((guess, level, precond)):
+        rows_out[i] = ref[mine, own, :]
     count = state_rows.shape[2]
     own = pl.ds(pl.multiple_of((chip * 2 + mine) * count, count), count)
-    state_rows[0, mine] = guess[mine, own, :]
-    state_rows[1, mine] = level[own, :]
-    state_rows[0, other] = guess[other, own, :]
-    state_rows[1, other] = guess[other, own, :] / rows_other[...]
+    for i, ref in enumerate((guess, level)):
+        for s in range(ref.shape[0]):
+            state_rows[i, s] = ref[s, own, :]
 
 
 def chunks_kernel(own, theirs, columns, flags, chunks, all_flags):
@@ -160,19 +159,15 @@
             out[k, s] = dot(turned, rotated).astype(BF16)
 
 
-def dots_kernel(flags, gathered, left, right, swapped, level, row_sums, out):
-    y = gathered[...].reshape(level.shape)
-    states = y.shape[1]
-    images = chip_image(jnp.concatenate([y, level[...].astype(BF16)], axis=1), flags, left, right, swapped)
-    image = images[:states]
-    d_hd = jnp.sum(level[...] * images[states:], axis=0, keepdims=True)
-    y_hy = jnp.sum(y.astype(F32) * image, axis=0, keepdims=True)
-    d_hy = jnp.sum(level[...] * image, axis=0, keepdims=True)
-    rest = jnp.zeros((5, y.shape[1]), F32)
-    sums = jnp.concatenate([row_sums[...], y_hy, d_hy, d_hd, rest], axis=0)
-    sums = jnp.sum(sums, axis=1, keepdims=True)
+def dots_kernel(flags, gathered, left, right, swapped, level, row_sums, d_hd, out):
+    d = level[lax.axis_index("core")]
+    y = gathered[...].reshape(d.shape)
+    image = chip_image(y, flags, left, right, swapped)
+    dots = [jnp.sum((x * image).reshape(-1, 8, d.shape[1]), axis=0) for x in (y.astype(F32), d)]
+    sums = jnp.sum(jnp.concatenate([row_sums[...]] + dots + [d_hd[...]], axis=0), axis=1, keepdims=True)
     extent = (sums.shape[0], out.shape[1])
-    here = lax.broadcasted_iota(jnp.int32, extent, 0) == lax.broadcasted_iota(jnp.int32, extent, 1)
+    row, lane = (lax.broadcasted_iota(jnp.int32, extent, i) for i in range(2))
+    here = jnp.where(row < 8, row, 7 + row // 8) == lane
     line = jnp.sum(jnp.where(here, sums, 0.0), axis=0, keepdims=True)
     out[...] = jnp.broadcast_to(line, out.shape)
 
@@ -239,7 +234,7 @@
         return lax.ppermute(x, "core", SWAP)
 
     operators = shape((ops,) + block, BF16)
-    part, left, right, others, guess, precond, rows_other, columns, flags = call(
+    part, left, right, others, guess, precond, columns, flags = call(
         other_kernel,
         (
             shape((states + 16, states), BF16),
@@ -247,27 +242,27 @@
             operators,
             shape((2, ops) + block, BF16),
             shape(guess_hbm.shape, F32),
-            shape(block, F32),
-            shape((count // cores, states), F32),
+            shape(guess_hbm.shape, F32),
             shape(columns.shape, BF16),
             shape((sectors, ops, states), F32),
         ),
         [HBM] * 6,
         flops // 2,
-        [pltpu.SMEM(pattern.shape, jnp.int32), dma, dma, dma, dma((2,)), dma((2,)), dma((2,)), dma],
+        [pltpu.SMEM(pattern.shape, jnp.int32), dma, dma, dma((2,)), dma((2,)), dma((2,)), dma],
     )(*(in_hbm(x) for x in (pattern, left_hbm, right_hbm, guess_hbm, precond_hbm, columns)))
     theirs = swap(part)
-    own, level, own_rows, state_rows = call(
+    own, level, own_rows, state_rows, d_hd = call(
         own_kernel,
         (
             shape(block, F32),
-            shape(block, F32),
+            shape(guess.shape, F32),
             shape((3, count, states), F32),
             shape((2, sectors, count // cores, states), F32),
+            shape((8, states), F32),
         ),
         [VMEM] * 6,
         flops // 2,
-    )(flags, left, right, guess, precond, rows_other)
+    )(flags, left, right, others, guess, precond)
     chunks, flags = call(
         chunks_kernel,
         (shape((chips, 2 * count, states), BF16), shape((2 * ops, states), F32)),
@@ -282,8 +277,8 @@
         [VMEM] * 2,
     )(received, own_rows)
     gathered = lax.all_to_all(chunks, "chip", 0, 0)
-    sums = call(dots_kernel, shape((chips * cores * zones, 128), F32), [VMEM] * 7, flops)(
-        flags, gathered, left, right, swapped, level, row_sums
+    sums = call(dots_kernel, shape((chips * cores * zones, 128), F32), [VMEM] * 8, flops)(
+        flags, gathered, left, right, swapped, level, row_sums, d_hd
     )
     sums, packed = lax.optimization_barrier((sums, packed))
     sums = lax.all_to_all(sums, OPS + ("sec",), 0, 0)

time: 59 us -> 59.1 us (level)
  transfers between devices with their start and end apart: 4 -> 4, of which waited for: 3 -> 2; matrix products, arithmetic and copies ran while one was open for 0% -> 0% of each run, Pallas kernels for 5% -> 6%
where the time goes in v9:
time: 59.1 us; the launch traced here: 58.9 us
  blocking collectives  23.1 us (39%)
  starting transfers between devices  18.2 us (31%)
  waiting for transfers between devices  8.86 us (15%)
  Pallas kernels  8.07 us (14%)
  between operations  0.67 us (1%)
    all_to_all x1, blocking collectives, local(): received = lax.all_to_all(chunks, 'chip', 0, 0)  13.3 us
    all_to_all x1, starting transfers between devices, local(): sums = lax.all_to_all(sums, OPS + ('sec',), 0, 0)  11.5 us
    all_to_all x1, blocking collectives, local(): gathered = lax.all_to_all(chunks, 'chip', 0, 0)  9.75 us
    all_to_all x1, waiting for transfers between devices, local(): sums = lax.all_to_all(sums, OPS + ('sec',), 0, 0)  7.84 us
    ppermute x3, starting transfers between devices, swap(): return lax.ppermute(x, 'core', SWAP)  6.69 us
    pallas_call x1, Pallas kernels, local(): call(other_kernel, (shape((states + 16, states), BF16), operators, operat...  2.1 us
    pallas_call x1, Pallas kernels, local(): call(renorm_kernel, (shape(left_hbm.shape, BF16), shape((sectors, count /...  1.94 us
    pallas_call x1, Pallas kernels, local(): call(dots_kernel, shape((chips * cores * zones, 128), F32), [VMEM] * 8, f...  1.83 us
  transfers between devices with their start and end apart: 4, of which 2 were waited for; matrix products, arithmetic and copies ran while one was open for 0% of the time, Pallas kernels for 6%

profile of v9, /device:TPU:1, one launch (start us, length us, event | category | flops | bytes accessed | tf_op | source)
XLA Modules:
  0.0 58.9 jit_solution(7977438808254952217)
XLA Ops:
  0.6 2.1 %shard_map.85 = (bf16[272,256]{1,0:T(8,128)(2,1)S(1)}, bf16[4,256,256]{2,1,0:T(8,128)(2,1)S(1)}, bf16[4,256,256]{2,1,0:T(8,128)(2,1)S(1)}, bf16[2,4,256,256]{3,2...) custom-call(s32[2,4]{1,0:T(2,128)} %bitcast.12, ...), custom_call_target="tpu_custom_call" | custom-call | flops 268435456 | bytes 1048576 | tf_op jit(solution)/shard_map/pallas_call | solution.py:237
  2.7 3.3 %collective-permute-start = (bf16[272,256]{1,0:T(8,128)(2,1)S(1)}, bf16[272,256]{1,0:T(8,128)(2,1)S(1)}, u32[]{:S(2)}, u32[]{:S(2)}) collective-permute-start(bf16[272,256]{1,0:T(8,128)(2,1)S(1)} %get-tuple-element.36), channel_id=1, source_target_pairs={{0,8},{8,0},{1,9},{9,1},{2,10},{10,2},{3,11},{11,3},{4,12},{12,4},... | collective-permute-start | bytes 417800 | tf_op jit(solution)/shard_map/ppermute | solution.py:234
  6.1 1.3 %shard_map.86 = (f32[256,256]{1,0:T(8,128)S(1)}, f32[2,256,256]{2,1,0:T(8,128)S(1)}, f32[3,16,256]{2,1,0:T(8,128)S(1)}, f32[2,2,8,256]{3,2,1,0:T(8,128)S(1)}, f32[8,256]{1,0:T(8,128)S(1)}) custom-call(f32[2,4,256]{2,1,0:T(4,128)S(1)} %get-tuple-element.29.flags, bf16[4,256,256]{2,1,0:T(8,128)(2,1)S(1)} %get-tuple-element.30.left, ...), custom_call_target="tpu_custom_call" | custom-call | flops 268435456 | bytes 1048576 | tf_op jit(solution)/shard_map/pallas_call | solution.py:254
  7.4 0.0 collective-permute-done.theirs
  7.4 13.3 %all_to_all.21.received = bf16[16,32,256]{2,1,0:T(8,128)(2,1)S(1)} all-to-all(bf16[16,32,256]{2,1,0:T(8,128)(2,1)S(1)} %get-tuple-element.39), channel_id=1, replica_groups=mesh['chip'=16,'core'=2,'sec'=8] {'chip'}, dimensions={0} | all-to-all | bytes 524288 | tf_op jit(solution)/shard_map/all_to_all | solution.py:271
  20.8 1.1 %collective-permute-start.1 = (bf16[2,4,256,256]{3,2,1,0:T(8,128)(2,1)S(1)}, bf16[2,4,256,256]{3,2,1,0:T(8,128)(2,1)S(1)}, u32[]{:S(2)}, u32[]{:S(2)}) collective-permute-start(bf16[2,4,256,256]{3,2,1,0:T(8,128)(2,1)S(1)} %get-tuple-element.43.operators), channel_id=1, source_target_pairs={{0,8},{8,0},{1,9},{9,1},{2,10},{10,2},{3,11},{11,3},{4,12},{12,4},... | collective-permute-start | bytes 3145736 | tf_op jit(solution)/shard_map/ppermute | solution.py:234
  21.9 0.1 shard_map.88
  22.0 9.8 %all_to_all.22.gathered = bf16[16,16,256]{2,1,0:T(8,128)(2,1)S(1)} all-to-all(bf16[16,16,256]{2,1,0:T(8,128)(2,1)S(1)} %get-tuple-element.42), channel_id=1, replica_groups=mesh['chip'=16,'core'=2,'sec'=8] {'chip'}, dimensions={0} | all-to-all | bytes 262144 | tf_op jit(solution)/shard_map/all_to_all | solution.py:279
  31.7 0.0 collective-permute-done.1.swapped
  31.7 1.8 %shard_map.89 = f32[256,128]{1,0:T(8,128)} custom-call(f32[8,256]{1,0:T(8,128)S(1)} %get-tuple-element.38.flags, bf16[16,16,256]{2,1,0:T(8,128)(2,1)S(1)} %all_to_all.22.gathered, bf16[4,256,256]{2,1,0:T(8,128)(2,1)S(1)} %get-tuple-element.30.left, bf16[4,256,256]{2,1,0:T(8,128)(2,1)S(1)} %get-tuple-element.31.right, ...), custom_call_target="tpu_custom_call" | custom-call | flops 536870912 | bytes 1048576 | tf_op jit(solution)/shard_map/pallas_call | solution.py:280
  33.5 11.5 %all-to-all-start.2 = ((f32[256,1,128]{2,1,0:T(1,128)}), f32[256,1,128]{2,1,0:T(1,128)S(1)}, u32[]{:S(2)}, u32[]{:S(2)}) async-start(f32[256,1,128]{2,1,0:T(1,128)} %bitcast.4), calls=%async_computation.2 | async-start | bytes 262144 | tf_op jit(solution)/shard_map/all_to_all | solution.py:284
  45.1 2.2 %collective-permute-start.2 = (bf16[304,256]{1,0:T(8,128)(2,1)S(1)}, bf16[304,256]{1,0:T(8,128)(2,1)S(1)}, u32[]{:S(2)}, u32[]{:S(2)}) collective-permute-start(bf16[304,256]{1,0:T(8,128)(2,1)S(1)} %get-tuple-element.50.packed), channel_id=1, source_target_pairs={{0,8},{8,0},{1,9},{9,1},{2,10},{10,2},{3,11},{11,3},{4,12},{12,4},... | collective-permute-start | bytes 466952 | tf_op jit(solution)/shard_map/ppermute | solution.py:234
  47.3 1.0 %collective-permute-done.2.packed_theirs = bf16[304,256]{1,0:T(8,128)(2,1)S(1)} collective-permute-done((bf16[304,256]{1,0:T(8,128)(2,1)S(1)}, bf16[304,256]{1,0:T(8,128)(2,1)S(1)}, u32[]{:S(2)}, u32[]{:S(2)}) %collective-permute-start.2) | collective-permute-done | bytes 155680 | tf_op jit(solution)/shard_map/ppermute | solution.py:234
  48.3 1.9 %shard_map.90 = (bf16[4,2,256,256]{3,2,1,0:T(8,128)(2,1)}, f32[2,8,256]{2,1,0:T(8,128)S(1)}) custom-call(bf16[4,256,256]{2,1,0:T(8,128)(2,1)S(1)} %get-tuple-element.30.left, bf16[2,4,256,256]{3,2,1,0:T(8,128)(2,1)S(1)} %get-tuple-element.43.operators, bf16[304,256]{1,0:T(8,128)(2,1)S(1)} %get-tuple-element.50.packed, ...), custom_call_target="tpu_custom_call" | custom-call | flops 1073741824 | bytes 1048576 | tf_op jit(solution)/shard_map/pallas_call | solution.py:285
  50.3 7.8 %all-to-all-done.2 = f32[256,1,128]{2,1,0:T(1,128)S(1)} async-done(((f32[256,1,128]{2,1,0:T(1,128)}), f32[256,1,128]{2,1,0:T(1,128)S(1)}, u32[]{:S(2)}, u32[]{:S(2)}) %all-to-all-start.2) | async-done | bytes 131104 | tf_op jit(solution)/shard_map/all_to_all | solution.py:284
  58.1 0.8 %shard_map.91 = (f32[2,8,256]{2,1,0:T(8,128)}, f32[1,128]{1,0:T(1,128)}) custom-call(f32[256,128]{1,0:T(8,128)S(1)} %bitcast.10, f32[2,2,8,256]{3,2,1,0:T(8,128)S(1)} %get-tuple-element.49.refs_1_, f32[2,8,256]{2,1,0:T(8,128)S(1)} %get-tuple-element.51.refs_2_), custom_call_target="tpu_custom_call" | custom-call | bytes 1048576 | tf_op jit(solution)/shard_map/pallas_call | solution.py:291
  (1 shorter events, 0.0 us)
Async XLA Ops:
  2.7 4.6 %collective-permute-start = (bf16[272,256]{1,0:T(8,128)(2,1)S(1)}, bf16[272,256]{1,0:T(8,128)(2,1)S(1)}, u32[]{:S(2)}, u32[]{:S(2)}) collective-permute-start(bf16[272,256]{1,0:T(8,128)(2,1)S(1)} %get-tuple-element.36), channel_id=1, source_target_pairs={{0,8},{8,0},{1,9},{9,1},{2,10},{10,2},{3,11},{11,3},{4,12},{12,4},... | collective-permute-start | bytes 417800 | tf_op jit(solution)/shard_map/ppermute | solution.py:234
  20.8 11.0 %collective-permute-start.1 = (bf16[2,4,256,256]{3,2,1,0:T(8,128)(2,1)S(1)}, bf16[2,4,256,256]{3,2,1,0:T(8,128)(2,1)S(1)}, u32[]{:S(2)}, u32[]{:S(2)}) collective-permute-start(bf16[2,4,256,256]{3,2,1,0:T(8,128)(2,1)S(1)} %get-tuple-element.43.operators), channel_id=1, source_target_pairs={{0,8},{8,0},{1,9},{9,1},{2,10},{10,2},{3,11},{11,3},{4,12},{12,4},... | collective-permute-start | bytes 3145736 | tf_op jit(solution)/shard_map/ppermute | solution.py:234
  33.5 24.6 %all-to-all-start.2 = ((f32[256,1,128]{2,1,0:T(1,128)}), f32[256,1,128]{2,1,0:T(1,128)S(1)}, u32[]{:S(2)}, u32[]{:S(2)}) async-start(f32[256,1,128]{2,1,0:T(1,128)} %bitcast.4), calls=%async_computation.2 | async-start | bytes 262144 | tf_op jit(solution)/shard_map/all_to_all | solution.py:284
  45.1 3.3 %collective-permute-start.2 = (bf16[304,256]{1,0:T(8,128)(2,1)S(1)}, bf16[304,256]{1,0:T(8,128)(2,1)S(1)}, u32[]{:S(2)}, u32[]{:S(2)}) collective-permute-start(bf16[304,256]{1,0:T(8,128)(2,1)S(1)} %get-tuple-element.50.packed), channel_id=1, source_target_pairs={{0,8},{8,0},{1,9},{9,1},{2,10},{10,2},{3,11},{11,3},{4,12},{12,4},... | collective-permute-start | bytes 466952 | tf_op jit(solution)/shard_map/ppermute | solution.py:234

commit v10 on v8

--- a/solution.py
+++ b/solution.py
@@ -73,7 +73,7 @@
         pltpu.make_async_copy(precond_hbm.at[mine], precond, precond_sem),
         pltpu.make_async_copy(precond_hbm.at[other, own], rows_other, rows_sem),
     ]
-    for copy in small + copies[0] + copies[1] + last:
+    for copy in copies[0] + small + copies[1] + last:
         copy.start()
     for copy in small:
         copy.wait()
@@ -165,14 +165,13 @@
     states = y.shape[1]
     images = chip_image(jnp.concatenate([y, level[...].astype(BF16)], axis=1), flags, left, right, swapped)
     image = images[:states]
-    d_hd = jnp.sum(level[...] * images[states:], axis=0, keepdims=True)
-    y_hy = jnp.sum(y.astype(F32) * image, axis=0, keepdims=True)
-    d_hy = jnp.sum(level[...] * image, axis=0, keepdims=True)
-    rest = jnp.zeros((5, y.shape[1]), F32)
-    sums = jnp.concatenate([row_sums[...], y_hy, d_hy, d_hd, rest], axis=0)
-    sums = jnp.sum(sums, axis=1, keepdims=True)
+    d = level[...]
+    pairs = ((y.astype(F32), image), (d, image), (d, images[states:]))
+    dots = [jnp.sum((a * b).reshape(-1, 8, states), axis=0) for a, b in pairs]
+    sums = jnp.sum(jnp.concatenate([row_sums[...]] + dots, axis=0), axis=1, keepdims=True)
     extent = (sums.shape[0], out.shape[1])
-    here = lax.broadcasted_iota(jnp.int32, extent, 0) == lax.broadcasted_iota(jnp.int32, extent, 1)
+    row, lane = (lax.broadcasted_iota(jnp.int32, extent, i) for i in range(2))
+    here = jnp.where(row < 8, row, 7 + row // 8) == lane
     line = jnp.sum(jnp.where(here, sums, 0.0), axis=0, keepdims=True)
     out[...] = jnp.broadcast_to(line, out.shape)
 

time: 59 us -> 59 us (level)
  no operation moved by 1% of the time
where the time goes in v10:
time: 59 us; the launch traced here: 58.7 us
  blocking collectives  22.7 us (38%)
  starting transfers between devices  18.6 us (32%)
  waiting for transfers between devices  9.13 us (15%)
  Pallas kernels  7.66 us (13%)
  between operations  0.66 us (1%)
    all_to_all x1, blocking collectives, local(): received = lax.all_to_all(chunks, 'chip', 0, 0)  12.9 us
    all_to_all x1, starting transfers between devices, local(): sums = lax.all_to_all(sums, OPS + ('sec',), 0, 0)  11.5 us
    all_to_all x1, blocking collectives, local(): gathered = lax.all_to_all(chunks, 'chip', 0, 0)  9.75 us
    all_to_all x1, waiting for transfers between devices, local(): sums = lax.all_to_all(sums, OPS + ('sec',), 0, 0)  7.84 us
    ppermute x3, starting transfers between devices, swap(): return lax.ppermute(x, 'core', SWAP)  7.07 us
    pallas_call x1, Pallas kernels, local(): call(other_kernel, (shape((states + 16, states), BF16), operators, operat...  2.11 us
    pallas_call x1, Pallas kernels, local(): call(dots_kernel, shape((chips * cores * zones, 128), F32), [VMEM] * 7, f...  2 us
    pallas_call x1, Pallas kernels, local(): call(renorm_kernel, (shape(left_hbm.shape, BF16), shape((sectors, count /...  1.94 us
  transfers between devices with their start and end apart: 4, of which 3 were waited for; matrix products, arithmetic and copies ran while one was open for 0% of the time, Pallas kernels for 5%

profile of v10, /device:TPU:1, one launch (start us, length us, event | category | flops | bytes accessed | tf_op | source)
XLA Modules:
  0.0 58.7 jit_solution(8694303778107749086)
XLA Ops:
  0.6 2.1 %shard_map.85 = (bf16[272,256]{1,0:T(8,128)(2,1)S(1)}, bf16[4,256,256]{2,1,0:T(8,128)(2,1)S(1)}, bf16[4,256,256]{2,1,0:T(8,128)(2,1)S(1)}, bf16[2,4,256,256]{3,2...) custom-call(s32[2,4]{1,0:T(2,128)} %bitcast.12, ...), custom_call_target="tpu_custom_call" | custom-call | flops 268435456 | bytes 1048576 | tf_op jit(solution)/shard_map/pallas_call | solution.py:241
  2.7 3.3 %collective-permute-start = (bf16[272,256]{1,0:T(8,128)(2,1)S(1)}, bf16[272,256]{1,0:T(8,128)(2,1)S(1)}, u32[]{:S(2)}, u32[]{:S(2)}) collective-permute-start(bf16[272,256]{1,0:T(8,128)(2,1)S(1)} %get-tuple-element.36), channel_id=1, source_target_pairs={{0,8},{8,0},{1,9},{9,1},{2,10},{10,2},{3,11},{11,3},{4,12},{12,4},... | collective-permute-start | bytes 417800 | tf_op jit(solution)/shard_map/ppermute | solution.py:238
  6.1 0.7 %shard_map.86 = (f32[256,256]{1,0:T(8,128)S(1)}, f32[256,256]{1,0:T(8,128)S(1)}, f32[3,16,256]{2,1,0:T(8,128)S(1)}, f32[2,2,8,256]{3,2,1,0:T(8,128)S(1)}) custom-call(f32[2,4,256]{2,1,0:T(4,128)S(1)} %get-tuple-element.29.flags, bf16[4,256,256]{2,1,0:T(8,128)(2,1)S(1)} %get-tuple-element.30.left, bf16[4,256,256]{2,1,0:T(8,128)(2,1)S(1)} %get-tuple-element.31.right, ...), custom_call_target="tpu_custom_call" | custom-call | flops 268435456 | bytes 1048576 | tf_op jit(solution)/shard_map/pallas_call | solution.py:259
  6.8 0.3 collective-permute-done.theirs
  7.1 12.9 %all_to_all.21.received = bf16[16,32,256]{2,1,0:T(8,128)(2,1)S(1)} all-to-all(bf16[16,32,256]{2,1,0:T(8,128)(2,1)S(1)} %get-tuple-element.39), channel_id=1, replica_groups=mesh['chip'=16,'core'=2,'sec'=8] {'chip'}, dimensions={0} | all-to-all | bytes 524288 | tf_op jit(solution)/shard_map/all_to_all | solution.py:275
  20.1 1.5 %collective-permute-start.1 = (bf16[2,4,256,256]{3,2,1,0:T(8,128)(2,1)S(1)}, bf16[2,4,256,256]{3,2,1,0:T(8,128)(2,1)S(1)}, u32[]{:S(2)}, u32[]{:S(2)}) collective-permute-start(bf16[2,4,256,256]{3,2,1,0:T(8,128)(2,1)S(1)} %get-tuple-element.44.operators), channel_id=1, source_target_pairs={{0,8},{8,0},{1,9},{9,1},{2,10},{10,2},{3,11},{11,3},{4,12},{12,4},... | collective-permute-start | bytes 3145736 | tf_op jit(solution)/shard_map/ppermute | solution.py:238
  21.6 0.1 shard_map.88
  21.6 9.8 %all_to_all.22.gathered = bf16[16,16,256]{2,1,0:T(8,128)(2,1)S(1)} all-to-all(bf16[16,16,256]{2,1,0:T(8,128)(2,1)S(1)} %get-tuple-element.43), channel_id=1, replica_groups=mesh['chip'=16,'core'=2,'sec'=8] {'chip'}, dimensions={0} | all-to-all | bytes 262144 | tf_op jit(solution)/shard_map/all_to_all | solution.py:283
  31.4 0.0 collective-permute-done.1.swapped
  31.4 2.0 %shard_map.89 = f32[256,128]{1,0:T(8,128)} custom-call(f32[8,256]{1,0:T(8,128)S(1)} %get-tuple-element.38.flags, bf16[16,16,256]{2,1,0:T(8,128)(2,1)S(1)} %all_to_all.22.gathered, bf16[4,256,256]{2,1,0:T(8,128)(2,1)S(1)} %get-tuple-element.30.left, bf16[4,256,256]{2,1,0:T(8,128)(2,1)S(1)} %get-tuple-element.31.right, ...), custom_call_target="tpu_custom_call" | custom-call | flops 536870912 | bytes 1048576 | tf_op jit(solution)/shard_map/pallas_call | solution.py:284
  33.4 11.5 %all-to-all-start.2 = ((f32[256,1,128]{2,1,0:T(1,128)}), f32[256,1,128]{2,1,0:T(1,128)S(1)}, u32[]{:S(2)}, u32[]{:S(2)}) async-start(f32[256,1,128]{2,1,0:T(1,128)} %bitcast.4), calls=%async_computation.2 | async-start | bytes 262144 | tf_op jit(solution)/shard_map/all_to_all | solution.py:288
  44.9 2.2 %collective-permute-start.2 = (bf16[304,256]{1,0:T(8,128)(2,1)S(1)}, bf16[304,256]{1,0:T(8,128)(2,1)S(1)}, u32[]{:S(2)}, u32[]{:S(2)}) collective-permute-start(bf16[304,256]{1,0:T(8,128)(2,1)S(1)} %get-tuple-element.50.packed), channel_id=1, source_target_pairs={{0,8},{8,0},{1,9},{9,1},{2,10},{10,2},{3,11},{11,3},{4,12},{12,4},... | collective-permute-start | bytes 466952 | tf_op jit(solution)/shard_map/ppermute | solution.py:238
  47.1 1.0 %collective-permute-done.2.packed_theirs = bf16[304,256]{1,0:T(8,128)(2,1)S(1)} collective-permute-done((bf16[304,256]{1,0:T(8,128)(2,1)S(1)}, bf16[304,256]{1,0:T(8,128)(2,1)S(1)}, u32[]{:S(2)}, u32[]{:S(2)}) %collective-permute-start.2) | collective-permute-done | bytes 155680 | tf_op jit(solution)/shard_map/ppermute | solution.py:238
  48.2 1.9 %shard_map.90 = (bf16[4,2,256,256]{3,2,1,0:T(8,128)(2,1)}, f32[2,8,256]{2,1,0:T(8,128)S(1)}) custom-call(bf16[4,256,256]{2,1,0:T(8,128)(2,1)S(1)} %get-tuple-element.30.left, bf16[2,4,256,256]{3,2,1,0:T(8,128)(2,1)S(1)} %get-tuple-element.44.operators, bf16[304,256]{1,0:T(8,128)(2,1)S(1)} %get-tuple-element.50.packed, ...), custom_call_target="tpu_custom_call" | custom-call | flops 1073741824 | bytes 1048576 | tf_op jit(solution)/shard_map/pallas_call | solution.py:289
  50.1 7.8 %all-to-all-done.2 = f32[256,1,128]{2,1,0:T(1,128)S(1)} async-done(((f32[256,1,128]{2,1,0:T(1,128)}), f32[256,1,128]{2,1,0:T(1,128)S(1)}, u32[]{:S(2)}, u32[]{:S(2)}) %all-to-all-start.2) | async-done | bytes 131104 | tf_op jit(solution)/shard_map/all_to_all | solution.py:288
  57.9 0.8 %shard_map.91 = (f32[2,8,256]{2,1,0:T(8,128)}, f32[1,128]{1,0:T(1,128)}) custom-call(f32[256,128]{1,0:T(8,128)S(1)} %bitcast.10, f32[2,2,8,256]{3,2,1,0:T(8,128)S(1)} %get-tuple-element.49.refs_1_, f32[2,8,256]{2,1,0:T(8,128)S(1)} %get-tuple-element.51.refs_2_), custom_call_target="tpu_custom_call" | custom-call | bytes 1048576 | tf_op jit(solution)/shard_map/pallas_call | solution.py:295
  (1 shorter events, 0.0 us)
Async XLA Ops:
  2.7 4.3 %collective-permute-start = (bf16[272,256]{1,0:T(8,128)(2,1)S(1)}, bf16[272,256]{1,0:T(8,128)(2,1)S(1)}, u32[]{:S(2)}, u32[]{:S(2)}) collective-permute-start(bf16[272,256]{1,0:T(8,128)(2,1)S(1)} %get-tuple-element.36), channel_id=1, source_target_pairs={{0,8},{8,0},{1,9},{9,1},{2,10},{10,2},{3,11},{11,3},{4,12},{12,4},... | collective-permute-start | bytes 417800 | tf_op jit(solution)/shard_map/ppermute | solution.py:238
  20.1 11.3 %collective-permute-start.1 = (bf16[2,4,256,256]{3,2,1,0:T(8,128)(2,1)S(1)}, bf16[2,4,256,256]{3,2,1,0:T(8,128)(2,1)S(1)}, u32[]{:S(2)}, u32[]{:S(2)}) collective-permute-start(bf16[2,4,256,256]{3,2,1,0:T(8,128)(2,1)S(1)} %get-tuple-element.44.operators), channel_id=1, source_target_pairs={{0,8},{8,0},{1,9},{9,1},{2,10},{10,2},{3,11},{11,3},{4,12},{12,4},... | collective-permute-start | bytes 3145736 | tf_op jit(solution)/shard_map/ppermute | solution.py:238
  33.4 24.6 %all-to-all-start.2 = ((f32[256,1,128]{2,1,0:T(1,128)}), f32[256,1,128]{2,1,0:T(1,128)S(1)}, u32[]{:S(2)}, u32[]{:S(2)}) async-start(f32[256,1,128]{2,1,0:T(1,128)} %bitcast.4), calls=%async_computation.2 | async-start | bytes 262144 | tf_op jit(solution)/shard_map/all_to_all | solution.py:288
  44.9 3.3 %collective-permute-start.2 = (bf16[304,256]{1,0:T(8,128)(2,1)S(1)}, bf16[304,256]{1,0:T(8,128)(2,1)S(1)}, u32[]{:S(2)}, u32[]{:S(2)}) collective-permute-start(bf16[304,256]{1,0:T(8,128)(2,1)S(1)} %get-tuple-element.50.packed), channel_id=1, source_target_pairs={{0,8},{8,0},{1,9},{9,1},{2,10},{10,2},{3,11},{11,3},{4,12},{12,4},... | collective-permute-start | bytes 466952 | tf_op jit(solution)/shard_map/ppermute | solution.py:238
